TPU v7x, 32 devices: a whole 2x2x4 slice. The times are simulated.
32 devices in a mesh: seq: 4 (over y, core), head: 4 (over z), role: 2 (over x).
Axes of the slice: x: 2, y: 2, z: 4, core: 2. Of those that a mesh axis runs over, the one named last changes fastest.
Arguments:
- prefill_queries: bfloat16 [2, 1024, 8192], P(None, 'seq', ('head', 'role')), may hold values from -64 to 64
- prefill_keys: bfloat16 [2, 1024, 1024], P(None, 'seq', ('head', 'role')), may hold values from -4 to 4
- prefill_values: bfloat16 [2, 1024, 1024], P(None, 'seq', ('head', 'role')), may hold values from -4 to 4
- prompt_len: int32 [2], replicated, may hold values from 512 to 1024, as said below
- assignment: int32 [16], P(('seq', 'role')), may hold values from 0 to 1
- cache_len: int32 [16], P(('seq', 'role')), may hold values from 8 to 1024, as said below
- cache_keys: bfloat16 [16, 1024, 1024], P(('seq', 'role'), None, 'head'), may hold values from -4 to 4
- cache_values: bfloat16 [16, 1024, 1024], P(('seq', 'role'), None, 'head'), may hold values from -4 to 4
- decode_queries: bfloat16 [4, 16, 8192], P(None, ('seq', 'role'), 'head'), may hold values from -64 to 64
- new_keys: bfloat16 [4, 16, 1024], P(None, ('seq', 'role'), 'head'), may hold values from -4 to 4
- new_values: bfloat16 [4, 16, 1024], P(None, ('seq', 'role'), 'head'), may hold values from -4 to 4
Outputs:
- prefill_out: bfloat16 [2, 1024, 8192], P(None, 'seq', ('head', 'role'))
- decode_out: bfloat16 [4, 16, 8192], P(None, ('seq', 'role'), 'head')
Inputs may be any that keep to these rules, and one draw needn't show every extreme that they name: `prompt_len`: one prompt of every draw holds all 1024 positions. `cache_len`: the own cache of some decode row is full in every draw.
All inputs are finite; a program needn't handle non-finite values.
Results may differ from a plain program's by a relative error of at most 0.0038.
Values may be sent and summed in bfloat16 or wider, within the bound.
No kernel may reach another device: no remote copies, remote signals or barrier semaphores. Data moves between devices by JAX's collectives and lax.ppermute only.
A program may use at most 192 MiB of HBM per device.

v0:
```python
import jax
import jax.numpy as jnp
from jax import lax
from jax.sharding import PartitionSpec as P

D_HEAD = 128


MASKED_SCORE = -1e30


def prompt_fold(queries, query_pos, head_width):
    score_scale = head_width ** (-0.5)

    def add_keys(running, pieces, offset):
        run_max, run_sum, weighted = running
        key_rows, value_rows = pieces
        row_count, key_count, merged = key_rows.shape
        head_count = merged // head_width
        keys_split = key_rows.reshape(row_count, key_count, head_count, head_width)
        values_split = value_rows.reshape(row_count, key_count, head_count, head_width)
        scores = (
            jnp.einsum("rpngd,rknd->rngpk", queries, keys_split, preferred_element_type=jnp.float32)
            * score_scale
        )
        key_pos = jnp.arange(key_count, dtype=jnp.int32)
        allowed = key_pos[None, :] <= query_pos[:, None]
        scores = jnp.where(allowed, scores, MASKED_SCORE)
        new_max = jnp.maximum(run_max, jnp.max(scores, axis=-1))
        weights = jnp.where(allowed, jnp.exp(scores - new_max[..., None]), 0.0)
        new_sum = jnp.sum(weights, axis=-1)
        update = jnp.einsum(
            "rngpk,rknd->rpngd",
            weights.astype(jnp.bfloat16),
            values_split,
            preferred_element_type=jnp.float32,
        )
        return (new_max, new_sum, update)

    return add_keys


def relay_heads(gathered, seq_count, role_count):
    slots, row_count, key_count, columns = gathered.shape
    split = gathered.reshape(seq_count, role_count, row_count, key_count, columns)
    ordered = jnp.transpose(split, (2, 0, 3, 1, 4))
    return ordered.reshape(row_count, seq_count * key_count, role_count * columns)


def decode_attend(
    decode_queries,
    prompt_keys,
    prompt_values,
    prompt_len,
    assignment,
    cache_len,
    cache_keys,
    cache_values,
    new_keys,
    new_values,
    head_width,
):
    score_scale = head_width ** (-0.5)
    step_count, local_rows, query_cols = decode_queries.shape
    kv_count = cache_keys.shape[2] // head_width
    group_size = query_cols // (kv_count * head_width)
    queries = decode_queries.reshape(step_count, local_rows, kv_count, group_size, head_width)
    row_keys = jnp.take(prompt_keys, assignment, axis=0)
    row_values = jnp.take(prompt_values, assignment, axis=0)
    prompt_count = prompt_len.shape[0]
    picks = assignment[:, None] == jnp.arange(prompt_count, dtype=jnp.int32)[None, :]
    row_len = jnp.sum(jnp.where(picks, prompt_len[None, :], 0), axis=1)
    prompt_span = row_keys.shape[1]
    cache_span = cache_keys.shape[1]
    prompt_mask = (jnp.arange(prompt_span, dtype=jnp.int32)[None, :] < row_len[:, None])[
        :, None, None, None, :
    ]
    cache_mask = (jnp.arange(cache_span, dtype=jnp.int32)[None, :] < cache_len[:, None])[
        :, None, None, None, :
    ]
    step_index = jnp.arange(step_count, dtype=jnp.int32)
    fresh_mask = (step_index[None, :] <= step_index[:, None])[None, None, None, :, :]
    prompt_scores = (
        jnp.einsum(
            "trngd,rknd->rngtk",
            queries,
            row_keys.reshape(local_rows, prompt_span, kv_count, head_width),
            preferred_element_type=jnp.float32,
        )
        * score_scale
    )
    cache_scores = (
        jnp.einsum(
            "trngd,rknd->rngtk",
            queries,
            cache_keys.reshape(local_rows, cache_span, kv_count, head_width),
            preferred_element_type=jnp.float32,
        )
        * score_scale
    )
    fresh_scores = (
        jnp.einsum(
            "trngd,urnd->rngtu",
            queries,
            new_keys.reshape(step_count, local_rows, kv_count, head_width),
            preferred_element_type=jnp.float32,
        )
        * score_scale
    )
    prompt_scores = jnp.where(prompt_mask, prompt_scores, MASKED_SCORE)
    cache_scores = jnp.where(cache_mask, cache_scores, MASKED_SCORE)
    fresh_scores = jnp.where(fresh_mask, fresh_scores, MASKED_SCORE)
    top_score = jnp.maximum(
        jnp.maximum(jnp.max(prompt_scores, axis=-1), jnp.max(cache_scores, axis=-1)),
        jnp.max(fresh_scores, axis=-1),
    )
    prompt_weights = jnp.where(prompt_mask, jnp.exp(prompt_scores - top_score[..., None]), 0.0)
    cache_weights = jnp.where(cache_mask, jnp.exp(cache_scores - top_score[..., None]), 0.0)
    fresh_weights = jnp.where(fresh_mask, jnp.exp(fresh_scores - top_score[..., None]), 0.0)
    weight_sum = (
        jnp.sum(prompt_weights, axis=-1)
        + jnp.sum(cache_weights, axis=-1)
        + jnp.sum(fresh_weights, axis=-1)
    )
    summed = jnp.einsum(
        "rngtk,rknd->trngd",
        prompt_weights.astype(jnp.bfloat16),
        row_values.reshape(local_rows, prompt_span, kv_count, head_width),
        preferred_element_type=jnp.float32,
    )
    summed = summed + jnp.einsum(
        "rngtk,rknd->trngd",
        cache_weights.astype(jnp.bfloat16),
        cache_values.reshape(local_rows, cache_span, kv_count, head_width),
        preferred_element_type=jnp.float32,
    )
    summed = summed + jnp.einsum(
        "rngtu,urnd->trngd",
        fresh_weights.astype(jnp.bfloat16),
        new_values.reshape(step_count, local_rows, kv_count, head_width),
        preferred_element_type=jnp.float32,
    )
    result = summed / jnp.transpose(weight_sum, (3, 0, 1, 2))[..., None]
    return result.reshape(step_count, local_rows, query_cols).astype(jnp.bfloat16)


def body(
    prefill_queries,
    prefill_keys,
    prefill_values,
    prompt_len,
    assignment,
    cache_len,
    cache_keys,
    cache_values,
    decode_queries,
    new_keys,
    new_values,
):
    head_width = D_HEAD
    row_count, key_count, query_cols = prefill_queries.shape
    kv_local = prefill_keys.shape[2] // head_width
    group_size = query_cols // (kv_local * head_width)
    queries = prefill_queries.reshape(row_count, key_count, kv_local, group_size, head_width)
    query_pos = lax.axis_index("seq") * key_count + jnp.arange(key_count, dtype=jnp.int32)
    start_state = (
        jnp.full((row_count, kv_local, group_size, key_count), MASKED_SCORE, jnp.float32),
        jnp.zeros((row_count, kv_local, group_size, key_count), jnp.float32),
        jnp.zeros((row_count, key_count, kv_local, group_size, head_width), jnp.float32),
    )
    add_keys = prompt_fold(queries, query_pos, head_width)
    run_max, run_sum, weighted = add_keys(
        start_state,
        (
            lax.all_gather(prefill_keys, "seq", axis=1, tiled=True),
            lax.all_gather(prefill_values, "seq", axis=1, tiled=True),
        ),
        jnp.int32(0),
    )
    result = weighted / jnp.transpose(run_sum, (0, 3, 1, 2))[..., None]
    live_rows = query_pos[None, :] < prompt_len[:, None]
    result = jnp.where(live_rows[:, :, None, None, None], result, 0.0)
    prefill_out = result.reshape(row_count, key_count, query_cols).astype(jnp.bfloat16)
    gathered_keys, gathered_values = (
        lax.all_gather(prefill_keys[None], ("seq", "role"), axis=0, tiled=True),
        lax.all_gather(prefill_values[None], ("seq", "role"), axis=0, tiled=True),
    )
    prompt_keys = relay_heads(gathered_keys, lax.axis_size("seq"), lax.axis_size("role"))
    prompt_values = relay_heads(gathered_values, lax.axis_size("seq"), lax.axis_size("role"))
    decode_out = decode_attend(
        decode_queries,
        prompt_keys,
        prompt_values,
        prompt_len,
        assignment,
        cache_len,
        cache_keys,
        cache_values,
        new_keys,
        new_values,
        head_width,
    )
    return (prefill_out, decode_out)


def solution(mesh):
    in_specs = (
        P(None, "seq", ("head", "role")),
        P(None, "seq", ("head", "role")),
        P(None, "seq", ("head", "role")),
        P(),
        P(("seq", "role")),
        P(("seq", "role")),
        P(("seq", "role"), None, "head"),
        P(("seq", "role"), None, "head"),
        P(None, ("seq", "role"), "head"),
        P(None, ("seq", "role"), "head"),
        P(None, ("seq", "role"), "head"),
    )
    out_specs = (P(None, "seq", ("head", "role")), P(None, ("seq", "role"), "head"))
    return jax.shard_map(body, mesh=mesh, in_specs=in_specs, out_specs=out_specs, check_vma=False)
```

profile of v0, /device:TPU:0, one launch (start us, length us, event | category | flops | bytes accessed | tf_op | source)
XLA Modules:
  0.0 84.3 jit_solution(3122609071325536500)
XLA Ops:
  7.2 0.7 all-gather.5.cloned.1.call-update
  8.0 0.7 all-gather.7.cloned.1.call-update
  8.7 8.9 %all_gather.12 = bf16[2,1024,128]{2,1,0:T(8,128)(2,1)S(1)} all-gather(bf16[2,256,128]{2,1,0:T(8,128)(2,1)} %param.14), channel_id=1, replica_groups=mesh['seq'=4,'head'=4,'role'=2] {'seq'}, dimensions={1}, use_global_device_ids=true | all-gather | bytes 655360 | tf_op jit(solution)/shard_map/all_gather | solution.py:175
  17.5 1.0 %copy.61 = bf16[2,256,128]{1,2,0:T(8,128)(2,1)S(1)} copy(bf16[2,256,128]{2,1,0:T(8,128)(2,1)} %param.15) | data formatting | bytes 262144 | tf_op args[2]
  18.8 2.6 %fusion = (f32[2,8,256]{2,1,0:T(8,128)S(1)}, f32[2,1024,256,8]{2,1,3,0:T(8,128)S(1)}) fusion(pred[256,1024]{0,1:T(8,128)(4,1)S(1)} %iota_compare_fusion, bf16[2,1024,128]{2,1,0:T(8,128)(2,1)S(1)} %all_gather.12, bf16[2,256,1024]{2,1,0:T(8,128)(2,1)S(1)} %copy-done), kind=kOutput, calls=%fused_computation.4 | convolution fusion | flops 1086320640 | bytes 18628608 | tf_op jit(solution)/shard_map/rpngd,rknd->rngpk/dot_general | solution.py:23
  21.5 7.5 %all_gather.13 = bf16[2,1024,128]{1,2,0:T(8,128)(2,1)S(1)} all-gather(bf16[2,256,128]{1,2,0:T(8,128)(2,1)S(1)} %copy.61), channel_id=1, replica_groups=mesh['seq'=4,'head'=4,'role'=2] {'seq'}, dimensions={1}, use_global_device_ids=true | all-gather | bytes 655360 | tf_op jit(solution)/shard_map/all_gather | solution.py:176
  29.0 4.0 %fusion.1 = f32[2,8,256]{2,1,0:T(8,128)S(1)} fusion(f32[2,1024,256,8]{2,1,3,0:T(8,128)S(1)} %get-tuple-element.16, f32[2,8,256]{2,1,0:T(8,128)S(1)} %broadcast_maximum_fusion, pred[256,1024]{0,1:T(8,128)(4,1)S(1)} %iota_compare_fusion), kind=kLoop, calls=%fused_computation.5 | loop fusion | flops 20967424 | bytes 17072128 | tf_op jit(solution)/shard_map/reduce_sum | solution.py:31
  33.0 5.2 %fusion.8 = bf16[2,256,1,8,128]{1,4,3,0,2:T(8,128)(2,1)} fusion(f32[2,1024,256,8]{2,1,3,0:T(8,128)S(1)} %get-tuple-element.16, f32[2,8,256]{2,1,0:T(8,128)S(1)} %broadcast_maximum_fusion, pred[256,1024]{0,1:T(8,128)(4,1)S(1)} %iota_compare_fusion, f32[2,256,8]{1,2,0:T(8,128)S(1)} %bitcast.127, pred[2,256]{1,0:T(4,128)(4,1)S(1)} %broadcast_compare_fusion, ...), kind=kOutput, calls=%fused_computation.12 | convolution fusion | flops 1096286208 | bytes 18645504 | tf_op jit(solution)/shard_map/rngpk,rknd->rpngd/dot_general | solution.py:32
  38.3 2.3 %copy.77 = bf16[2,256,1024]{2,1,0:T(8,128)(2,1)} copy(bf16[2,256,1024]{1,2,0:T(8,128)(2,1)} %bitcast.121) | data formatting | bytes 2097152
  40.5 1.1 %reshape.183 = bf16[2,1024,2,128]{3,2,1,0:T(2,128)(2,1)} reshape(bf16[2,1024,256]{2,1,0:T(8,128)(2,1)S(1)} %copy-done.1) | data formatting | bytes 2097152 | tf_op jit(solution)/shard_map/reshape | solution.py:134
  42.7 1.3 %fusion.60 = (f32[2,2,8,4]{2,3,1,0:T(4,128)S(1)}, f32[2,2,8,4,1024]{4,2,3,1,0:T(8,128)}) fusion(bf16[4,2,2,8,128]{4,3,2,1,0:T(8,128)(2,1)S(1)} %reshape.180, bf16[2,1024,2,128,1]{3,2,1,0,4:T(2,128)(2,1)S(1)} %bitcast.119, pred[2,1024]{1,0:T(4,128)(4,1)S(1)} %get-tuple-element.23), kind=kOutput, calls=%fused_computation.85 | convolution fusion | flops 33947520 | bytes 1608192 | tf_op jit(solution)/shard_map/trngd,rknd->rngtk/dot_general | solution.py:93
  43.9 2.3 %copy.133 = bf16[4,2,2,256,128]{4,1,3,0,2:T(2,128)(2,1)S(1)} copy(bf16[4,2,2,256,128]{4,3,2,1,0:T(8,128)(2,1)} %bitcast.116) | data formatting | bytes 2097152 | tf_op jit(solution)/shard_map/reshape | solution.py:45
  46.2 0.7 reshape.175
  47.0 14.6 %all-gather.7.cloned.1.call-done = bf16[16,256,128]{2,1,0:T(8,128)(2,1)} async-done(((bf16[2,256,128]{2,1,0:T(8,128)(2,1)}), bf16[16,256,128]{2,1,0:T(8,128)(2,1)}) %all-gather.7.cloned.1.call-update) | async-done | bytes 1048592 | tf_op jit(solution)/shard_map/all_gather | solution.py:185
  61.5 2.3 %copy.132 = bf16[4,2,2,256,128]{4,1,3,0,2:T(2,128)(2,1)S(1)} copy(bf16[4,2,2,256,128]{4,3,2,1,0:T(8,128)(2,1)} %bitcast.117) | data formatting | bytes 2097152 | tf_op jit(solution)/shard_map/reshape | solution.py:45
  63.8 1.5 %reshape.178 = bf16[2,1024,256]{2,1,0:T(8,128)(2,1)} reshape(bf16[2,4,256,2,128]{4,3,2,1,0:T(2,128)(2,1)S(1)} %bitcast.115) | data formatting | bytes 2097152 | tf_op jit(solution)/shard_map/reshape | solution.py:47
  65.3 0.6 gather_fusion
  66.0 1.8 %gather_fusion.1 = bf16[2,1024,256]{2,1,0:T(8,128)(2,1)S(1)} fusion(bf16[2,1024,256]{2,1,0:T(8,128)(2,1)} %reshape.178, s32[1024]{0:T(1024)S(1)} %pad_clamp_fusion), kind=kCustom, calls=%fused_computation.1.clone | custom fusion | bytes 2097160 | tf_op jit(solution)/shard_map/jit(_take)/gather | solution.py:68
  67.8 1.6 %broadcast_select_fusion.1 = (bf16[2,1024,256]{2,1,0:T(8,128)(2,1)}, bf16[2,1024,256]{2,1,0:T(8,128)(2,1)}) fusion(bf16[2,1024,256]{2,1,0:T(8,128)(2,1)S(1)} %gather_fusion, pred[2]{0:T(512)(128)(4,1)S(1)} %compare_and_fusion, bf16[2,1024,256]{2,1,0:T(8,128)(2,1)S(1)} %gather_fusion.1), kind=kLoop, calls=%fused_computation.38 | loop fusion | flops 1048576 | bytes 4194306 | tf_op jit(solution)/shard_map/jit(_take)/select_n | solution.py:69
  69.4 1.5 %copy.66 = bf16[2,1024,256]{1,2,0:T(8,128)(2,1)S(1)} copy(bf16[2,1024,256]{2,1,0:T(8,128)(2,1)} %get-tuple-element.14) | data formatting | bytes 2097152 | tf_op jit(solution)/shard_map/jit(_take)/select_n | solution.py:68
  70.9 1.5 %copy.64 = bf16[2,1024,256]{1,2,0:T(8,128)(2,1)S(1)} copy(bf16[2,1024,256]{2,1,0:T(8,128)(2,1)} %get-tuple-element.13) | data formatting | bytes 2097152 | tf_op jit(solution)/shard_map/jit(_take)/select_n | solution.py:69
  72.9 1.7 %convolution_bitcast_fusion.1 = f32[4,2,2,8,128]{4,3,0,2,1:T(8,128)S(1)} fusion(bf16[2,1024,2,128,1]{3,2,1,0,4:T(2,128)(2,1)} %bitcast.118, f32[2,2,8,4,1024]{4,2,3,1,0:T(8,128)} %get-tuple-element.22, f32[2,2,8,4]{2,3,1,0:T(4,128)S(1)} %bitcast.123, pred[2,1024]{1,0:T(4,128)(4,1)S(1)} %get-tuple-element.23), kind=kOutput, calls=%fused_computation.22 | convolution fusion | flops 33947648 | bytes 1640960 | tf_op jit(solution)/shard_map/rngtk,rknd->trngd/dot_general | solution.py:131
  74.6 1.4 %fusion.30 = (f32[2,2,8,4]{2,3,1,0:T(4,128)S(1)}, f32[2,2,8,4]{2,3,1,0:T(4,128)S(1)}) fusion(f32[2,2,8,4,1024]{4,2,3,1,0:T(8,128)} %get-tuple-element.22, f32[2,2,8,4]{2,3,1,0:T(4,128)S(1)} %bitcast.124, pred[2,1024]{1,0:T(4,128)(4,1)S(1)} %get-tuple-element.23, f32[2,2,8,4,1024]{4,2,3,1,0:T(8,128)S(1)} %get-tuple-element.20, ...), kind=kLoop, calls=%fused_computation.45 | loop fusion | flops 786176 | bytes 1054208 | tf_op jit(solution)/shard_map/reduce_sum | solution.py:122
  76.8 0.6 convert_element_type.31
  (43 shorter events, 2.5 us)
Async XLA Ops:
  7.2 11.6 %copy-start = (bf16[2,256,1024]{2,1,0:T(8,128)(2,1)S(1)}, bf16[2,256,1024]{2,1,0:T(8,128)(2,1)}, u32[]{:S(2)}) copy-start(bf16[2,256,1024]{2,1,0:T(8,128)(2,1)} %param.13) | copy-start | bytes 3145732
  7.2 36.7 %all-gather.5.cloned.1.call-start = ((), (), s32[]{:S(2)}) async-start(), calls=%async_computation | async-start | bytes 1179648 | tf_op jit(solution)/shard_map/all_gather | solution.py:186
  7.9 53.6 %all-gather.7.cloned.1.call-start = ((), (), s32[]{:S(2)}) async-start(), calls=%async_computation.1 | async-start | bytes 1179648 | tf_op jit(solution)/shard_map/all_gather | solution.py:185
  17.5 3.9 %copy-start.6 = (s32[2]{0:T(128)S(1)}, s32[2]{0:T(128)}, u32[]{:S(2)}) copy-start(s32[2]{0:T(128)} %param.16) | copy-start | bytes 28
  33.0 7.6 %copy-start.1 = (bf16[2,1024,256]{2,1,0:T(8,128)(2,1)S(1)}, bf16[2,1024,256]{2,1,0:T(8,128)(2,1)}, u32[]{:S(2)}) copy-start(bf16[2,1024,256]{2,1,0:T(8,128)(2,1)} %param.20) | copy-start | bytes 3145732
  33.0 8.7 %copy-start.3 = (bf16[4,2,2048]{2,1,0:T(2,128)(2,1)S(1)}, bf16[4,2,2048]{2,1,0:T(2,128)(2,1)}, u32[]{:S(2)}) copy-start(bf16[4,2,2048]{2,1,0:T(2,128)(2,1)} %param.21) | copy-start | bytes 98308
  33.0 8.7 %copy-start.2 = (bf16[2,1024,256]{2,1,0:T(8,128)(2,1)S(1)}, bf16[2,1024,256]{2,1,0:T(8,128)(2,1)}, u32[]{:S(2)}) copy-start(bf16[2,1024,256]{2,1,0:T(8,128)(2,1)} %param.19) | copy-start | bytes 3145732
  33.0 9.0 %copy-start.4 = (bf16[4,2,256]{2,1,0:T(2,128)(2,1)S(1)}, bf16[4,2,256]{2,1,0:T(2,128)(2,1)}, u32[]{:S(2)}) copy-start(bf16[4,2,256]{2,1,0:T(2,128)(2,1)} %param.22) | copy-start | bytes 12292
  33.0 9.0 %copy-start.5 = (bf16[4,2,256]{2,1,0:T(2,128)(2,1)S(1)}, bf16[4,2,256]{2,1,0:T(2,128)(2,1)}, u32[]{:S(2)}) copy-start(bf16[4,2,256]{2,1,0:T(2,128)(2,1)} %param.23) | copy-start | bytes 12292
  33.0 9.1 %copy-start.8 = (s32[2]{0:T(128)S(1)}, s32[2]{0:T(128)}, u32[]{:S(2)}) copy-start(s32[2]{0:T(128)} %param.17) | copy-start | bytes 28
  33.0 9.3 %copy-start.7 = (s32[2]{0:T(128)S(1)}, s32[2]{0:T(128)}, u32[]{:S(2)}) copy-start(s32[2]{0:T(128)} %param.18) | copy-start | bytes 28
Sparse Core Ops, SparseCore 0:
  9.9 26.1 all-gather.4
  38.0 23.4 all-gather.6
where the time goes:
time: 84.7 us; the launch traced here: 84.3 us
  local copies, waits for them, and re-layouts  17.7 us (21%)
  blocking collectives  16.3 us (19%)
  waiting for transfers between devices  15.9 us (19%)
  between operations  14.3 us (17%)
  matrix products  12.3 us (15%)
  other arithmetic  7.62 us (9%)
    all_gather x1, waiting for transfers between devices, body(): lax.all_gather(prefill_keys[None], ('seq', 'role'), axis=0, tiled=True)  14.6 us
    all_gather x1, blocking collectives, body(): lax.all_gather(prefill_keys, 'seq', axis=1, tiled=True)  8.86 us
    all_gather x1, blocking collectives, body(): lax.all_gather(prefill_values, 'seq', axis=1, tiled=True)  7.46 us
    dot_general x1, matrix products, add_keys(): jnp.einsum('rngpk,rknd->rpngd', weights.astype(jnp.bfloat16), values_spli...  5.24 us
    reshape x2, local copies, waits for them, and re-layouts, relay_heads(): gathered.reshape(seq_count, role_count, row_count, key_count, columns)  4.63 us
    reduce_sum x1, other arithmetic, add_keys(): new_sum = jnp.sum(weights, axis=-1)  3.98 us
    unnamed x20, local copies, waits for them, and re-layouts  3.34 us
    dot_general x1, matrix products, add_keys(): jnp.einsum('rpngd,rknd->rngpk', queries, keys_split, preferred_element_ty...  2.64 us
  transfers between devices with their start and end apart: 2, of which 1 were waited for; matrix products, arithmetic and copies ran while one was open for 26% of the time, Pallas kernels for 0%

commit v1 on v0

v1 whole, which is shorter than its diff:
```python
import functools
import math

import jax
import jax.numpy as jnp
from jax import lax
from jax.experimental import pallas as pl
from jax.experimental.pallas import tpu as pltpu
from jax.sharding import PartitionSpec as P

D_HEAD = 128
MASKED_SCORE = -1e30
EXP2_SCALE = D_HEAD**-0.5 * math.log2(math.e)
VMEM_BYTES = 40 * 2**20
NT = (((1,), (1,)), ((), ()))


def scores_of(queries, keys):
    return lax.dot_general(queries, keys, NT, preferred_element_type=jnp.float32)


def weighted(weights, values):
    return jnp.dot(weights.astype(jnp.bfloat16), values, preferred_element_type=jnp.float32)


def eye_of(rows):
    shape = (rows, 128)
    return lax.broadcasted_iota(jnp.int32, shape, 0) == lax.broadcasted_iota(jnp.int32, shape, 1)


def column_to_row(column):
    spread = jnp.where(eye_of(column.shape[0]), column, 0.0)
    return jnp.sum(spread, axis=0, keepdims=True)


def row_to_column(row, rows):
    spread = jnp.where(eye_of(rows), jnp.broadcast_to(row, (rows, 128)), 0.0)
    return jnp.sum(spread, axis=1, keepdims=True)


def soft_parts(score_parts, masks, value_parts):
    masked = [jnp.where(mask, part * EXP2_SCALE, MASKED_SCORE) for part, mask in zip(score_parts, masks)]
    top = functools.reduce(jnp.maximum, [jnp.max(part, axis=1, keepdims=True) for part in masked])
    total = jnp.zeros_like(top)
    summed = jnp.zeros((top.shape[0], D_HEAD), jnp.float32)
    for part, mask, values in zip(masked, masks, value_parts):
        weights = jnp.where(mask, jnp.exp2(part - top), 0.0)
        total = total + jnp.sum(weights, axis=1, keepdims=True)
        summed = summed + weighted(weights, values)
    return summed, top, total


def pack_kernel(asg_ref, dq_ref, own_ref, other_ref, flat):
    steps, rows, columns = dq_ref.shape
    span = steps * rows
    for step in range(steps):
        flat[step * rows : (step + 1) * rows, :] = dq_ref[step].astype(jnp.float32)
    role = lax.axis_index("role")
    half = columns // 2
    group = half // D_HEAD
    row_index = lax.broadcasted_iota(jnp.int32, (span, 128), 0) % rows
    prompt = jnp.zeros((span, 128), jnp.float32)
    for row in range(rows):
        prompt = jnp.where(row_index == row, asg_ref[row].astype(jnp.float32), prompt)
    for out, kv in ((own_ref, role), (other_ref, 1 - role)):
        for pair in range(group // 2):
            two = [
                flat[:, pl.ds(pl.multiple_of(kv * half + (2 * pair + i) * D_HEAD, D_HEAD), D_HEAD)] for i in (0, 1)
            ]
            out[2 * span * pair : 2 * span * (pair + 1), :] = jnp.concatenate(two, axis=0).astype(jnp.bfloat16)
        out[span * group : span * (group + 2), :] = jnp.concatenate([prompt, prompt], axis=0).astype(jnp.bfloat16)


def cache_kernel(rows, steps, len_ref, own_ref, other_ref, ck_ref, cv_ref, nk_ref, nv_ref, sum_ref, top_ref, tot_ref, fk, fv):
    span = steps * rows
    queries = own_ref.shape[0] - 2 * span
    role = lax.axis_index("role")
    slots = ck_ref.shape[1]
    fk[...] = jnp.zeros_like(fk)
    fv[...] = jnp.zeros_like(fv)
    for step in range(steps):
        fk[step * rows : (step + 1) * rows, :] = nk_ref[step].astype(jnp.float32)
        fv[step * rows : (step + 1) * rows, :] = nv_ref[step].astype(jnp.float32)
    q_index = lax.broadcasted_iota(jnp.int32, (queries, 1), 0) % span
    q_step, q_row = q_index // rows, q_index % rows
    lane = lax.broadcasted_iota(jnp.int32, (queries, 128), 1)
    fresh_mask = (lane < span) & (lane % rows == q_row) & (lane // rows <= q_step)
    slot = lax.broadcasted_iota(jnp.int32, (queries, slots), 1)
    for index, (message, kv) in enumerate(((own_ref, role), (other_ref, 1 - role))):
        q = message[:queries, :]
        columns = pl.ds(pl.multiple_of(kv * D_HEAD, D_HEAD), D_HEAD)
        parts = [scores_of(q, fk[:, columns].astype(jnp.bfloat16))]
        masks = [fresh_mask]
        values = [fv[:, columns].astype(jnp.bfloat16)]
        for row in range(rows):
            parts.append(scores_of(q, ck_ref[row, :, columns]))
            masks.append((slot < len_ref[row]) & (q_row == row))
            values.append(cv_ref[row, :, columns])
        summed, top, total = soft_parts(parts, masks, values)
        sum_ref[index] = summed
        top_ref[index] = jnp.broadcast_to(top, (queries, 128))
        tot_ref[index] = jnp.broadcast_to(total, (queries, 128))


def jobs_over(q, prompt, plen_ref, chunks):
    parts, masks, values = [], [], []
    count = q.shape[0]
    for first, keys, vals in chunks:
        position = first + lax.broadcasted_iota(jnp.int32, (count, keys.shape[1]), 1)
        for row in range(keys.shape[0]):
            parts.append(scores_of(q, keys[row]))
            masks.append((position < plen_ref[row]) & (prompt == row))
            values.append(vals[row])
    return soft_parts(parts, masks, values)


def prompt_column(message, span, queries):
    eight = message[queries : queries + 2 * span, :].astype(jnp.float32)[:span, :1]
    return jnp.concatenate([eight] * (queries // span), axis=0)


def jobs_kernel(span, count, plen_ref, *refs):
    messages = refs[:count]
    k_own, v_own, k_near, v_near = refs[count : count + 4]
    outs = refs[count + 4 :]
    queries = messages[0].shape[0] - 2 * span
    seq = lax.axis_index("seq")
    length = k_own.shape[1]
    q = jnp.concatenate([m[:queries, :] for m in messages], axis=0)
    prompt = jnp.concatenate([prompt_column(m, span, queries) for m in messages], axis=0)
    near = seq + 1 - 2 * (seq % 2)
    summed, top, total = jobs_over(
        q, prompt, plen_ref, [(seq * length, k_own, v_own), (near * length, k_near, v_near)]
    )
    for index, out in enumerate(outs):
        rows = slice(index * queries, (index + 1) * queries)
        out[:queries, :] = summed[rows]
        out[queries : queries + 8, :] = jnp.concatenate(
            [column_to_row(top[rows]), column_to_row(total[rows]), jnp.zeros((6, 128), jnp.float32)], axis=0
        )


def local_kernel(q_ref, k_own, v_own, k_near, v_near, sum_ref, top_ref, tot_ref, ones):
    prompts, length, columns = q_ref.shape
    group = columns // D_HEAD
    seq = lax.axis_index("seq")
    ones[:, :, D_HEAD:] = jnp.ones((prompts, 2 * length, D_HEAD), jnp.bfloat16)
    ones[:, :length, :D_HEAD] = v_own[...]
    ones[:, length:, :D_HEAD] = v_near[...]
    causal = lax.broadcasted_iota(jnp.int32, (length, length), 1) <= lax.broadcasted_iota(
        jnp.int32, (length, length), 0
    )

    def run(with_near):
        for row in range(prompts):
            for head in range(group):
                cols = slice(head * D_HEAD, (head + 1) * D_HEAD)
                q = q_ref[row, :, cols]
                own = jnp.where(causal, scores_of(q, k_own[row]), MASKED_SCORE)
                top = jnp.max(own, axis=1, keepdims=True)
                if with_near:
                    near = scores_of(q, k_near[row])
                    top = jnp.maximum(top, jnp.max(near, axis=1, keepdims=True))
                top = top * EXP2_SCALE
                summed = weighted(jnp.exp2(own * EXP2_SCALE - top), ones[row, :length, :])
                if with_near:
                    summed = summed + weighted(jnp.exp2(near * EXP2_SCALE - top), ones[row, length:, :])
                sum_ref[row, :, cols] = summed[:, :D_HEAD]
                tot_ref[row, :, cols] = summed[:, D_HEAD:]
                top_ref[row, :, cols] = jnp.broadcast_to(top, (length, D_HEAD))

    @pl.when(seq % 2 == 0)
    def _():
        run(False)

    @pl.when(seq % 2 == 1)
    def _():
        run(True)


def far_scores_kernel(shift, q_ref, k_one, k_two, sum_in, top_in, tot_in, w_ref, sum_ref, top_ref, tot_ref):
    prompts, length, columns = q_ref.shape
    group = columns // D_HEAD

    @pl.when(lax.axis_index("seq") // 2 >= shift)
    def _():
        for row in range(prompts):
            for head in range(group):
                cols = slice(head * D_HEAD, (head + 1) * D_HEAD)
                q = q_ref[row, :, cols]
                one = scores_of(q, k_one[row])
                two = scores_of(q, k_two[row])
                new = jnp.maximum(jnp.max(one, axis=1, keepdims=True), jnp.max(two, axis=1, keepdims=True))
                old = top_in[row, :, cols]
                top = jnp.maximum(old, new * EXP2_SCALE)
                wide = jnp.concatenate([top] * (length // D_HEAD), axis=1)
                w_ref[row, head, :, :length] = jnp.exp2(one * EXP2_SCALE - wide).astype(jnp.bfloat16)
                w_ref[row, head, :, length:] = jnp.exp2(two * EXP2_SCALE - wide).astype(jnp.bfloat16)
                alpha = jnp.exp2(old - top)
                sum_ref[row, :, cols] = sum_in[row, :, cols] * alpha
                tot_ref[row, :, cols] = tot_in[row, :, cols] * alpha
                top_ref[row, :, cols] = top


def far_values_kernel(shift, last, span, n_other, n_own, *refs):
    plen_ref, w_ref, k_one, v_one, k_two, v_two, sum_in, tot_in, own_msg = refs[:9]
    rest = refs[9:]
    prompts, length, columns = sum_in.shape
    group = columns // D_HEAD
    seq = lax.axis_index("seq")
    role = lax.axis_index("role")
    pairs = lax.axis_size("seq") // 2
    outer = seq // 2
    queries = own_msg.shape[0] - 2 * span
    if last:
        cache_sum, cache_top, cache_tot = rest[:3]
        own_parts = rest[3 : 3 + n_own]
        other_parts = rest[3 + n_own : 3 + n_own + n_other]
        late_parts = rest[3 + n_own + n_other : -6]
        out_ref, dec_ref, late_ref, flat, ones_one, ones_two = rest[-6:]
    else:
        sum_ref, tot_ref, late_ref, ones_one, ones_two = rest

    def finish(row, cols, summed, total):
        if last:
            position = seq * length + lax.broadcasted_iota(jnp.int32, (length, D_HEAD), 0)
            result = jnp.where(position < plen_ref[row], summed / total, 0.0)
            out_ref[row, :, cols] = result.astype(jnp.bfloat16)
        else:
            sum_ref[row, :, cols] = summed
            tot_ref[row, :, cols] = total

    @pl.when(outer >= shift)
    def _():
        for ones, vals in ((ones_one, v_one), (ones_two, v_two)):
            ones[:, :, :D_HEAD] = vals[...]
            ones[:, :, D_HEAD:] = jnp.ones((prompts, length, D_HEAD), jnp.bfloat16)
        for row in range(prompts):
            for head in range(group):
                cols = slice(head * D_HEAD, (head + 1) * D_HEAD)
                far = jnp.dot(w_ref[row, head, :, :length], ones_one[row], preferred_element_type=jnp.float32)
                far = far + jnp.dot(w_ref[row, head, :, length:], ones_two[row], preferred_element_type=jnp.float32)
                finish(row, cols, sum_in[row, :, cols] + far[:, :D_HEAD], tot_in[row, :, cols] + far[:, D_HEAD:])
        near = 1 - 2 * (seq % 2)
        first = (seq - 2 * shift) * length
        summed, top, total = jobs_over(
            own_msg[:queries, :],
            prompt_column(own_msg, span, queries),
            plen_ref,
            [(first, k_one, v_one), (first + near * length, k_two, v_two)],
        )
        late_ref[:queries, :] = summed
        late_ref[queries : queries + 8, :] = jnp.concatenate(
            [column_to_row(top), column_to_row(total), jnp.zeros((6, 128), jnp.float32)], axis=0
        )

    @pl.when(outer < shift)
    def _():
        for row in range(prompts):
            for head in range(group):
                cols = slice(head * D_HEAD, (head + 1) * D_HEAD)
                finish(row, cols, sum_in[row, :, cols], tot_in[row, :, cols])
        late_ref[...] = jnp.zeros_like(late_ref)

    if not last:
        return
    half = group * D_HEAD
    lates = [(part, outer >= s + 1) for s, part in enumerate(list(late_parts) + [late_ref])]
    owns = [(own_parts[0], True)] + [(part, outer + s + 1 < pairs) for s, part in enumerate(own_parts[1:])]
    others = [(part, True) for part in other_parts]
    for index, (parts, kv) in enumerate(((owns + lates, role), (others, 1 - role))):
        sums, tops, tots = [cache_sum[index]], [cache_top[index][:, :1]], [cache_tot[index][:, :1]]
        for part, valid in parts:
            top = row_to_column(part[queries : queries + 1, :], queries)
            total = row_to_column(part[queries + 1 : queries + 2, :], queries)
            summed = part[:queries, :]
            if valid is not True:
                top = jnp.where(valid, top, MASKED_SCORE)
                total = jnp.where(valid, total, 0.0)
                summed = jnp.where(valid, summed, 0.0)
            sums.append(summed)
            tops.append(top)
            tots.append(total)
        high = functools.reduce(jnp.maximum, tops)
        factors = [jnp.exp2(top - high) for top in tops]
        summed = functools.reduce(jnp.add, [f * s for f, s in zip(factors, sums)])
        total = functools.reduce(jnp.add, [f * t for f, t in zip(factors, tots)])
        result = summed / total
        for head in range(group):
            start = pl.multiple_of(kv * half + head * D_HEAD, D_HEAD)
            flat[:, pl.ds(start, D_HEAD)] = result[head * span : (head + 1) * span]
    steps, rows, _ = dec_ref.shape
    for step in range(steps):
        dec_ref[step] = flat[step * rows : (step + 1) * rows, :].astype(jnp.bfloat16)


VMEM = pl.BlockSpec(memory_space=pltpu.VMEM)
SMEM = pl.BlockSpec(memory_space=pltpu.SMEM)


def call(kernel, args, outs, scratch=(), scalars=1, aliases=None, flops=0, moved=0):
    return pl.pallas_call(
        kernel,
        out_shape=outs,
        in_specs=[SMEM] * scalars + [VMEM] * (len(args) - scalars),
        out_specs=[VMEM] * len(outs),
        scratch_shapes=list(scratch),
        input_output_aliases=aliases or {},
        compiler_params=pltpu.CompilerParams(vmem_limit_bytes=VMEM_BYTES),
        cost_estimate=pl.CostEstimate(flops=flops, bytes_accessed=moved, transcendentals=0),
    )(*args)


def body(
    prefill_queries,
    prefill_keys,
    prefill_values,
    prompt_len,
    assignment,
    cache_len,
    cache_keys,
    cache_values,
    decode_queries,
    new_keys,
    new_values,
):
    seqs, roles = lax.axis_size("seq"), lax.axis_size("role")
    pairs = seqs // 2
    prompts, length, columns = prefill_queries.shape
    steps, rows, dec_columns = decode_queries.shape
    group = columns // D_HEAD
    span = steps * rows
    queries = group * span
    f32, bf16 = jnp.float32, jnp.bfloat16
    shape = jax.ShapeDtypeStruct

    swap = [(i, i ^ 1) for i in range(seqs)]

    def near(x):
        return lax.ppermute(x, "seq", swap)

    def forward(x, shift):
        return lax.ppermute(x, "seq", [(i, i + 2 * shift) for i in range(seqs - 2 * shift)])

    def back(x, shift):
        return lax.ppermute(x, "seq", [(i + 2 * shift, i) for i in range(seqs - 2 * shift)])

    def across(x, shift):
        moves = [
            (i * roles + r, (i + 2 * shift) % seqs * roles + (1 - r)) for i in range(seqs) for r in range(roles)
        ]
        return lax.ppermute(x, ("seq", "role"), moves)

    shifts = range(1, pairs)
    far_keys = [forward(prefill_keys, s) for s in shifts]
    far_values = [forward(prefill_values, s) for s in shifts]
    near_keys, near_values = near(prefill_keys), near(prefill_values)
    message = shape((queries + 2 * span, 128), bf16)
    own_msg, other_msg = call(
        pack_kernel, (assignment, decode_queries), [message] * 2, [pltpu.VMEM((span, dec_columns), f32)]
    )
    other_msgs = [across(other_msg, s) for s in range(pairs)]
    own_msgs = [forward(own_msg, s) for s in shifts]
    state = shape((2, queries, 128), f32)
    cache_parts = call(
        functools.partial(cache_kernel, rows, steps),
        (cache_len, own_msg, other_msg, cache_keys, cache_values, new_keys, new_values),
        [state] * 3,
        [pltpu.VMEM((128, 2 * D_HEAD), f32)] * 2,
    )
    messages = [own_msg] + other_msgs + own_msgs
    part = shape((queries + 8, 128), f32)
    parts = call(
        functools.partial(jobs_kernel, span, len(messages)),
        (prompt_len, *messages, prefill_keys, prefill_values, near_keys, near_values),
        [part] * len(messages),
    )
    other_parts = [across(p, -s) for s, p in enumerate(parts[1 : 1 + pairs])]
    own_parts = [parts[0]] + [back(p, s) for s, p in zip(shifts, parts[1 + pairs :])]
    run = shape((prompts, length, columns), f32)
    summed, top, total = call(
        local_kernel,
        (prefill_queries, prefill_keys, prefill_values, near_keys, near_values),
        [run] * 3,
        [pltpu.VMEM((prompts, 2 * length, 2 * D_HEAD), bf16)],
        scalars=0,
    )
    lates = []
    for index, shift in enumerate(shifts):
        last = shift == pairs - 1
        k_one, v_one = far_keys[index], far_values[index]
        k_two, v_two = near(k_one), near(v_one)
        weights, summed, top, total = call(
            functools.partial(far_scores_kernel, shift),
            (prefill_queries, k_one, k_two, summed, top, total),
            [shape((prompts, group, length, 2 * length), bf16)] + [run] * 3,
            scalars=0,
            aliases={3: 1, 4: 2, 5: 3},
        )
        args = (prompt_len, weights, k_one, v_one, k_two, v_two, summed, total, own_msg)
        ones = [pltpu.VMEM((prompts, length, 2 * D_HEAD), bf16)] * 2
        if last:
            prefill_out, decode_out, _ = call(
                functools.partial(far_values_kernel, shift, True, span, len(other_parts), len(own_parts)),
                (*args, *cache_parts, *own_parts, *other_parts, *lates),
                [shape(prefill_queries.shape, bf16), shape(decode_queries.shape, bf16), part],
                [pltpu.VMEM((span, dec_columns), f32)] + ones,
            )
        else:
            summed, total, late = call(
                functools.partial(far_values_kernel, shift, False, span, 0, 0),
                args,
                [run, run, part],
                ones,
                aliases={6: 0, 7: 1},
            )
            lates.append(late)
    return (prefill_out, decode_out)


def solution(mesh):
    in_specs = (
        P(None, "seq", ("head", "role")),
        P(None, "seq", ("head", "role")),
        P(None, "seq", ("head", "role")),
        P(),
        P(("seq", "role")),
        P(("seq", "role")),
        P(("seq", "role"), None, "head"),
        P(("seq", "role"), None, "head"),
        P(None, ("seq", "role"), "head"),
        P(None, ("seq", "role"), "head"),
        P(None, ("seq", "role"), "head"),
    )
    out_specs = (P(None, "seq", ("head", "role")), P(None, ("seq", "role"), "head"))
    return jax.shard_map(body, mesh=mesh, in_specs=in_specs, out_specs=out_specs, check_vma=False)
```

time: 84.7 us -> 50.9 us (0.60)
  the two profiles are of different devices: /device:TPU:0 before, /device:TPU:28 now
where the time goes in v1:
time: 50.9 us; the launch traced here: 50.4 us
  waiting for transfers between devices  17.7 us (35%)
  starting transfers between devices  12.2 us (24%)
  Pallas kernels  11.4 us (22%)
  local copies, waits for them, and re-layouts  8.36 us (16%)
  between operations  0.82 us (2%)
    pallas_call x6, Pallas kernels, call(): pl.pallas_call(kernel, out_shape=outs, in_specs=[SMEM] * scalars + [VMEM]...  11.4 us
    ppermute x3, waiting for transfers between devices, forward(): lax.ppermute(x, 'seq', [(i, i + 2 * shift) for i in range(seqs - 2 * shif...  11.3 us
    unnamed x28, local copies, waits for them, and re-layouts  8.36 us
    ppermute x4, waiting for transfers between devices, across(): return lax.ppermute(x, ('seq', 'role'), moves)  6.32 us
    ppermute x3, starting transfers between devices, forward(): lax.ppermute(x, 'seq', [(i, i + 2 * shift) for i in range(seqs - 2 * shif...  4.01 us
    ppermute x1, starting transfers between devices, back(): lax.ppermute(x, 'seq', [(i + 2 * shift, i) for i in range(seqs - 2 * shif...  3.89 us
    ppermute x4, starting transfers between devices, across(): return lax.ppermute(x, ('seq', 'role'), moves)  3.7 us
  transfers between devices with their start and end apart: 12, of which 5 were waited for; matrix products, arithmetic and copies ran while one was open for 0% of the time, Pallas kernels for 16%

profile of v1, /device:TPU:28, one launch (start us, length us, event | category | flops | bytes accessed | tf_op | source)
XLA Modules:
  0.0 50.4 jit_solution(6958130685514119443)
XLA Ops:
  0.6 1.4 %collective-permute-start = (bf16[2,256,128]{2,1,0:T(8,128)(2,1)}, bf16[2,256,128]{2,1,0:T(8,128)(2,1)S(1)}, u32[]{:S(2)}, u32[]{:S(2)}) collective-permute-start(bf16[2,256,128]{2,1,0:T(8,128)(2,1)} %refs_4_.1), channel_id=1, source_target_pairs={{0,16},{8,24},{1,17},{9,25},{2,18},{10,26},{3,19},{11,27},{4,20},{... | collective-permute-start | bytes 393224 | tf_op jit(solution)/shard_map/ppermute | solution.py:343
  2.1 1.3 %collective-permute-start.4 = (bf16[2,256,128]{2,1,0:T(8,128)(2,1)}, bf16[2,256,128]{2,1,0:T(8,128)(2,1)S(1)}, u32[]{:S(2)}, u32[]{:S(2)}) collective-permute-start(bf16[2,256,128]{2,1,0:T(8,128)(2,1)} %refs_5_.1), channel_id=1, source_target_pairs={{0,16},{8,24},{1,17},{9,25},{2,18},{10,26},{3,19},{11,27},{4,20},{... | collective-permute-start | bytes 393224 | tf_op jit(solution)/shard_map/ppermute | solution.py:343
  3.9 5.3 %collective-permute-done.k_one.refs_2_ = bf16[2,256,128]{2,1,0:T(8,128)(2,1)S(1)} collective-permute-done((bf16[2,256,128]{2,1,0:T(8,128)(2,1)}, bf16[2,256,128]{2,1,0:T(8,128)(2,1)S(1)}, u32[]{:S(2)}, u32[]{:S(2)}) %collective-permute-start) | collective-permute-done | bytes 131104 | tf_op jit(solution)/shard_map/ppermute | solution.py:343
  9.3 1.7 %collective-permute-done.4.refs_3_ = bf16[2,256,128]{2,1,0:T(8,128)(2,1)S(1)} collective-permute-done((bf16[2,256,128]{2,1,0:T(8,128)(2,1)}, bf16[2,256,128]{2,1,0:T(8,128)(2,1)S(1)}, u32[]{:S(2)}, u32[]{:S(2)}) %collective-permute-start.4) | collective-permute-done | bytes 131104 | tf_op jit(solution)/shard_map/ppermute | solution.py:343
  10.9 0.8 %copy-done.7 = bf16[4,2,2048]{2,1,0:T(2,128)(2,1)S(1)} copy-done((bf16[4,2,2048]{2,1,0:T(2,128)(2,1)S(1)}, bf16[4,2,2048]{2,1,0:T(2,128)(2,1)}, u32[]{:S(2)}) %copy-start.7) | copy-done | bytes 32792
  11.7 0.7 %copy-done.12 = s32[2]{0:T(128)S(1)} copy-done((s32[2]{0:T(128)S(1)}, s32[2]{0:T(128)}, u32[]{:S(2)}) %copy-start.12) | copy-done | bytes 32
  12.9 1.3 %collective-permute-start.8 = (bf16[80,128]{1,0:T(8,128)(2,1)S(1)}, bf16[80,128]{1,0:T(8,128)(2,1)S(1)}, u32[]{:S(2)}, u32[]{:S(2)}) collective-permute-start(bf16[80,128]{1,0:T(8,128)(2,1)S(1)} %get-tuple-element.25.own_ref.refs_0_.refs_8_), channel_id=1, source_target_pairs={{0,16},{8,24},{1,17},{9,25},{2,18},{10,26},{3,19},{11,27},{4,20},{... | collective-permute-start | bytes 61448 | tf_op jit(solution)/shard_map/ppermute | solution.py:343
  14.2 4.4 %collective-permute-done.8.refs_3_ = bf16[80,128]{1,0:T(8,128)(2,1)S(1)} collective-permute-done((bf16[80,128]{1,0:T(8,128)(2,1)S(1)}, bf16[80,128]{1,0:T(8,128)(2,1)S(1)}, u32[]{:S(2)}, u32[]{:S(2)}) %collective-permute-start.8) | collective-permute-done | bytes 20512 | tf_op jit(solution)/shard_map/ppermute | solution.py:343
  18.6 1.5 %collective-permute-start.6 = (bf16[80,128]{1,0:T(8,128)(2,1)S(1)}, bf16[80,128]{1,0:T(8,128)(2,1)S(1)}, u32[]{:S(2)}, u32[]{:S(2)}) collective-permute-start(bf16[80,128]{1,0:T(8,128)(2,1)S(1)} %get-tuple-element.26.other_ref), channel_id=1, source_target_pairs={{0,1},{1,0},{8,9},{9,8},{16,17},{17,16},{24,25},{25,24},{2,3},{3,2... | collective-permute-start | bytes 61448 | tf_op jit(solution)/shard_map/ppermute | solution.py:352
  20.1 2.3 %collective-permute-done.6.refs_1_ = bf16[80,128]{1,0:T(8,128)(2,1)S(1)} collective-permute-done((bf16[80,128]{1,0:T(8,128)(2,1)S(1)}, bf16[80,128]{1,0:T(8,128)(2,1)S(1)}, u32[]{:S(2)}, u32[]{:S(2)}) %collective-permute-start.6) | collective-permute-done | bytes 20512 | tf_op jit(solution)/shard_map/ppermute | solution.py:352
  23.0 4.0 %collective-permute-done.7.refs_2_ = bf16[80,128]{1,0:T(8,128)(2,1)S(1)} collective-permute-done((bf16[80,128]{1,0:T(8,128)(2,1)S(1)}, bf16[80,128]{1,0:T(8,128)(2,1)S(1)}, u32[]{:S(2)}, u32[]{:S(2)}) %collective-permute-start.7) | collective-permute-done | bytes 20512 | tf_op jit(solution)/shard_map/ppermute | solution.py:352
  27.1 0.9 %copy-done.3 = bf16[2,256,128]{2,1,0:T(8,128)(2,1)S(1)} copy-done((bf16[2,256,128]{2,1,0:T(8,128)(2,1)S(1)}, bf16[2,256,128]{2,1,0:T(8,128)(2,1)}, u32[]{:S(2)}) %copy-start.3) | copy-done | bytes 131096
  28.0 0.9 %copy-done.5 = bf16[2,256,128]{2,1,0:T(8,128)(2,1)S(1)} copy-done((bf16[2,256,128]{2,1,0:T(8,128)(2,1)S(1)}, bf16[2,256,128]{2,1,0:T(8,128)(2,1)}, u32[]{:S(2)}) %copy-start.5) | copy-done | bytes 131096
  29.5 1.2 %shard_map.126 = (f32[72,128]{1,0:T(8,128)S(1)}, f32[72,128]{1,0:T(8,128)S(1)}, f32[72,128]{1,0:T(8,128)S(1)}, f32[72,128]{1,0:T(8,128)S(1)}) custom-call(s32[2]{0:T(128)S(1)} %copy-done.10, bf16[80,128]{1,0:T(8,128)(2,1)S(1)} %get-tuple-element.25.own_ref.refs_0_.refs_8_, bf16[80,128]{1,0:T(8,128)(2,1)S(1)} %collective-permute-done.6.refs_1_, ...), custom_call_target="tpu_custom_call" | custom-call | tf_op jit(solution)/shard_map/pallas_call | solution.py:302
  30.7 1.6 %collective-permute-start.10 = (f32[72,128]{1,0:T(8,128)S(1)}, f32[72,128]{1,0:T(8,128)S(1)}, u32[]{:S(2)}, u32[]{:S(2)}) collective-permute-start(f32[72,128]{1,0:T(8,128)S(1)} %get-tuple-element.32), channel_id=1, source_target_pairs={{0,1},{1,0},{8,9},{9,8},{16,17},{17,16},{24,25},{25,24},{2,3},{3,2... | collective-permute-start | bytes 110600 | tf_op jit(solution)/shard_map/ppermute | solution.py:352
  32.3 3.9 %collective-permute-start.9 = (f32[72,128]{1,0:T(8,128)S(1)}, f32[72,128]{1,0:T(8,128)S(1)}, u32[]{:S(2)}, u32[]{:S(2)}) collective-permute-start(f32[72,128]{1,0:T(8,128)S(1)} %get-tuple-element.31), channel_id=1, source_target_pairs={{16,0},{24,8},{17,1},{25,9},{18,2},{26,10},{19,3},{27,11},{20,4},{... | collective-permute-start | bytes 110600 | tf_op jit(solution)/shard_map/ppermute | solution.py:346
  36.2 1.2 %copy-done.1 = bf16[2,1024,256]{2,1,0:T(8,128)(2,1)S(1)} copy-done((bf16[2,1024,256]{2,1,0:T(8,128)(2,1)S(1)}, bf16[2,1024,256]{2,1,0:T(8,128)(2,1)}, u32[]{:S(2)}) %copy-start.1) | copy-done | bytes 1048600
  37.4 1.2 %copy-done.2 = bf16[2,1024,256]{2,1,0:T(8,128)(2,1)S(1)} copy-done((bf16[2,1024,256]{2,1,0:T(8,128)(2,1)S(1)}, bf16[2,1024,256]{2,1,0:T(8,128)(2,1)}, u32[]{:S(2)}) %copy-start.2) | copy-done | bytes 1048600
  38.6 0.7 %copy-done.8 = bf16[4,2,256]{2,1,0:T(2,128)(2,1)S(1)} copy-done((bf16[4,2,256]{2,1,0:T(2,128)(2,1)S(1)}, bf16[4,2,256]{2,1,0:T(2,128)(2,1)}, u32[]{:S(2)}) %copy-start.8) | copy-done | bytes 4120
  39.3 0.7 %copy-done.9 = bf16[4,2,256]{2,1,0:T(2,128)(2,1)S(1)} copy-done((bf16[4,2,256]{2,1,0:T(2,128)(2,1)S(1)}, bf16[4,2,256]{2,1,0:T(2,128)(2,1)}, u32[]{:S(2)}) %copy-start.9) | copy-done | bytes 4120
  40.7 1.8 %shard_map.125 = (f32[2,64,128]{2,1,0:T(8,128)S(1)}, f32[2,64,128]{2,1,0:T(8,128)S(1)}, f32[2,64,128]{2,1,0:T(8,128)S(1)}) custom-call(s32[2]{0:T(128)S(1)} %copy-done.13, bf16[80,128]{1,0:T(8,128)(2,1)S(1)} %get-tuple-element.25.own_ref.refs_0_.refs_8_, bf16[80,128]{1,0:T(8,128)(2,1)S(1)} %get-tuple-element.26.other_ref, ...), custom_call_target="tpu_custom_call" | custom-call | tf_op jit(solution)/shard_map/pallas_call | solution.py:302
  42.5 1.5 %shard_map.122 = (f32[2,256,1024]{2,1,0:T(8,128)S(1)}, f32[2,256,1024]{2,1,0:T(8,128)S(1)}, f32[2,256,1024]{2,1,0:T(8,128)S(1)}) custom-call(bf16[2,256,1024]{2,1,0:T(8,128)(2,1)S(1)} %copy-done, bf16[2,256,128]{2,1,0:T(8,128)(2,1)S(1)} %copy-done.4, bf16[2,256,128]{2,1,0:T(8,128)(2,1)S(1)} %copy-done.6, ...), custom_call_target="tpu_custom_call" | custom-call | tf_op jit(solution)/shard_map/pallas_call | solution.py:302
  44.0 3.0 %shard_map.123 = (bf16[2,8,256,512]{3,2,1,0:T(8,128)(2,1)S(1)}, f32[2,256,1024]{2,1,0:T(8,128)S(1)}, f32[2,256,1024]{2,1,0:T(8,128)S(1)}, f32[2,256,1024]{2,1,0:T(8,128)S(1)}) custom-call(bf16[2,256,1024]{2,1,0:T(8,128)(2,1)S(1)} %copy-done, ...), custom_call_target="tpu_custom_call", output_to_operand_aliasing={{1}: (3, {}), {2}: (4, {}), {3}: (5, {})} | custom-call | tf_op jit(solution)/shard_map/pallas_call | solution.py:302
  47.1 3.3 %shard_map.127 = (bf16[2,256,1024]{2,1,0:T(8,128)(2,1)}, bf16[4,2,2048]{2,1,0:T(2,128)(2,1)}, f32[72,128]{1,0:T(8,128)}) custom-call(s32[2]{0:T(128)S(1)} %copy-done.11, bf16[2,8,256,512]{3,2,1,0:T(8,128)(2,1)S(1)} %get-tuple-element.22.refs_1_, bf16[2,256,128]{2,1,0:T(8,128)(2,1)S(1)} %collective-permute-done.k_one.refs_2_, ...), custom_call_target="tpu_custom_call" | custom-call | tf_op jit(solution)/shard_map/pallas_call | solution.py:302
  (34 shorter events, 3.2 us)
Async XLA Ops:
  0.6 41.8 %copy-start = (bf16[2,256,1024]{2,1,0:T(8,128)(2,1)S(1)}, bf16[2,256,1024]{2,1,0:T(8,128)(2,1)}, u32[]{:S(2)}) copy-start(bf16[2,256,1024]{2,1,0:T(8,128)(2,1)} %q_ref.3) | copy-start | bytes 3145732
  0.6 8.6 %collective-permute-start = (bf16[2,256,128]{2,1,0:T(8,128)(2,1)}, bf16[2,256,128]{2,1,0:T(8,128)(2,1)S(1)}, u32[]{:S(2)}, u32[]{:S(2)}) collective-permute-start(bf16[2,256,128]{2,1,0:T(8,128)(2,1)} %refs_4_.1), channel_id=1, source_target_pairs={{0,16},{8,24},{1,17},{9,25},{2,18},{10,26},{3,19},{11,27},{4,20},{... | collective-permute-start | bytes 393224 | tf_op jit(solution)/shard_map/ppermute | solution.py:343
  2.1 8.9 %collective-permute-start.4 = (bf16[2,256,128]{2,1,0:T(8,128)(2,1)}, bf16[2,256,128]{2,1,0:T(8,128)(2,1)S(1)}, u32[]{:S(2)}, u32[]{:S(2)}) collective-permute-start(bf16[2,256,128]{2,1,0:T(8,128)(2,1)} %refs_5_.1), channel_id=1, source_target_pairs={{0,16},{8,24},{1,17},{9,25},{2,18},{10,26},{3,19},{11,27},{4,20},{... | collective-permute-start | bytes 393224 | tf_op jit(solution)/shard_map/ppermute | solution.py:343
  3.4 23.7 %collective-permute-start.2 = (bf16[2,256,128]{2,1,0:T(8,128)(2,1)}, bf16[2,256,128]{2,1,0:T(8,128)(2,1)S(1)}, u32[]{:S(2)}, u32[]{:S(2)}) collective-permute-start(bf16[2,256,128]{2,1,0:T(8,128)(2,1)} %refs_4_.1), channel_id=1, source_target_pairs={{0,8},{8,0},{16,24},{24,16},{1,9},{9,1},{17,25},{25,17},{2,10},{10... | collective-permute-start | bytes 393224 | tf_op jit(solution)/shard_map/ppermute | solution.py:340
  3.5 23.6 %collective-permute-start.3 = (bf16[2,256,128]{2,1,0:T(8,128)(2,1)}, bf16[2,256,128]{2,1,0:T(8,128)(2,1)S(1)}, u32[]{:S(2)}, u32[]{:S(2)}) collective-permute-start(bf16[2,256,128]{2,1,0:T(8,128)(2,1)} %refs_5_.1), channel_id=1, source_target_pairs={{0,8},{8,0},{16,24},{24,16},{1,9},{9,1},{17,25},{25,17},{2,10},{10... | collective-permute-start | bytes 393224 | tf_op jit(solution)/shard_map/ppermute | solution.py:340
  9.3 34.8 %collective-permute-start.1 = (bf16[2,256,128]{2,1,0:T(8,128)(2,1)S(1)}, bf16[2,256,128]{2,1,0:T(8,128)(2,1)S(1)}, u32[]{:S(2)}, u32[]{:S(2)}) collective-permute-start(bf16[2,256,128]{2,1,0:T(8,128)(2,1)S(1)} %collective-permute-done.k_one.refs_2_), channel_id=1, source_target_pairs={{0,8},{8,0},{16,24},{24,16},{1,9},{9,1},{17,25},{25,17},{2,10},{10... | collective-permute-start | bytes 393224 | tf_op jit(solution)/shard_map/ppermute | solution.py:340
  10.9 36.1 %collective-permute-start.5 = (bf16[2,256,128]{2,1,0:T(8,128)(2,1)S(1)}, bf16[2,256,128]{2,1,0:T(8,128)(2,1)S(1)}, u32[]{:S(2)}, u32[]{:S(2)}) collective-permute-start(bf16[2,256,128]{2,1,0:T(8,128)(2,1)S(1)} %collective-permute-done.4.refs_3_), channel_id=1, source_target_pairs={{0,8},{8,0},{16,24},{24,16},{1,9},{9,1},{17,25},{25,17},{2,10},{10... | collective-permute-start | bytes 393224 | tf_op jit(solution)/shard_map/ppermute | solution.py:340
  10.9 0.8 %copy-start.7 = (bf16[4,2,2048]{2,1,0:T(2,128)(2,1)S(1)}, bf16[4,2,2048]{2,1,0:T(2,128)(2,1)}, u32[]{:S(2)}) copy-start(bf16[4,2,2048]{2,1,0:T(2,128)(2,1)} %dq_ref.1) | copy-start | bytes 98308
  12.9 5.7 %collective-permute-start.8 = (bf16[80,128]{1,0:T(8,128)(2,1)S(1)}, bf16[80,128]{1,0:T(8,128)(2,1)S(1)}, u32[]{:S(2)}, u32[]{:S(2)}) collective-permute-start(bf16[80,128]{1,0:T(8,128)(2,1)S(1)} %get-tuple-element.25.own_ref.refs_0_.refs_8_), channel_id=1, source_target_pairs={{0,16},{8,24},{1,17},{9,25},{2,18},{10,26},{3,19},{11,27},{4,20},{... | collective-permute-start | bytes 61448 | tf_op jit(solution)/shard_map/ppermute | solution.py:343
  18.6 3.8 %collective-permute-start.6 = (bf16[80,128]{1,0:T(8,128)(2,1)S(1)}, bf16[80,128]{1,0:T(8,128)(2,1)S(1)}, u32[]{:S(2)}, u32[]{:S(2)}) collective-permute-start(bf16[80,128]{1,0:T(8,128)(2,1)S(1)} %get-tuple-element.26.other_ref), channel_id=1, source_target_pairs={{0,1},{1,0},{8,9},{9,8},{16,17},{17,16},{24,25},{25,24},{2,3},{3,2... | collective-permute-start | bytes 61448 | tf_op jit(solution)/shard_map/ppermute | solution.py:352
  22.4 4.7 %collective-permute-start.7 = (bf16[80,128]{1,0:T(8,128)(2,1)S(1)}, bf16[80,128]{1,0:T(8,128)(2,1)S(1)}, u32[]{:S(2)}, u32[]{:S(2)}) collective-permute-start(bf16[80,128]{1,0:T(8,128)(2,1)S(1)} %get-tuple-element.26.other_ref), channel_id=1, source_target_pairs={{0,17},{1,16},{8,25},{9,24},{16,1},{17,0},{24,9},{25,8},{2,19},{3,... | collective-permute-start | bytes 61448 | tf_op jit(solution)/shard_map/ppermute | solution.py:352
  27.1 0.9 %copy-start.3 = (bf16[2,256,128]{2,1,0:T(8,128)(2,1)S(1)}, bf16[2,256,128]{2,1,0:T(8,128)(2,1)}, u32[]{:S(2)}) copy-start(bf16[2,256,128]{2,1,0:T(8,128)(2,1)} %refs_4_.1) | copy-start | bytes 393220
  28.0 0.9 %copy-start.5 = (bf16[2,256,128]{2,1,0:T(8,128)(2,1)S(1)}, bf16[2,256,128]{2,1,0:T(8,128)(2,1)}, u32[]{:S(2)}) copy-start(bf16[2,256,128]{2,1,0:T(8,128)(2,1)} %refs_5_.1) | copy-start | bytes 393220
  28.9 0.7 %copy-start.10 = (s32[2]{0:T(128)S(1)}, s32[2]{0:T(128)}, u32[]{:S(2)}) copy-start(s32[2]{0:T(128)} %refs_0_.1) | copy-start | bytes 28
  30.7 16.3 %collective-permute-start.10 = (f32[72,128]{1,0:T(8,128)S(1)}, f32[72,128]{1,0:T(8,128)S(1)}, u32[]{:S(2)}, u32[]{:S(2)}) collective-permute-start(f32[72,128]{1,0:T(8,128)S(1)} %get-tuple-element.32), channel_id=1, source_target_pairs={{0,1},{1,0},{8,9},{9,8},{16,17},{17,16},{24,25},{25,24},{2,3},{3,2... | collective-permute-start | bytes 110600 | tf_op jit(solution)/shard_map/ppermute | solution.py:352
  32.3 14.8 %collective-permute-start.11 = (f32[72,128]{1,0:T(8,128)S(1)}, f32[72,128]{1,0:T(8,128)S(1)}, u32[]{:S(2)}, u32[]{:S(2)}) collective-permute-start(f32[72,128]{1,0:T(8,128)S(1)} %get-tuple-element.33), channel_id=1, source_target_pairs={{0,17},{1,16},{8,25},{9,24},{16,1},{17,0},{24,9},{25,8},{2,19},{3,... | collective-permute-start | bytes 110600 | tf_op jit(solution)/shard_map/ppermute | solution.py:352
  32.3 14.8 %collective-permute-start.9 = (f32[72,128]{1,0:T(8,128)S(1)}, f32[72,128]{1,0:T(8,128)S(1)}, u32[]{:S(2)}, u32[]{:S(2)}) collective-permute-start(f32[72,128]{1,0:T(8,128)S(1)} %get-tuple-element.31), channel_id=1, source_target_pairs={{16,0},{24,8},{17,1},{25,9},{18,2},{26,10},{19,3},{27,11},{20,4},{... | collective-permute-start | bytes 110600 | tf_op jit(solution)/shard_map/ppermute | solution.py:346
  36.2 1.2 %copy-start.1 = (bf16[2,1024,256]{2,1,0:T(8,128)(2,1)S(1)}, bf16[2,1024,256]{2,1,0:T(8,128)(2,1)}, u32[]{:S(2)}) copy-start(bf16[2,1024,256]{2,1,0:T(8,128)(2,1)} %ck_ref.1) | copy-start | bytes 3145732
  37.4 1.2 %copy-start.2 = (bf16[2,1024,256]{2,1,0:T(8,128)(2,1)S(1)}, bf16[2,1024,256]{2,1,0:T(8,128)(2,1)}, u32[]{:S(2)}) copy-start(bf16[2,1024,256]{2,1,0:T(8,128)(2,1)} %cv_ref.1) | copy-start | bytes 3145732
  38.6 0.7 %copy-start.8 = (bf16[4,2,256]{2,1,0:T(2,128)(2,1)S(1)}, bf16[4,2,256]{2,1,0:T(2,128)(2,1)}, u32[]{:S(2)}) copy-start(bf16[4,2,256]{2,1,0:T(2,128)(2,1)} %nk_ref.1) | copy-start | bytes 12292
  39.3 0.7 %copy-start.9 = (bf16[4,2,256]{2,1,0:T(2,128)(2,1)S(1)}, bf16[4,2,256]{2,1,0:T(2,128)(2,1)}, u32[]{:S(2)}) copy-start(bf16[4,2,256]{2,1,0:T(2,128)(2,1)} %nv_ref.1) | copy-start | bytes 12292
  40.7 1.8 %copy-start.4 = (bf16[2,256,128]{2,1,0:T(8,128)(2,1)S(1)}, bf16[2,256,128]{2,1,0:T(8,128)(2,1)}, u32[]{:S(2)}) copy-start(bf16[2,256,128]{2,1,0:T(8,128)(2,1)} %refs_4_.1) | copy-start | bytes 393220
  40.7 1.8 %copy-start.6 = (bf16[2,256,128]{2,1,0:T(8,128)(2,1)S(1)}, bf16[2,256,128]{2,1,0:T(8,128)(2,1)}, u32[]{:S(2)}) copy-start(bf16[2,256,128]{2,1,0:T(8,128)(2,1)} %refs_5_.1) | copy-start | bytes 393220
  44.0 3.0 %copy-start.11 = (s32[2]{0:T(128)S(1)}, s32[2]{0:T(128)}, u32[]{:S(2)}) copy-start(s32[2]{0:T(128)} %refs_0_.1) | copy-start | bytes 28
  (2 other events, 1.3 us)

commit v2 on v1

v2 whole, which is shorter than its diff:
```python
import functools
import math

import jax
import jax.numpy as jnp
from jax import lax
from jax.experimental import pallas as pl
from jax.experimental.pallas import tpu as pltpu
from jax.sharding import PartitionSpec as P

D_HEAD = 128
MASKED_SCORE = -1e30
EXP2_SCALE = D_HEAD**-0.5 * math.log2(math.e)
VMEM_BYTES = 40 * 2**20
NT = (((1,), (1,)), ((), ()))


def scores_of(queries, keys):
    return lax.dot_general(queries, keys, NT, preferred_element_type=jnp.float32)


def weighted(weights, values):
    return jnp.dot(weights.astype(jnp.bfloat16), values, preferred_element_type=jnp.float32)


def eye_of(rows):
    shape = (rows, 128)
    return lax.broadcasted_iota(jnp.int32, shape, 0) == lax.broadcasted_iota(jnp.int32, shape, 1)


def column_to_row(column):
    spread = jnp.where(eye_of(column.shape[0]), column, 0.0)
    return jnp.sum(spread, axis=0, keepdims=True)


def row_to_column(row, rows):
    spread = jnp.where(eye_of(rows), jnp.broadcast_to(row, (rows, 128)), 0.0)
    return jnp.sum(spread, axis=1, keepdims=True)


def select_rows(index, parts):
    chosen = parts[-1]
    for number in range(len(parts) - 2, -1, -1):
        chosen = jnp.where(index == number, parts[number], chosen)
    return chosen


def lane_sum(x):
    tiles = [x[:, i : i + 128] for i in range(0, x.shape[1], 128)]
    return jnp.sum(functools.reduce(jnp.add, tiles), axis=1, keepdims=True)


def lane_max(x):
    tiles = [x[:, i : i + 128] for i in range(0, x.shape[1], 128)]
    return jnp.max(functools.reduce(jnp.maximum, tiles), axis=1, keepdims=True)


def pack_kernel(
    dq_hbm, asg_hbm, plen_hbm, clen_hbm, nk_hbm, nv_hbm, own_ref, other_ref, info_ref, nk_ref, nv_ref, dq, nk, nv, asg, plen, clen, flat, sems
):
    moves = [(dq_hbm, dq), (asg_hbm, asg), (plen_hbm, plen), (clen_hbm, clen), (nk_hbm, nk), (nv_hbm, nv)]
    copies = [pltpu.make_async_copy(a, b, sems.at[i]) for i, (a, b) in enumerate(moves)]
    for copy in copies:
        copy.start()
    steps, rows, columns = dq.shape
    span = steps * rows
    role = lax.axis_index("role")
    half = columns // 2
    group = half // D_HEAD
    row_index = lax.broadcasted_iota(jnp.int32, (span, 128), 0)
    nk_ref[...] = jnp.zeros_like(nk_ref)
    nv_ref[...] = jnp.zeros_like(nv_ref)
    for copy in copies:
        copy.wait()
    for step in range(steps):
        flat[step * rows : (step + 1) * rows, :] = dq[step].astype(jnp.float32)
        nk_ref[step * rows : (step + 1) * rows, :] = nk[step].astype(jnp.float32)
        nv_ref[step * rows : (step + 1) * rows, :] = nv[step].astype(jnp.float32)
    prompt = jnp.zeros((span, 128), jnp.float32)
    for row in range(rows):
        prompt = jnp.where(row_index % rows == row, asg[row].astype(jnp.float32), prompt)
    info = jnp.zeros((span, 128), jnp.int32)
    for row in range(plen.shape[0]):
        info = jnp.where(row_index == row, plen[row], info)
    for row in range(rows):
        info = jnp.where(row_index == 4 + row, clen[row], info)
    info_ref[...] = info
    for out, kv in ((own_ref, role), (other_ref, 1 - role)):
        for pair in range(group // 2):
            two = [
                flat[:, pl.ds(pl.multiple_of(kv * half + (2 * pair + i) * D_HEAD, D_HEAD), D_HEAD)] for i in (0, 1)
            ]
            out[2 * span * pair : 2 * span * (pair + 1), :] = jnp.concatenate(two, axis=0).astype(jnp.bfloat16)
        out[span * group : span * (group + 2), :] = jnp.concatenate([prompt, prompt], axis=0).astype(jnp.bfloat16)


def cache_kernel(rows, steps, info_ref, own_ref, other_ref, ck_ref, cv_ref, nk_ref, nv_ref, sum_ref, top_ref, tot_ref):
    span = steps * rows
    queries = own_ref.shape[0] - 2 * span
    role = lax.axis_index("role")
    slots = ck_ref.shape[1]
    q_index = lax.broadcasted_iota(jnp.int32, (queries, 1), 0) % span
    q_step, q_row = q_index // rows, q_index % rows
    lane = lax.broadcasted_iota(jnp.int32, (queries, 128), 1)
    fresh_mask = (lane < span) & (lane % rows == q_row) & (lane // rows <= q_step)
    limit = select_rows(q_row, [jnp.broadcast_to(info_ref[4 + r : 5 + r, :1], (queries, 1)) for r in range(rows)])
    live = lax.broadcasted_iota(jnp.int32, (queries, slots), 1) < limit
    for index, (message, kv) in enumerate(((own_ref, role), (other_ref, 1 - role))):
        q = message[:queries, :]
        columns = pl.ds(pl.multiple_of(kv * D_HEAD, D_HEAD), D_HEAD)
        fresh = scores_of(q, nk_ref[:, columns].astype(jnp.bfloat16))
        fresh = jnp.where(fresh_mask, fresh * EXP2_SCALE, MASKED_SCORE)
        old = select_rows(q_row, [scores_of(q, ck_ref[r, :, columns]) for r in range(rows)])
        old = jnp.where(live, old * EXP2_SCALE, MASKED_SCORE)
        top = jnp.maximum(lane_max(fresh), lane_max(old))
        fresh = jnp.exp2(fresh - top)
        old = jnp.exp2(old - top)
        total = lane_sum(fresh) + lane_sum(old)
        summed = weighted(fresh, nv_ref[:, columns].astype(jnp.bfloat16))
        for r in range(rows):
            summed = summed + weighted(jnp.where(q_row == r, old, 0.0), cv_ref[r, :, columns])
        sum_ref[index] = summed
        top_ref[index] = jnp.broadcast_to(top, (queries, 128))
        tot_ref[index] = jnp.broadcast_to(total, (queries, 128))


def jobs_kernel(span, count, *refs):
    messages = refs[:count]
    info_ref, k_own, v_own, k_near, v_near, _ = refs[count : count + 6]
    outs = refs[count + 6 : -1]
    wide = refs[-1]
    queries = messages[0].shape[0] - 2 * span
    seq = lax.axis_index("seq")
    prompts, length, _ = k_own.shape
    wide[:, :length, :D_HEAD] = v_own[...]
    wide[:, length:, :D_HEAD] = v_near[...]
    wide[:, :, D_HEAD:] = jnp.ones((prompts, 2 * length, D_HEAD), jnp.bfloat16)
    q = jnp.concatenate([m[:queries, :] for m in messages], axis=0)
    columns = []
    for m in messages:
        eight = m[queries : queries + 2 * span, :].astype(jnp.float32)[:span, :1]
        columns += [eight] * (queries // span)
    prompt = jnp.concatenate(columns, axis=0).astype(jnp.int32)
    limit = select_rows(prompt, [jnp.broadcast_to(info_ref[r : r + 1, :1], prompt.shape) for r in range(prompts)])
    parts = []
    for first, keys in ((seq * length, k_own), ((seq + 1 - 2 * (seq % 2)) * length, k_near)):
        position = first + lax.broadcasted_iota(jnp.int32, (q.shape[0], length), 1)
        part = select_rows(prompt, [scores_of(q, keys[r]) for r in range(prompts)])
        parts.append(jnp.where(position < limit, part * EXP2_SCALE, MASKED_SCORE))
    scores = jnp.concatenate(parts, axis=1)
    top = lane_max(scores)
    weights = jnp.exp2(scores - jnp.maximum(top, 0.5 * MASKED_SCORE))
    summed = jnp.zeros((q.shape[0], 2 * D_HEAD), jnp.float32)
    for r in range(prompts):
        summed = summed + weighted(jnp.where(prompt == r, weights, 0.0), wide[r])
    for index, out in enumerate(outs):
        rows = slice(index * queries, (index + 1) * queries)
        out[:queries, :] = summed[rows, :D_HEAD]
        out[queries : queries + 8, :] = jnp.concatenate(
            [column_to_row(top[rows]), column_to_row(summed[rows, D_HEAD:]), jnp.zeros((6, 128), jnp.float32)], axis=0
        )


def local_kernel(q_ref, k_own, k_near, wide, _, sum_ref, top_ref, tot_ref):
    prompts, length, columns = q_ref.shape
    group = columns // D_HEAD
    seq = lax.axis_index("seq")
    causal = lax.broadcasted_iota(jnp.int32, (length, length), 1) <= lax.broadcasted_iota(
        jnp.int32, (length, length), 0
    )

    def run(with_near):
        for row in range(prompts):
            for head in range(group):
                cols = slice(head * D_HEAD, (head + 1) * D_HEAD)
                q = q_ref[row, :, cols]
                scores = jnp.where(causal, scores_of(q, k_own[row]), MASKED_SCORE)
                if with_near:
                    scores = jnp.concatenate([scores, scores_of(q, k_near[row])], axis=1)
                top = jnp.max(scores, axis=1, keepdims=True) * EXP2_SCALE
                weights = jnp.exp2(scores * EXP2_SCALE - top)
                summed = weighted(weights, wide[row, : scores.shape[1], :])
                sum_ref[row, :, cols] = summed[:, :D_HEAD]
                tot_ref[row, :, cols] = summed[:, D_HEAD:]
                top_ref[row, :, cols] = jnp.broadcast_to(top, (length, D_HEAD))

    @pl.when(seq % 2 == 0)
    def _():
        run(False)

    @pl.when(seq % 2 == 1)
    def _():
        run(True)


def merge_kernel(span, n_own, n_other, group, *refs):
    cache_sum, cache_top, cache_tot = refs[:3]
    own_parts = refs[3 : 3 + n_own]
    other_parts = refs[3 + n_own : 3 + n_own + n_other]
    dec_ref, flat = refs[-2:]
    role = lax.axis_index("role")
    queries = group * span
    half = group * D_HEAD
    for index, (parts, kv) in enumerate(((own_parts, role), (other_parts, 1 - role))):
        sums, tops, tots = [cache_sum[index]], [cache_top[index][:, :1]], [cache_tot[index][:, :1]]
        for part in parts:
            sums.append(part[:queries, :])
            tops.append(row_to_column(part[queries : queries + 1, :], queries))
            tots.append(row_to_column(part[queries + 1 : queries + 2, :], queries))
        high = functools.reduce(jnp.maximum, tops)
        factors = [jnp.exp2(top - high) for top in tops]
        summed = functools.reduce(jnp.add, [f * s for f, s in zip(factors, sums)])
        total = functools.reduce(jnp.add, [f * t for f, t in zip(factors, tots)])
        result = summed / total
        for head in range(group):
            start = pl.multiple_of(kv * half + head * D_HEAD, D_HEAD)
            flat[:, pl.ds(start, D_HEAD)] = result[head * span : (head + 1) * span]
    steps, rows, _ = dec_ref.shape
    for step in range(steps):
        dec_ref[step] = flat[step * rows : (step + 1) * rows, :].astype(jnp.bfloat16)


def far_kernel(shift, last, info_ref, q_ref, k_one, v_one, k_two, v_two, sum_in, top_in, tot_in, _, *refs):
    prompts, length, columns = q_ref.shape
    group = columns // D_HEAD
    seq = lax.axis_index("seq")
    if last:
        out_hbm, out, wide, sems = refs
    else:
        sum_ref, top_ref, tot_ref, wide = refs

    def finish(row, cols, summed, top, total):
        if last:
            position = seq * length + lax.broadcasted_iota(jnp.int32, (length, D_HEAD), 0)
            live = position < info_ref[row : row + 1, :]
            out[row, :, cols] = jnp.where(live, summed / total, 0.0).astype(jnp.bfloat16)
        else:
            sum_ref[row, :, cols] = summed
            top_ref[row, :, cols] = top
            tot_ref[row, :, cols] = total

    def moves(row, part):
        wide_cols = slice(part * columns // 2, (part + 1) * columns // 2)
        return pltpu.make_async_copy(
            out.at[row, :, wide_cols], out_hbm.at[row, :, wide_cols], sems.at[row * 2 + part]
        )

    def run(with_far):
        for row in range(prompts):
            for head in range(group):
                cols = slice(head * D_HEAD, (head + 1) * D_HEAD)
                summed, total = sum_in[row, :, cols], tot_in[row, :, cols]
                top = top_in[row, :, cols]
                if with_far:
                    q = q_ref[row, :, cols]
                    scores = jnp.concatenate([scores_of(q, k_one[row]), scores_of(q, k_two[row])], axis=1)
                    new = jnp.maximum(top, jnp.max(scores, axis=1, keepdims=True) * EXP2_SCALE)
                    high = jnp.concatenate([new] * (2 * length // D_HEAD), axis=1)
                    far = weighted(jnp.exp2(scores * EXP2_SCALE - high), wide[row])
                    alpha = jnp.exp2(top - new)
                    summed = summed * alpha + far[:, :D_HEAD]
                    total = total * alpha + far[:, D_HEAD:]
                    top = new
                finish(row, cols, summed, top, total)
                if last and (head + 1) % (group // 2) == 0:
                    moves(row, (head + 1) // (group // 2) - 1).start()

    @pl.when(seq // 2 >= shift)
    def _():
        wide[:, :length, :D_HEAD] = v_one[...]
        wide[:, length:, :D_HEAD] = v_two[...]
        wide[:, :, D_HEAD:] = jnp.ones((prompts, 2 * length, D_HEAD), jnp.bfloat16)
        run(True)

    @pl.when(seq // 2 < shift)
    def _():
        run(False)

    if last:
        for row in range(prompts):
            for part in range(2):
                moves(row, part).wait()


VMEM = pl.BlockSpec(memory_space=pltpu.VMEM)
ANY = pl.BlockSpec(memory_space=pl.ANY)


def in_hbm(x):
    return pltpu.with_memory_space_constraint(x, pltpu.HBM)


def call(kernel, args, outs, scratch=(), specs=None, out_specs=None, us=1.0):
    return pl.pallas_call(
        kernel,
        out_shape=outs,
        in_specs=specs or [VMEM] * len(args),
        out_specs=out_specs or [VMEM] * len(outs),
        scratch_shapes=list(scratch),
        compiler_params=pltpu.CompilerParams(vmem_limit_bytes=VMEM_BYTES),
        cost_estimate=pl.CostEstimate(flops=int(us * 1.1e9), bytes_accessed=int(us * 3e6), transcendentals=0),
    )(*args)


def body(
    prefill_queries,
    prefill_keys,
    prefill_values,
    prompt_len,
    assignment,
    cache_len,
    cache_keys,
    cache_values,
    decode_queries,
    new_keys,
    new_values,
):
    seqs, roles = lax.axis_size("seq"), lax.axis_size("role")
    pairs = seqs // 2
    prompts, length, columns = prefill_queries.shape
    steps, rows, dec_columns = decode_queries.shape
    group = columns // D_HEAD
    span = steps * rows
    queries = group * span
    f32, bf16, i32 = jnp.float32, jnp.bfloat16, jnp.int32
    shape = jax.ShapeDtypeStruct

    def near(x):
        return lax.ppermute(x, "seq", [(i, i ^ 1) for i in range(seqs)])

    def forward(x, shift):
        return lax.ppermute(x, "seq", [(i, i + 2 * shift) for i in range(seqs - 2 * shift)])

    def around(x, shift, flip):
        moves = [
            (i * roles + r, (i + 2 * shift) % seqs * roles + (1 - r if flip else r))
            for i in range(seqs)
            for r in range(roles)
        ]
        return lax.ppermute(x, ("seq", "role"), moves)

    shifts = range(1, pairs)
    far_keys = [forward(prefill_keys, s) for s in shifts]
    far_values = [forward(prefill_values, s) for s in shifts]
    near_keys, near_values = near(prefill_keys), near(prefill_values)
    message = shape((queries + 2 * span, 128), bf16)
    small = [decode_queries, assignment, prompt_len, cache_len, new_keys, new_values]
    own_msg, other_msg, info, fresh_keys, fresh_values = call(
        pack_kernel,
        [in_hbm(x) for x in small],
        [message] * 2 + [shape((span, 128), i32)] + [shape((128, 2 * D_HEAD), f32)] * 2,
        [
            pltpu.VMEM(decode_queries.shape, bf16),
            pltpu.VMEM(new_keys.shape, bf16),
            pltpu.VMEM(new_values.shape, bf16),
            pltpu.SMEM(assignment.shape, i32),
            pltpu.SMEM(prompt_len.shape, i32),
            pltpu.SMEM(cache_len.shape, i32),
            pltpu.VMEM((span, dec_columns), f32),
            pltpu.SemaphoreType.DMA((6,)),
        ],
        specs=[ANY] * 6,
        us=1.0,
    )
    other_msgs = [around(other_msg, s, True) for s in range(pairs)]
    own_msgs = [own_msg] + [around(own_msg, s, False) for s in shifts]
    state = shape((2, queries, 128), f32)
    cache_parts = call(
        functools.partial(cache_kernel, rows, steps),
        (info, own_msg, other_msg, cache_keys, cache_values, fresh_keys, fresh_values),
        [state] * 3,
        us=1.2,
    )
    messages = own_msgs + other_msgs
    part = shape((queries + 8, 128), f32)
    *parts, wide = call(
        functools.partial(jobs_kernel, span, len(messages)),
        (*messages, info, prefill_keys, prefill_values, near_keys, near_values, cache_parts[0]),
        [part] * len(messages) + [shape((prompts, 2 * length, 2 * D_HEAD), bf16)],
        specs=[VMEM] * (len(messages) + 5) + [ANY],
        us=0.8,
    )
    own_parts = [parts[0]] + [around(parts[s], -s, False) for s in shifts]
    other_parts = [around(parts[pairs + s], -s, True) for s in range(pairs)]
    run = shape((prompts, length, columns), f32)
    summed, top, total = call(
        local_kernel,
        (prefill_queries, prefill_keys, near_keys, wide, parts[0]),
        [run] * 3,
        specs=[VMEM] * 4 + [ANY],
        us=2.5,
    )
    (decode_out,) = call(
        functools.partial(merge_kernel, span, len(own_parts), len(other_parts), group),
        (*cache_parts, *own_parts, *other_parts, total),
        [shape(decode_queries.shape, bf16)],
        [pltpu.VMEM((span, dec_columns), f32)],
        specs=[VMEM] * (3 + 2 * pairs) + [ANY],
        us=0.6,
    )
    for index, shift in enumerate(shifts):
        last = shift == pairs - 1
        k_one, v_one = far_keys[index], far_values[index]
        k_two, v_two = near(k_one), near(v_one)
        args = (info, prefill_queries, k_one, v_one, k_two, v_two, summed, top, total, decode_out)
        wide_scratch = pltpu.VMEM((prompts, 2 * length, 2 * D_HEAD), bf16)
        kernel = functools.partial(far_kernel, shift, last)
        specs = [VMEM] * (len(args) - 1) + [ANY]
        if last:
            (prefill_out,) = call(
                kernel,
                args,
                [shape(prefill_queries.shape, bf16)],
                [pltpu.VMEM(prefill_queries.shape, bf16), wide_scratch, pltpu.SemaphoreType.DMA((2 * prompts,))],
                specs=specs,
                out_specs=[ANY],
                us=3.0,
            )
        else:
            summed, top, total = call(kernel, args, [run] * 3, [wide_scratch], specs=specs, us=3.0)
    return (prefill_out, decode_out)


def solution(mesh):
    in_specs = (
        P(None, "seq", ("head", "role")),
        P(None, "seq", ("head", "role")),
        P(None, "seq", ("head", "role")),
        P(),
        P(("seq", "role")),
        P(("seq", "role")),
        P(("seq", "role"), None, "head"),
        P(("seq", "role"), None, "head"),
        P(None, ("seq", "role"), "head"),
        P(None, ("seq", "role"), "head"),
        P(None, ("seq", "role"), "head"),
    )
    out_specs = (P(None, "seq", ("head", "role")), P(None, ("seq", "role"), "head"))
    return jax.shard_map(body, mesh=mesh, in_specs=in_specs, out_specs=out_specs, check_vma=False)
```

time: 50.9 us -> 27.1 us (0.53)
  waiting for transfers between devices: 17.7 us -> 3.91 us
  local copies, waits for them, and re-layouts: 8.36 us -> 0.78 us
  Pallas kernels: 11.4 us -> 9.83 us
  starting transfers between devices: 12.2 us -> 11.6 us
    ppermute x3 -> x2, waiting for transfers between devices: 11.3 us -> 0.01 us  [forward(): lax.ppermute(x, 'seq', [(i, i + 2 * shift) for i in range(seqs - 2 * shif...]
    unnamed x28 -> x12, local copies, waits for them, and re-layouts: 8.36 us -> 0.78 us
    ppermute x9 -> x10, waiting for transfers between devices: 6.34 us -> 3.9 us  [the longest x6 3.89 us: around(): return lax.ppermute(x, ('seq', 'role'), moves)]
    pallas_call x6, Pallas kernels: 11.4 us -> 9.83 us  [call(): pl.pallas_call(kernel, out_shape=outs, in_specs=specs or [VMEM] * len(arg...]
    ppermute x3 -> x2, starting transfers between devices: 4.01 us -> 2.57 us  [forward(): lax.ppermute(x, 'seq', [(i, i + 2 * shift) for i in range(seqs - 2 * shif...]
    ppermute x9 -> x10, starting transfers between devices: 8.16 us -> 9.06 us  [the longest x6 8.04 us: around(): return lax.ppermute(x, ('seq', 'role'), moves)]
  transfers between devices with their start and end apart: 12 -> 12, of which waited for: 5 -> 3; matrix products, arithmetic and copies ran while one was open for 0% -> 0% of each run, Pallas kernels for 16% -> 17%
where the time goes in v2:
time: 27.1 us; the launch traced here: 26.9 us
  starting transfers between devices  11.6 us (43%)
  Pallas kernels  9.83 us (36%)
  waiting for transfers between devices  3.91 us (14%)
  local copies, waits for them, and re-layouts  0.78 us (3%)
  between operations  0.76 us (3%)
    pallas_call x6, Pallas kernels, call(): pl.pallas_call(kernel, out_shape=outs, in_specs=specs or [VMEM] * len(arg...  9.83 us
    ppermute x6, starting transfers between devices, around(): return lax.ppermute(x, ('seq', 'role'), moves)  8.04 us
    ppermute x6, waiting for transfers between devices, around(): return lax.ppermute(x, ('seq', 'role'), moves)  3.89 us
    ppermute x2, starting transfers between devices, forward(): lax.ppermute(x, 'seq', [(i, i + 2 * shift) for i in range(seqs - 2 * shif...  2.57 us
    ppermute x4, starting transfers between devices, near(): return lax.ppermute(x, 'seq', [(i, i ^ 1) for i in range(seqs)])  1.02 us
    unnamed x12, local copies, waits for them, and re-layouts  0.78 us
  transfers between devices with their start and end apart: 12, of which 3 were waited for; matrix products, arithmetic and copies ran while one was open for 0% of the time, Pallas kernels for 17%

profile of v2, /device:TPU:28, one launch (start us, length us, event | category | flops | bytes accessed | tf_op | source)
XLA Modules:
  0.0 26.9 jit_solution(15330239428815129880)
XLA Ops:
  0.7 1.0 %shard_map.122 = (bf16[80,128]{1,0:T(8,128)(2,1)S(1)}, bf16[80,128]{1,0:T(8,128)(2,1)S(1)}, s32[8,128]{1,0:T(8,128)S(1)}, f32[128,256]{1,0:T(8,128)S(1)}, f32[128,256]{1,0:T(8,128)S(1)}) custom-call(bf16[4,2,2048]{2,1,0:T(2,128)(2,1)} %dq_hbm.1, s32[2]{0:T(128)} %asg_hbm.1, s32[2]{0:T(128)} %plen_hbm.1, s32[2]{0:T(128)} %clen_hbm.1, ...), custom_call_target="tpu_custom_call" | custom-call | flops 1100000000 | bytes 3000000 | tf_op jit(solution)/shard_map/pallas_call | solution.py:294
  1.7 0.6 %collective-permute-start.5 = (bf16[80,128]{1,0:T(8,128)(2,1)S(1)}, bf16[80,128]{1,0:T(8,128)(2,1)S(1)}, u32[]{:S(2)}, u32[]{:S(2)}) collective-permute-start(bf16[80,128]{1,0:T(8,128)(2,1)S(1)} %get-tuple-element.19.own_ref.refs_0_), channel_id=1, source_target_pairs={{0,16},{1,17},{8,24},{9,25},{16,0},{17,1},{24,8},{25,9},{2,18},{3,... | collective-permute-start | bytes 61448 | tf_op jit(solution)/shard_map/ppermute | solution.py:340
  2.3 2.4 %collective-permute-start.7 = (bf16[80,128]{1,0:T(8,128)(2,1)S(1)}, bf16[80,128]{1,0:T(8,128)(2,1)S(1)}, u32[]{:S(2)}, u32[]{:S(2)}) collective-permute-start(bf16[80,128]{1,0:T(8,128)(2,1)S(1)} %get-tuple-element.20.other_ref), channel_id=1, source_target_pairs={{0,17},{1,16},{8,25},{9,24},{16,1},{17,0},{24,9},{25,8},{2,19},{3,... | collective-permute-start | bytes 61448 | tf_op jit(solution)/shard_map/ppermute | solution.py:340
  4.7 0.5 %collective-permute-start.4 = (bf16[2,256,128]{2,1,0:T(8,128)(2,1)S(1)}, bf16[2,256,128]{2,1,0:T(8,128)(2,1)S(1)}, u32[]{:S(2)}, u32[]{:S(2)}) collective-permute-start(bf16[2,256,128]{2,1,0:T(8,128)(2,1)S(1)} %copy-done.5), channel_id=1, source_target_pairs={{0,8},{8,0},{16,24},{24,16},{1,9},{9,1},{17,25},{25,17},{2,10},{10... | collective-permute-start | bytes 393224 | tf_op jit(solution)/shard_map/ppermute | solution.py:329
  5.2 1.3 %collective-permute-start.1 = (bf16[2,256,128]{2,1,0:T(8,128)(2,1)S(1)}, bf16[2,256,128]{2,1,0:T(8,128)(2,1)S(1)}, u32[]{:S(2)}, u32[]{:S(2)}) collective-permute-start(bf16[2,256,128]{2,1,0:T(8,128)(2,1)S(1)} %copy-done.4), channel_id=1, source_target_pairs={{0,16},{8,24},{1,17},{9,25},{2,18},{10,26},{3,19},{11,27},{4,20},{... | collective-permute-start | bytes 393224 | tf_op jit(solution)/shard_map/ppermute | solution.py:332
  6.5 1.3 %collective-permute-start = (bf16[2,256,128]{2,1,0:T(8,128)(2,1)S(1)}, bf16[2,256,128]{2,1,0:T(8,128)(2,1)S(1)}, u32[]{:S(2)}, u32[]{:S(2)}) collective-permute-start(bf16[2,256,128]{2,1,0:T(8,128)(2,1)S(1)} %copy-done.5), channel_id=1, source_target_pairs={{0,16},{8,24},{1,17},{9,25},{2,18},{10,26},{3,19},{11,27},{4,20},{... | collective-permute-start | bytes 393224 | tf_op jit(solution)/shard_map/ppermute | solution.py:332
  7.8 0.0 collective-permute-done.7.refs_3_
  7.9 0.8 %collective-permute-start.6 = (bf16[80,128]{1,0:T(8,128)(2,1)S(1)}, bf16[80,128]{1,0:T(8,128)(2,1)S(1)}, u32[]{:S(2)}, u32[]{:S(2)}) collective-permute-start(bf16[80,128]{1,0:T(8,128)(2,1)S(1)} %get-tuple-element.20.other_ref), channel_id=1, source_target_pairs={{0,1},{1,0},{8,9},{9,8},{16,17},{17,16},{24,25},{25,24},{2,3},{3,2... | collective-permute-start | bytes 61448 | tf_op jit(solution)/shard_map/ppermute | solution.py:340
  8.6 1.1 %shard_map.123 = (f32[2,64,128]{2,1,0:T(8,128)S(1)}, f32[2,64,128]{2,1,0:T(8,128)S(1)}, f32[2,64,128]{2,1,0:T(8,128)S(1)}) custom-call(s32[8,128]{1,0:T(8,128)S(1)} %get-tuple-element.18.info_ref.refs_4_, bf16[80,128]{1,0:T(8,128)(2,1)S(1)} %get-tuple-element.19.own_ref.refs_0_, bf16[80,128]{1,0:T(8,128)(2,1)S(1)} %get-tuple-element.20.other_ref, ...), custom_call_target="tpu_custom_call" | custom-call | flops 1320000000 | bytes 3600000 | tf_op jit(solution)/shard_map/pallas_call | solution.py:294
  9.8 0.0 copy-start.3
  9.8 1.9 %collective-permute-done.6.refs_2_ = bf16[80,128]{1,0:T(8,128)(2,1)S(1)} collective-permute-done((bf16[80,128]{1,0:T(8,128)(2,1)S(1)}, bf16[80,128]{1,0:T(8,128)(2,1)S(1)}, u32[]{:S(2)}, u32[]{:S(2)}) %collective-permute-start.6) | collective-permute-done | bytes 20512 | tf_op jit(solution)/shard_map/ppermute | solution.py:340
  11.7 0.0 collective-permute-done.8.refs_8_
  11.7 0.0 collective-permute-done.4.refs_7_.k_near
  11.7 0.9 %shard_map.124 = (f32[72,128]{1,0:T(8,128)S(1)}, f32[72,128]{1,0:T(8,128)S(1)}, f32[72,128]{1,0:T(8,128)S(1)}, f32[72,128]{1,0:T(8,128)S(1)}, bf16[2,512,256]{2,1,0:T(8,128)(2,1)S(1)}) custom-call(bf16[80,128]{1,0:T(8,128)(2,1)S(1)} %get-tuple-element.19.own_ref.refs_0_, bf16[80,128]{1,0:T(8,128)(2,1)S(1)} %collective-permute-done.5.refs_1_, ...), custom_call_target="tpu_custom_call" | custom-call | flops 880000000 | bytes 2400000 | tf_op jit(solution)/shard_map/pallas_call | solution.py:294
  12.6 2.7 %collective-permute-start.9 = (f32[72,128]{1,0:T(8,128)S(1)}, f32[72,128]{1,0:T(8,128)S(1)}, u32[]{:S(2)}, u32[]{:S(2)}) collective-permute-start(f32[72,128]{1,0:T(8,128)S(1)} %get-tuple-element.31), channel_id=1, source_target_pairs={{0,16},{1,17},{8,24},{9,25},{16,0},{17,1},{24,8},{25,9},{2,18},{3,... | collective-permute-start | bytes 110600 | tf_op jit(solution)/shard_map/ppermute | solution.py:340
  15.3 0.7 %collective-permute-start.10 = (f32[72,128]{1,0:T(8,128)S(1)}, f32[72,128]{1,0:T(8,128)S(1)}, u32[]{:S(2)}, u32[]{:S(2)}) collective-permute-start(f32[72,128]{1,0:T(8,128)S(1)} %get-tuple-element.32), channel_id=1, source_target_pairs={{0,1},{1,0},{8,9},{9,8},{16,17},{17,16},{24,25},{25,24},{2,3},{3,2... | collective-permute-start | bytes 110600 | tf_op jit(solution)/shard_map/ppermute | solution.py:340
  16.0 0.8 %collective-permute-start.11 = (f32[72,128]{1,0:T(8,128)S(1)}, f32[72,128]{1,0:T(8,128)S(1)}, u32[]{:S(2)}, u32[]{:S(2)}) collective-permute-start(f32[72,128]{1,0:T(8,128)S(1)} %get-tuple-element.33), channel_id=1, source_target_pairs={{0,17},{1,16},{8,25},{9,24},{16,1},{17,0},{24,9},{25,8},{2,19},{3,... | collective-permute-start | bytes 110600 | tf_op jit(solution)/shard_map/ppermute | solution.py:340
  16.9 0.5 %collective-permute-start.2 = (bf16[2,256,128]{2,1,0:T(8,128)(2,1)S(1)}, bf16[2,256,128]{2,1,0:T(8,128)(2,1)S(1)}, u32[]{:S(2)}, u32[]{:S(2)}) collective-permute-start(bf16[2,256,128]{2,1,0:T(8,128)(2,1)S(1)} %collective-permute-done.k_one), channel_id=1, source_target_pairs={{0,8},{8,0},{16,24},{24,16},{1,9},{9,1},{17,25},{25,17},{2,10},{10... | collective-permute-start | bytes 393224 | tf_op jit(solution)/shard_map/ppermute | solution.py:329
  17.4 1.5 %shard_map.125 = (f32[2,256,1024]{2,1,0:T(8,128)S(1)}, f32[2,256,1024]{2,1,0:T(8,128)S(1)}, f32[2,256,1024]{2,1,0:T(8,128)S(1)}) custom-call(bf16[2,256,1024]{2,1,0:T(8,128)(2,1)S(1)} %copy-done.3, bf16[2,256,128]{2,1,0:T(8,128)(2,1)S(1)} %copy-done.5, bf16[2,256,128]{2,1,0:T(8,128)(2,1)S(1)} %collective-permute-done.4.refs_7_.k_near, ...), custom_call_target="tpu_custom_call" | custom-call | flops 2750000128 | bytes 7500000 | tf_op jit(solution)/shard_map/pallas_call | solution.py:294
  18.9 0.4 %collective-permute-done.10.refs_5_ = f32[72,128]{1,0:T(8,128)S(1)} collective-permute-done((f32[72,128]{1,0:T(8,128)S(1)}, f32[72,128]{1,0:T(8,128)S(1)}, u32[]{:S(2)}, u32[]{:S(2)}) %collective-permute-start.10) | collective-permute-done | bytes 36896 | tf_op jit(solution)/shard_map/ppermute | solution.py:340
  19.3 1.6 %collective-permute-done.11.refs_6_ = f32[72,128]{1,0:T(8,128)S(1)} collective-permute-done((f32[72,128]{1,0:T(8,128)S(1)}, f32[72,128]{1,0:T(8,128)S(1)}, u32[]{:S(2)}, u32[]{:S(2)}) %collective-permute-start.11) | collective-permute-done | bytes 36896 | tf_op jit(solution)/shard_map/ppermute | solution.py:340
  20.9 0.9 %shard_map.126._ = bf16[4,2,2048]{2,1,0:T(2,128)(2,1)} custom-call(f32[2,64,128]{2,1,0:T(8,128)S(1)} %get-tuple-element.23.refs_9_.refs_0_, f32[2,64,128]{2,1,0:T(8,128)S(1)} %get-tuple-element.29.refs_1_, f32[2,64,128]{2,1,0:T(8,128)S(1)} %get-tuple-element.30.refs_2_, f32[72,128]{1,0:T(8,128)S(1)} %get-tuple-element.25._.refs_3_, ...), custom_call_target="tpu_custom_call" | custom-call | flops 660000000 | bytes 1800000 | tf_op jit(solution)/shard_map/pallas_call | solution.py:294
  21.8 0.8 %copy-done = bf16[4,2,2048]{2,1,0:T(2,128)(2,1)S(1)} copy-done((bf16[4,2,2048]{2,1,0:T(2,128)(2,1)S(1)}, bf16[4,2,2048]{2,1,0:T(2,128)(2,1)}, u32[]{:S(2)}) %copy-start) | copy-done | bytes 32792
  22.6 4.3 %shard_map.127 = bf16[2,256,1024]{2,1,0:T(8,128)(2,1)} custom-call(s32[8,128]{1,0:T(8,128)S(1)} %get-tuple-element.18.info_ref.refs_4_, bf16[2,256,1024]{2,1,0:T(8,128)(2,1)S(1)} %copy-done.3, bf16[2,256,128]{2,1,0:T(8,128)(2,1)S(1)} %collective-permute-done.k_one, bf16[2,256,128]{2,1,0:T(8,128)(2,1)S(1)} %collective-permute-done.1.v_one, ...), custom_call_target="tpu_custom_call" | custom-call | flops 3300000000 | bytes 9000000 | tf_op jit(solution)/shard_map/pallas_call | solution.py:294
  (18 shorter events, 0.0 us)
Async XLA Ops:
  0.6 4.1 %copy-start.4 = (bf16[2,256,128]{2,1,0:T(8,128)(2,1)S(1)}, bf16[2,256,128]{2,1,0:T(8,128)(2,1)}, u32[]{:S(2)}) copy-start(bf16[2,256,128]{2,1,0:T(8,128)(2,1)} %refs_6_.1) | copy-start | bytes 393220
  0.6 4.1 %copy-start.5 = (bf16[2,256,128]{2,1,0:T(8,128)(2,1)S(1)}, bf16[2,256,128]{2,1,0:T(8,128)(2,1)}, u32[]{:S(2)}) copy-start(bf16[2,256,128]{2,1,0:T(8,128)(2,1)} %k_own.1) | copy-start | bytes 393220
  0.7 8.0 %copy-start.2 = (bf16[2,1024,256]{2,1,0:T(8,128)(2,1)S(1)}, bf16[2,1024,256]{2,1,0:T(8,128)(2,1)}, u32[]{:S(2)}) copy-start(bf16[2,1024,256]{2,1,0:T(8,128)(2,1)} %cv_ref.1) | copy-start | bytes 3145732
  0.7 8.0 %copy-start.1 = (bf16[2,1024,256]{2,1,0:T(8,128)(2,1)S(1)}, bf16[2,1024,256]{2,1,0:T(8,128)(2,1)}, u32[]{:S(2)}) copy-start(bf16[2,1024,256]{2,1,0:T(8,128)(2,1)} %ck_ref.1) | copy-start | bytes 3145732
  1.7 4.8 %collective-permute-start.5 = (bf16[80,128]{1,0:T(8,128)(2,1)S(1)}, bf16[80,128]{1,0:T(8,128)(2,1)S(1)}, u32[]{:S(2)}, u32[]{:S(2)}) collective-permute-start(bf16[80,128]{1,0:T(8,128)(2,1)S(1)} %get-tuple-element.19.own_ref.refs_0_), channel_id=1, source_target_pairs={{0,16},{1,17},{8,24},{9,25},{16,0},{17,1},{24,8},{25,9},{2,18},{3,... | collective-permute-start | bytes 61448 | tf_op jit(solution)/shard_map/ppermute | solution.py:340
  2.3 5.6 %collective-permute-start.7 = (bf16[80,128]{1,0:T(8,128)(2,1)S(1)}, bf16[80,128]{1,0:T(8,128)(2,1)S(1)}, u32[]{:S(2)}, u32[]{:S(2)}) collective-permute-start(bf16[80,128]{1,0:T(8,128)(2,1)S(1)} %get-tuple-element.20.other_ref), channel_id=1, source_target_pairs={{0,17},{1,16},{8,25},{9,24},{16,1},{17,0},{24,9},{25,8},{2,19},{3,... | collective-permute-start | bytes 61448 | tf_op jit(solution)/shard_map/ppermute | solution.py:340
  4.7 7.0 %collective-permute-start.8 = (bf16[2,256,128]{2,1,0:T(8,128)(2,1)S(1)}, bf16[2,256,128]{2,1,0:T(8,128)(2,1)S(1)}, u32[]{:S(2)}, u32[]{:S(2)}) collective-permute-start(bf16[2,256,128]{2,1,0:T(8,128)(2,1)S(1)} %copy-done.4), channel_id=1, source_target_pairs={{0,8},{8,0},{16,24},{24,16},{1,9},{9,1},{17,25},{25,17},{2,10},{10... | collective-permute-start | bytes 393224 | tf_op jit(solution)/shard_map/ppermute | solution.py:329
  4.7 7.0 %collective-permute-start.4 = (bf16[2,256,128]{2,1,0:T(8,128)(2,1)S(1)}, bf16[2,256,128]{2,1,0:T(8,128)(2,1)S(1)}, u32[]{:S(2)}, u32[]{:S(2)}) collective-permute-start(bf16[2,256,128]{2,1,0:T(8,128)(2,1)S(1)} %copy-done.5), channel_id=1, source_target_pairs={{0,8},{8,0},{16,24},{24,16},{1,9},{9,1},{17,25},{25,17},{2,10},{10... | collective-permute-start | bytes 393224 | tf_op jit(solution)/shard_map/ppermute | solution.py:329
  5.2 11.6 %collective-permute-start.1 = (bf16[2,256,128]{2,1,0:T(8,128)(2,1)S(1)}, bf16[2,256,128]{2,1,0:T(8,128)(2,1)S(1)}, u32[]{:S(2)}, u32[]{:S(2)}) collective-permute-start(bf16[2,256,128]{2,1,0:T(8,128)(2,1)S(1)} %copy-done.4), channel_id=1, source_target_pairs={{0,16},{8,24},{1,17},{9,25},{2,18},{10,26},{3,19},{11,27},{4,20},{... | collective-permute-start | bytes 393224 | tf_op jit(solution)/shard_map/ppermute | solution.py:332
  6.5 10.3 %collective-permute-start = (bf16[2,256,128]{2,1,0:T(8,128)(2,1)S(1)}, bf16[2,256,128]{2,1,0:T(8,128)(2,1)S(1)}, u32[]{:S(2)}, u32[]{:S(2)}) collective-permute-start(bf16[2,256,128]{2,1,0:T(8,128)(2,1)S(1)} %copy-done.5), channel_id=1, source_target_pairs={{0,16},{8,24},{1,17},{9,25},{2,18},{10,26},{3,19},{11,27},{4,20},{... | collective-permute-start | bytes 393224 | tf_op jit(solution)/shard_map/ppermute | solution.py:332
  7.9 3.8 %collective-permute-start.6 = (bf16[80,128]{1,0:T(8,128)(2,1)S(1)}, bf16[80,128]{1,0:T(8,128)(2,1)S(1)}, u32[]{:S(2)}, u32[]{:S(2)}) collective-permute-start(bf16[80,128]{1,0:T(8,128)(2,1)S(1)} %get-tuple-element.20.other_ref), channel_id=1, source_target_pairs={{0,1},{1,0},{8,9},{9,8},{16,17},{17,16},{24,25},{25,24},{2,3},{3,2... | collective-permute-start | bytes 61448 | tf_op jit(solution)/shard_map/ppermute | solution.py:340
  9.8 7.6 %copy-start.3 = (bf16[2,256,1024]{2,1,0:T(8,128)(2,1)S(1)}, bf16[2,256,1024]{2,1,0:T(8,128)(2,1)}, u32[]{:S(2)}) copy-start(bf16[2,256,1024]{2,1,0:T(8,128)(2,1)} %q_ref.3) | copy-start | bytes 3145732
  12.6 6.3 %collective-permute-start.9 = (f32[72,128]{1,0:T(8,128)S(1)}, f32[72,128]{1,0:T(8,128)S(1)}, u32[]{:S(2)}, u32[]{:S(2)}) collective-permute-start(f32[72,128]{1,0:T(8,128)S(1)} %get-tuple-element.31), channel_id=1, source_target_pairs={{0,16},{1,17},{8,24},{9,25},{16,0},{17,1},{24,8},{25,9},{2,18},{3,... | collective-permute-start | bytes 110600 | tf_op jit(solution)/shard_map/ppermute | solution.py:340
  15.3 4.0 %collective-permute-start.10 = (f32[72,128]{1,0:T(8,128)S(1)}, f32[72,128]{1,0:T(8,128)S(1)}, u32[]{:S(2)}, u32[]{:S(2)}) collective-permute-start(f32[72,128]{1,0:T(8,128)S(1)} %get-tuple-element.32), channel_id=1, source_target_pairs={{0,1},{1,0},{8,9},{9,8},{16,17},{17,16},{24,25},{25,24},{2,3},{3,2... | collective-permute-start | bytes 110600 | tf_op jit(solution)/shard_map/ppermute | solution.py:340
  16.0 4.9 %collective-permute-start.11 = (f32[72,128]{1,0:T(8,128)S(1)}, f32[72,128]{1,0:T(8,128)S(1)}, u32[]{:S(2)}, u32[]{:S(2)}) collective-permute-start(f32[72,128]{1,0:T(8,128)S(1)} %get-tuple-element.33), channel_id=1, source_target_pairs={{0,17},{1,16},{8,25},{9,24},{16,1},{17,0},{24,9},{25,8},{2,19},{3,... | collective-permute-start | bytes 110600 | tf_op jit(solution)/shard_map/ppermute | solution.py:340
  16.9 4.9 %collective-permute-start.3 = (bf16[2,256,128]{2,1,0:T(8,128)(2,1)S(1)}, bf16[2,256,128]{2,1,0:T(8,128)(2,1)S(1)}, u32[]{:S(2)}, u32[]{:S(2)}) collective-permute-start(bf16[2,256,128]{2,1,0:T(8,128)(2,1)S(1)} %collective-permute-done.1.v_one), channel_id=1, source_target_pairs={{0,8},{8,0},{16,24},{24,16},{1,9},{9,1},{17,25},{25,17},{2,10},{10... | collective-permute-start | bytes 393224 | tf_op jit(solution)/shard_map/ppermute | solution.py:329
  16.9 4.9 %collective-permute-start.2 = (bf16[2,256,128]{2,1,0:T(8,128)(2,1)S(1)}, bf16[2,256,128]{2,1,0:T(8,128)(2,1)S(1)}, u32[]{:S(2)}, u32[]{:S(2)}) collective-permute-start(bf16[2,256,128]{2,1,0:T(8,128)(2,1)S(1)} %collective-permute-done.k_one), channel_id=1, source_target_pairs={{0,8},{8,0},{16,24},{24,16},{1,9},{9,1},{17,25},{25,17},{2,10},{10... | collective-permute-start | bytes 393224 | tf_op jit(solution)/shard_map/ppermute | solution.py:329
  21.8 0.8 %copy-start = (bf16[4,2,2048]{2,1,0:T(2,128)(2,1)S(1)}, bf16[4,2,2048]{2,1,0:T(2,128)(2,1)}, u32[]{:S(2)}) copy-start(bf16[4,2,2048]{2,1,0:T(2,128)(2,1)} %shard_map.126._) | copy-start | bytes 98308

commit v3 on v2

v3 whole, which is shorter than its diff:
```python
import functools
import math

import jax
import jax.numpy as jnp
from jax import lax
from jax.experimental import pallas as pl
from jax.experimental.pallas import tpu as pltpu
from jax.sharding import PartitionSpec as P

D_HEAD = 128
MASKED_SCORE = -1e30
EXP2_SCALE = D_HEAD**-0.5 * math.log2(math.e)
VMEM_BYTES = 40 * 2**20
NT = (((1,), (1,)), ((), ()))


def scores_of(queries, keys):
    return lax.dot_general(queries, keys, NT, preferred_element_type=jnp.float32)


def weighted(weights, values):
    return jnp.dot(weights.astype(jnp.bfloat16), values, preferred_element_type=jnp.float32)


def eye_of(rows):
    shape = (rows, 128)
    return lax.broadcasted_iota(jnp.int32, shape, 0) == lax.broadcasted_iota(jnp.int32, shape, 1)


def column_to_row(column):
    spread = jnp.where(eye_of(column.shape[0]), column, 0.0)
    return jnp.sum(spread, axis=0, keepdims=True)


def row_to_column(row, rows):
    spread = jnp.where(eye_of(rows), jnp.broadcast_to(row, (rows, 128)), 0.0)
    return jnp.sum(spread, axis=1, keepdims=True)


def select_rows(index, parts):
    chosen = parts[-1]
    for number in range(len(parts) - 2, -1, -1):
        chosen = jnp.where(index == number, parts[number], chosen)
    return chosen


def lane_sum(x):
    tiles = [x[:, i : i + 128] for i in range(0, x.shape[1], 128)]
    return jnp.sum(functools.reduce(jnp.add, tiles), axis=1, keepdims=True)


def lane_max(x):
    tiles = [x[:, i : i + 128] for i in range(0, x.shape[1], 128)]
    return jnp.max(functools.reduce(jnp.maximum, tiles), axis=1, keepdims=True)


def own_kernel(
    dq_hbm, asg_hbm, plen_hbm, clen_hbm, nk_hbm, nv_hbm, ck_hbm, cv_hbm,
    own_ref, other_ref, info_ref, sum_ref, top_ref, tot_ref,
    dq, nk, nv, asg, plen, clen, flat, fk, fv, ck_ref, cv_ref, sems,
):
    moves = [(dq_hbm, dq), (nk_hbm, nk), (nv_hbm, nv), (asg_hbm, asg), (plen_hbm, plen), (clen_hbm, clen)]
    role = lax.axis_index("role")
    for kv in (role, 1 - role):
        cols = pl.ds(pl.multiple_of(kv * D_HEAD, D_HEAD), D_HEAD)
        moves += [(ck_hbm.at[:, :, cols], ck_ref.at[:, :, cols]), (cv_hbm.at[:, :, cols], cv_ref.at[:, :, cols])]
    copies = [pltpu.make_async_copy(a, b, sems.at[i]) for i, (a, b) in enumerate(moves)]
    for copy in copies:
        copy.start()
    steps, rows, columns = dq.shape
    span = steps * rows
    half = columns // 2
    group = half // D_HEAD
    queries = group * span
    slots = ck_ref.shape[1]
    fk[...] = jnp.zeros_like(fk)
    fv[...] = jnp.zeros_like(fv)
    for copy in copies[:6]:
        copy.wait()
    for step in range(steps):
        at = slice(step * rows, (step + 1) * rows)
        flat[at, :] = dq[step].astype(jnp.float32)
        fk[at, :] = nk[step].astype(jnp.float32)
        fv[at, :] = nv[step].astype(jnp.float32)
    row_index = lax.broadcasted_iota(jnp.int32, (span, 128), 0)
    prompt = jnp.zeros((span, 128), jnp.float32)
    for row in range(rows):
        prompt = jnp.where(row_index % rows == row, asg[row].astype(jnp.float32), prompt)
    info = jnp.zeros((span, 128), jnp.int32)
    for row in range(plen.shape[0]):
        info = jnp.where(row_index == row, plen[row], info)
    info_ref[...] = info

    q_index = lax.broadcasted_iota(jnp.int32, (queries, 1), 0) % span
    q_step, q_row = q_index // rows, q_index % rows
    lane = lax.broadcasted_iota(jnp.int32, (queries, 128), 1)
    fresh_mask = (lane < span) & (lane % rows == q_row) & (lane // rows <= q_step)
    limit = select_rows(q_row, [clen[r] for r in range(rows)])
    live = lax.broadcasted_iota(jnp.int32, (queries, slots), 1) < limit
    for index, (out, kv) in enumerate(((own_ref, role), (other_ref, 1 - role))):
        heads = [flat[:, pl.ds(pl.multiple_of(kv * half + i * D_HEAD, D_HEAD), D_HEAD)] for i in range(group)]
        q = jnp.concatenate(heads, axis=0).astype(jnp.bfloat16)
        out[:queries, :] = q
        out[queries : queries + 2 * span, :] = jnp.concatenate([prompt, prompt], axis=0).astype(jnp.bfloat16)
        cols = pl.ds(pl.multiple_of(kv * D_HEAD, D_HEAD), D_HEAD)
        fresh = scores_of(q, fk[:, cols].astype(jnp.bfloat16))
        fresh = jnp.where(fresh_mask, fresh * EXP2_SCALE, MASKED_SCORE)
        copies[6 + 2 * index].wait()
        old = select_rows(q_row, [scores_of(q, ck_ref[r, :, cols]) for r in range(rows)])
        old = jnp.where(live, old * EXP2_SCALE, MASKED_SCORE)
        top = jnp.maximum(lane_max(fresh), lane_max(old))
        fresh = jnp.exp2(fresh - top)
        old = jnp.exp2(old - top)
        total = lane_sum(fresh) + lane_sum(old)
        summed = weighted(fresh, fv[:, cols].astype(jnp.bfloat16))
        copies[7 + 2 * index].wait()
        for r in range(rows):
            summed = summed + weighted(jnp.where(q_row == r, old, 0.0), cv_ref[r, :, cols])
        sum_ref[index] = summed
        top_ref[index] = jnp.broadcast_to(top, (queries, 128))
        tot_ref[index] = jnp.broadcast_to(total, (queries, 128))


def prompt_kernel(span, *refs):
    messages, info_ref = refs[:2], refs[2]
    chunk_refs, outs = refs[3:-3], refs[-2:]
    queries = messages[0].shape[0] - 2 * span
    seqs, seq = lax.axis_size("seq"), lax.axis_index("seq")
    prompts, length, _ = chunk_refs[0].shape
    q = jnp.concatenate([m[:queries, :] for m in messages], axis=0)
    columns = []
    for m in messages:
        eight = m[queries : queries + 2 * span, :].astype(jnp.float32)[:span, :1]
        columns += [eight] * (queries // span)
    prompt = jnp.concatenate(columns, axis=0).astype(jnp.int32)
    limit = select_rows(prompt, [jnp.broadcast_to(info_ref[r : r + 1, :1], prompt.shape) for r in range(prompts)])
    parts = []
    for index in range(seqs):
        base = (seq + seqs - 2 * (index // 2)) % seqs
        chunk = base + (index % 2) * (1 - 2 * (seq % 2))
        keys = chunk_refs[2 * index]
        position = chunk * length + lax.broadcasted_iota(jnp.int32, (q.shape[0], length), 1)
        part = select_rows(prompt, [scores_of(q, keys[r]) for r in range(prompts)])
        parts.append(jnp.where(position < limit, part * EXP2_SCALE, MASKED_SCORE))
    top = lane_max(jnp.concatenate(parts, axis=1))
    summed = jnp.zeros((q.shape[0], D_HEAD), jnp.float32)
    total = jnp.zeros((q.shape[0], 1), jnp.float32)
    for index, part in enumerate(parts):
        weights = jnp.exp2(part - top)
        total = total + lane_sum(weights)
        for r in range(prompts):
            summed = summed + weighted(jnp.where(prompt == r, weights, 0.0), chunk_refs[2 * index + 1][r])
    for index, out in enumerate(outs):
        rows = slice(index * queries, (index + 1) * queries)
        out[:queries, :] = summed[rows]
        out[queries : queries + 8, :] = jnp.concatenate(
            [column_to_row(top[rows]), column_to_row(total[rows]), jnp.zeros((6, 128), jnp.float32)], axis=0
        )


def local_kernel(row, q_ref, k_own, v_own, k_near, v_near, _, sum_ref, top_ref, tot_ref, wide):
    _, length, columns = q_ref.shape
    group = columns // D_HEAD
    seq = lax.axis_index("seq")
    wide[:length, :D_HEAD] = v_own[row]
    wide[length:, :D_HEAD] = v_near[row]
    wide[:, D_HEAD:] = jnp.ones((2 * length, D_HEAD), jnp.bfloat16)
    causal = lax.broadcasted_iota(jnp.int32, (length, length), 1) <= lax.broadcasted_iota(
        jnp.int32, (length, length), 0
    )

    def run(with_near):
        for head in range(group):
            cols = slice(head * D_HEAD, (head + 1) * D_HEAD)
            q = q_ref[row, :, cols]
            scores = jnp.where(causal, scores_of(q, k_own[row]), MASKED_SCORE)
            if with_near:
                scores = jnp.concatenate([scores, scores_of(q, k_near[row])], axis=1)
            top = jnp.max(scores, axis=1, keepdims=True) * EXP2_SCALE
            summed = weighted(jnp.exp2(scores * EXP2_SCALE - top), wide[: scores.shape[1], :])
            sum_ref[:, cols] = summed[:, :D_HEAD]
            tot_ref[:, cols] = summed[:, D_HEAD:]
            top_ref[:, cols] = jnp.broadcast_to(top, (length, D_HEAD))

    @pl.when(seq % 2 == 0)
    def _():
        run(False)

    @pl.when(seq % 2 == 1)
    def _():
        run(True)


def merge_rows(span, cache, own_part, other_part, dec, flat):
    steps, rows, columns = dec.shape
    half = columns // 2
    group = half // D_HEAD
    queries = group * span
    role = lax.axis_index("role")
    for index, (part, kv) in enumerate(((own_part, role), (other_part, 1 - role))):
        top = row_to_column(part[queries : queries + 1, :], queries)
        total = row_to_column(part[queries + 1 : queries + 2, :], queries)
        cache_sum, cache_top, cache_tot = (ref[index] for ref in cache)
        high = jnp.maximum(top, cache_top)
        one, two = jnp.exp2(cache_top - high), jnp.exp2(top - high)
        result = (one * cache_sum + two * part[:queries, :]) / (one * cache_tot + two * total)
        for head in range(group):
            start = pl.multiple_of(kv * half + head * D_HEAD, D_HEAD)
            flat[:, pl.ds(start, D_HEAD)] = result[head * span : (head + 1) * span]
    for step in range(steps):
        dec[step] = flat[step * rows : (step + 1) * rows, :].astype(jnp.bfloat16)


def far_kernel(shift, row, last, final, span, info_ref, q_ref, k_one, v_one, k_two, v_two, sum_in, top_in, tot_in, *refs):
    _, length, columns = q_ref.shape
    group = columns // D_HEAD
    seq = lax.axis_index("seq")
    if final:
        _, *cache, own_part, other_part, out_hbm, dec_hbm, wide, out, sems, dec, flat = refs
        merge_rows(span, cache, own_part, other_part, dec, flat)
        dec_copy = pltpu.make_async_copy(dec, dec_hbm, sems.at[group])
        dec_copy.start()
    elif last:
        out_hbm, wide, out, sems = refs[-4:]
    else:
        sum_ref, top_ref, tot_ref, wide = refs[-4:]

    def move(head):
        cols = slice(head * D_HEAD, (head + 1) * D_HEAD)
        return pltpu.make_async_copy(out.at[:, cols], out_hbm.at[row, :, cols], sems.at[head])

    def run(with_far):
        position = seq * length + lax.broadcasted_iota(jnp.int32, (length, D_HEAD), 0)
        live = position < info_ref[row : row + 1, :]
        for head in range(group):
            cols = slice(head * D_HEAD, (head + 1) * D_HEAD)
            summed, total, top = sum_in[:, cols], tot_in[:, cols], top_in[:, cols]
            if with_far:
                q = q_ref[row, :, cols]
                scores = jnp.concatenate([scores_of(q, k_one[row]), scores_of(q, k_two[row])], axis=1)
                new = jnp.maximum(top, jnp.max(scores, axis=1, keepdims=True) * EXP2_SCALE)
                high = jnp.concatenate([new] * (2 * length // D_HEAD), axis=1)
                far = weighted(jnp.exp2(scores * EXP2_SCALE - high), wide[...])
                alpha = jnp.exp2(top - new)
                summed = summed * alpha + far[:, :D_HEAD]
                total = total * alpha + far[:, D_HEAD:]
                top = new
            if last:
                out[:, cols] = jnp.where(live, summed / total, 0.0).astype(jnp.bfloat16)
                move(head).start()
            else:
                sum_ref[:, cols], top_ref[:, cols], tot_ref[:, cols] = summed, top, total

    @pl.when(seq // 2 >= shift)
    def _():
        wide[:length, :D_HEAD] = v_one[row]
        wide[length:, :D_HEAD] = v_two[row]
        wide[:, D_HEAD:] = jnp.ones((2 * length, D_HEAD), jnp.bfloat16)
        run(True)

    @pl.when(seq // 2 < shift)
    def _():
        run(False)

    if last:
        for head in range(group):
            move(head).wait()
    if final:
        dec_copy.wait()


VMEM = pl.BlockSpec(memory_space=pltpu.VMEM)
ANY = pl.BlockSpec(memory_space=pl.ANY)


def in_hbm(x):
    return pltpu.with_memory_space_constraint(x, pltpu.HBM)


def call(kernel, args, outs, scratch=(), specs=None, out_specs=None, aliases=None, us=1.0):
    return pl.pallas_call(
        kernel,
        out_shape=outs,
        in_specs=specs or [VMEM] * len(args),
        out_specs=out_specs or [VMEM] * len(outs),
        scratch_shapes=list(scratch),
        input_output_aliases=aliases or {},
        compiler_params=pltpu.CompilerParams(vmem_limit_bytes=VMEM_BYTES),
        cost_estimate=pl.CostEstimate(flops=int(us * 1.1e9), bytes_accessed=int(us * 3e6), transcendentals=0),
    )(*args)


def body(
    prefill_queries,
    prefill_keys,
    prefill_values,
    prompt_len,
    assignment,
    cache_len,
    cache_keys,
    cache_values,
    decode_queries,
    new_keys,
    new_values,
):
    seqs = lax.axis_size("seq")
    prompts, length, columns = prefill_queries.shape
    steps, rows, dec_columns = decode_queries.shape
    group = columns // D_HEAD
    span = steps * rows
    queries = group * span
    f32, bf16, i32 = jnp.float32, jnp.bfloat16, jnp.int32
    shape = jax.ShapeDtypeStruct
    after = lax.optimization_barrier

    def near(x):
        return lax.ppermute(x, "seq", [(i, i ^ 1) for i in range(seqs)])

    def around(x, shift):
        return lax.ppermute(x, "seq", [(i, (i + 2 * shift) % seqs) for i in range(seqs)])

    def partner(x):
        return lax.ppermute(x, "role", [(0, 1), (1, 0)])

    shifts = range(1, seqs // 2)
    far_keys = [around(prefill_keys, s) for s in shifts]
    far_values = [around(prefill_values, s) for s in shifts]
    near_keys, near_values = near(prefill_keys), near(prefill_values)
    message = shape((queries + 2 * span, 128), bf16)
    state = shape((2, queries, 128), f32)
    small = [decode_queries, assignment, prompt_len, cache_len, new_keys, new_values]
    own_msg, other_msg, info, *cache = call(
        own_kernel,
        [in_hbm(x) for x in small + [cache_keys, cache_values]],
        [message] * 2 + [shape((span, 128), i32)] + [state] * 3,
        [
            pltpu.VMEM(decode_queries.shape, bf16),
            pltpu.VMEM(new_keys.shape, bf16),
            pltpu.VMEM(new_values.shape, bf16),
            pltpu.SMEM(assignment.shape, i32),
            pltpu.SMEM(prompt_len.shape, i32),
            pltpu.SMEM(cache_len.shape, i32),
            pltpu.VMEM((span, dec_columns), f32),
            pltpu.VMEM((128, 2 * D_HEAD), f32),
            pltpu.VMEM((128, 2 * D_HEAD), f32),
            pltpu.VMEM(cache_keys.shape, bf16),
            pltpu.VMEM(cache_values.shape, bf16),
            pltpu.SemaphoreType.DMA((len(small) + 4,)),
        ],
        specs=[ANY] * (len(small) + 2),
        us=1.7,
    )
    partner_msg = partner(other_msg)
    far_keys, info = after((far_keys, info))
    far_near_keys = [near(k) for k in far_keys]
    run = shape((length, columns), f32)
    states = []
    marker = info
    for row in range(prompts):
        states.append(
            call(
                functools.partial(local_kernel, row),
                (prefill_queries, prefill_keys, prefill_values, near_keys, near_values, marker),
                [run] * 3,
                [pltpu.VMEM((2 * length, 2 * D_HEAD), bf16)],
                specs=[VMEM] * 5 + [ANY],
                us=1.3,
            )
        )
        marker = states[-1][0]
        if row == 0:
            far_values, marker = after((far_values, marker))
    far_near_values = [near(v) for v in far_values]
    chunks = [prefill_keys, prefill_values, near_keys, near_values]
    for quad in zip(far_keys, far_values, far_near_keys, far_near_values):
        chunks += quad
    part = shape((queries + 8, 128), f32)
    own_part, partner_part = call(
        functools.partial(prompt_kernel, span),
        (own_msg, partner_msg, info, *chunks, marker),
        [part] * 2,
        specs=[VMEM] * (3 + len(chunks)) + [ANY],
        us=0.9,
    )
    other_part = partner(partner_part)
    marker = own_part
    wide = pltpu.VMEM((2 * length, 2 * D_HEAD), bf16)
    out = None
    for index, shift in enumerate(shifts):
        last = index == len(shifts) - 1
        far = chunks[4 * (index + 1) : 4 * (index + 2)]
        for row in range(prompts):
            final = last and row == prompts - 1
            args = [info, prefill_queries, *far, *states[row], marker if out is None else out]
            specs = [VMEM] * (len(args) - 1) + [ANY]
            outs, out_specs, scratch, aliases = [run] * 3, [VMEM] * 3, [wide], {}
            if last:
                outs, out_specs = [shape(prefill_queries.shape, bf16)], [ANY]
                scratch += [pltpu.VMEM((length, columns), bf16), pltpu.SemaphoreType.DMA((group + 1,))]
                aliases = {} if out is None else {len(args) - 1: 0}
            if final:
                args += [*cache, own_part, other_part]
                specs += [VMEM] * 5
                outs.append(shape(decode_queries.shape, bf16))
                out_specs.append(ANY)
                scratch += [pltpu.VMEM(decode_queries.shape, bf16), pltpu.VMEM((span, dec_columns), f32)]
            result = call(
                functools.partial(far_kernel, shift, row, last, final, span),
                args, outs, scratch, specs=specs, out_specs=out_specs, aliases=aliases, us=1.7,
            )
            if last:
                out = result[0]
            else:
                states[row] = result
                marker = result[0]
    return (out, result[1])


def solution(mesh):
    in_specs = (
        P(None, "seq", ("head", "role")),
        P(None, "seq", ("head", "role")),
        P(None, "seq", ("head", "role")),
        P(),
        P(("seq", "role")),
        P(("seq", "role")),
        P(("seq", "role"), None, "head"),
        P(("seq", "role"), None, "head"),
        P(None, ("seq", "role"), "head"),
        P(None, ("seq", "role"), "head"),
        P(None, ("seq", "role"), "head"),
    )
    out_specs = (P(None, "seq", ("head", "role")), P(None, ("seq", "role"), "head"))
    return jax.shard_map(body, mesh=mesh, in_specs=in_specs, out_specs=out_specs, check_vma=False)
```

time: 27.1 us -> 19.3 us (0.71)
  the two profiles are of different devices: /device:TPU:28 before, /device:TPU:29 now
where the time goes in v3:
time: 19.3 us; the launch traced here: 19.1 us
  Pallas kernels  11.8 us (61%)
  starting transfers between devices  6.59 us (34%)
  between operations  0.76 us (4%)
    pallas_call x6, Pallas kernels, call(): pl.pallas_call(kernel, out_shape=outs, in_specs=specs or [VMEM] * len(arg...  11.8 us
    ppermute x2, starting transfers between devices, partner(): return lax.ppermute(x, 'role', [(0, 1), (1, 0)])  2.56 us
    ppermute x4, starting transfers between devices, near(): return lax.ppermute(x, 'seq', [(i, i ^ 1) for i in range(seqs)])  2.55 us
    ppermute x2, starting transfers between devices, around(): lax.ppermute(x, 'seq', [(i, (i + 2 * shift) % seqs) for i in range(seqs)])  1.48 us
  transfers between devices with their start and end apart: 8, of which 0 were waited for; matrix products, arithmetic and copies ran while one was open for 0% of the time, Pallas kernels for 44%

profile of v3, /device:TPU:29, one launch (start us, length us, event | category | flops | bytes accessed | tf_op | source)
XLA Modules:
  0.0 19.1 jit_solution(6813782979252227230)
XLA Ops:
  0.6 0.0 copy-start.1
  0.6 0.0 copy-start.2
  0.7 0.7 %collective-permute-start.2 = (bf16[2,256,128]{2,1,0:T(8,128)(2,1)}, bf16[2,256,128]{2,1,0:T(8,128)(2,1)S(1)}, u32[]{:S(2)}, u32[]{:S(2)}) collective-permute-start(bf16[2,256,128]{2,1,0:T(8,128)(2,1)} %refs_3_.1), channel_id=1, source_target_pairs={{0,8},{8,0},{16,24},{24,16},{1,9},{9,1},{17,25},{25,17},{2,10},{10... | collective-permute-start | bytes 393224 | tf_op jit(solution)/shard_map/ppermute | solution.py:318
  1.4 0.2 %collective-permute-start = (bf16[2,256,128]{2,1,0:T(8,128)(2,1)}, bf16[2,256,128]{2,1,0:T(8,128)(2,1)S(1)}, u32[]{:S(2)}, u32[]{:S(2)}) collective-permute-start(bf16[2,256,128]{2,1,0:T(8,128)(2,1)} %refs_3_.1), channel_id=1, source_target_pairs={{0,16},{8,24},{16,0},{24,8},{1,17},{9,25},{17,1},{25,9},{2,18},{10... | collective-permute-start | bytes 393224 | tf_op jit(solution)/shard_map/ppermute | solution.py:321
  1.6 0.3 %collective-permute-start.3 = (bf16[2,256,128]{2,1,0:T(8,128)(2,1)}, bf16[2,256,128]{2,1,0:T(8,128)(2,1)S(1)}, u32[]{:S(2)}, u32[]{:S(2)}) collective-permute-start(bf16[2,256,128]{2,1,0:T(8,128)(2,1)} %refs_4_.1), channel_id=1, source_target_pairs={{0,8},{8,0},{16,24},{24,16},{1,9},{9,1},{17,25},{25,17},{2,10},{10... | collective-permute-start | bytes 393224 | tf_op jit(solution)/shard_map/ppermute | solution.py:318
  2.0 1.2 %collective-permute-start.1 = (bf16[2,256,128]{2,1,0:T(8,128)(2,1)}, bf16[2,256,128]{2,1,0:T(8,128)(2,1)S(1)}, u32[]{:S(2)}, u32[]{:S(2)}) collective-permute-start(bf16[2,256,128]{2,1,0:T(8,128)(2,1)} %refs_4_.1), channel_id=1, source_target_pairs={{0,16},{8,24},{16,0},{24,8},{1,17},{9,25},{17,1},{25,9},{2,18},{10... | collective-permute-start | bytes 393224 | tf_op jit(solution)/shard_map/ppermute | solution.py:321
  3.2 2.7 %shard_map.122 = (bf16[80,128]{1,0:T(8,128)(2,1)S(1)}, bf16[80,128]{1,0:T(8,128)(2,1)S(1)}, s32[8,128]{1,0:T(8,128)S(1)}, f32[2,64,128]{2,1,0:T(8,128)S(1)}, f32...) custom-call(bf16[4,2,2048]{2,1,0:T(2,128)(2,1)} %dq_hbm.1, s32[2]{0:T(128)} %asg_hbm.1, s32[2]{0:T(128)} %plen_hbm.1, ...), custom_call_target="tpu_custom_call" | custom-call | flops 1870000000 | bytes 5100000 | tf_op jit(solution)/shard_map/pallas_call | solution.py:282
  5.9 1.3 %collective-permute-start.6 = (bf16[80,128]{1,0:T(8,128)(2,1)S(1)}, bf16[80,128]{1,0:T(8,128)(2,1)S(1)}, u32[]{:S(2)}, u32[]{:S(2)}) collective-permute-start(bf16[80,128]{1,0:T(8,128)(2,1)S(1)} %get-tuple-element.32), channel_id=1, source_target_pairs={{0,1},{1,0},{2,3},{3,2},{4,5},{5,4},{6,7},{7,6},{8,9},{9,8},{10,11... | collective-permute-start | bytes 61448 | tf_op jit(solution)/shard_map/ppermute | solution.py:324
  7.2 0.0 collective-permute-done.refs_7_.k_one
  7.2 0.8 %collective-permute-start.4 = (bf16[2,256,128]{2,1,0:T(8,128)(2,1)S(1)}, bf16[2,256,128]{2,1,0:T(8,128)(2,1)S(1)}, u32[]{:S(2)}, u32[]{:S(2)}) collective-permute-start(bf16[2,256,128]{2,1,0:T(8,128)(2,1)S(1)} %collective-permute-done.refs_7_.k_one), channel_id=1, source_target_pairs={{0,8},{8,0},{16,24},{24,16},{1,9},{9,1},{17,25},{25,17},{2,10},{10... | collective-permute-start | bytes 393224 | tf_op jit(solution)/shard_map/ppermute | solution.py:318
  8.0 0.0 collective-permute-done.2.k_near.refs_5_
  8.0 0.0 collective-permute-done.3.v_near.refs_6_
  8.0 1.6 %shard_map.123 = (f32[256,1024]{1,0:T(8,128)S(1)}, f32[256,1024]{1,0:T(8,128)S(1)}, f32[256,1024]{1,0:T(8,128)S(1)}) custom-call(bf16[2,256,1024]{2,1,0:T(8,128)(2,1)S(1)} %copy-done, bf16[2,256,128]{2,1,0:T(8,128)(2,1)S(1)} %copy-done.1, bf16[2,256,128]{2,1,0:T(8,128)(2,1)S(1)} %copy-done.2, bf16[2,256,128]{2,1,0:T(8,128)(2,1)S(1)} %collective-permute-done.2.k_near.refs_5_, ...), custom_call_target="tpu_custom_call" | custom-call | flops 1430000000 | bytes 3900000 | tf_op jit(solution)/shard_map/pallas_call | solution.py:282
  9.7 0.0 collective-permute-done.1.refs_8_.v_one
  9.7 0.7 %collective-permute-start.5 = (bf16[2,256,128]{2,1,0:T(8,128)(2,1)S(1)}, bf16[2,256,128]{2,1,0:T(8,128)(2,1)S(1)}, u32[]{:S(2)}, u32[]{:S(2)}) collective-permute-start(bf16[2,256,128]{2,1,0:T(8,128)(2,1)S(1)} %collective-permute-done.1.refs_8_.v_one), channel_id=1, source_target_pairs={{0,8},{8,0},{16,24},{24,16},{1,9},{9,1},{17,25},{25,17},{2,10},{10... | collective-permute-start | bytes 393224 | tf_op jit(solution)/shard_map/ppermute | solution.py:318
  10.4 1.6 %shard_map.124 = (f32[256,1024]{1,0:T(8,128)S(1)}, f32[256,1024]{1,0:T(8,128)S(1)}, f32[256,1024]{1,0:T(8,128)S(1)}) custom-call(bf16[2,256,1024]{2,1,0:T(8,128)(2,1)S(1)} %copy-done, bf16[2,256,128]{2,1,0:T(8,128)(2,1)S(1)} %copy-done.1, bf16[2,256,128]{2,1,0:T(8,128)(2,1)S(1)} %copy-done.2, bf16[2,256,128]{2,1,0:T(8,128)(2,1)S(1)} %collective-permute-done.2.k_near.refs_5_, ...), custom_call_target="tpu_custom_call" | custom-call | flops 1430000000 | bytes 3900000 | tf_op jit(solution)/shard_map/pallas_call | solution.py:282
  12.0 0.0 collective-permute-done.6.refs_1_
  12.0 0.0 collective-permute-done.4.refs_9_.k_two
  12.0 0.0 collective-permute-done.5.refs_10_.v_two
  12.0 0.7 %shard_map.125 = (f32[72,128]{1,0:T(8,128)S(1)}, f32[72,128]{1,0:T(8,128)S(1)}) custom-call(bf16[80,128]{1,0:T(8,128)(2,1)S(1)} %get-tuple-element.31.refs_0_, bf16[80,128]{1,0:T(8,128)(2,1)S(1)} %collective-permute-done.6.refs_1_, s32[8,128]{1,0:T(8,128)S(1)} %get-tuple-element.21._.refs_2_.info_ref, bf16[2,256,128]{2,1,0:T(8,128)(2,1)S(1)} %copy-done.1, ...), custom_call_target="tpu_custom_call" | custom-call | flops 990000000 | bytes 2700000 | tf_op jit(solution)/shard_map/pallas_call | solution.py:282
  12.7 1.3 %collective-permute-start.7 = (f32[72,128]{1,0:T(8,128)S(1)}, f32[72,128]{1,0:T(8,128)S(1)}, u32[]{:S(2)}, u32[]{:S(2)}) collective-permute-start(f32[72,128]{1,0:T(8,128)S(1)} %get-tuple-element.37), channel_id=1, source_target_pairs={{0,1},{1,0},{2,3},{3,2},{4,5},{5,4},{6,7},{7,6},{8,9},{9,8},{10,11... | collective-permute-start | bytes 110600 | tf_op jit(solution)/shard_map/ppermute | solution.py:324
  14.0 2.5 %shard_map.126.refs_0_ = bf16[2,256,1024]{2,1,0:T(8,128)(2,1)} custom-call(s32[8,128]{1,0:T(8,128)S(1)} %get-tuple-element.21._.refs_2_.info_ref, bf16[2,256,1024]{2,1,0:T(8,128)(2,1)S(1)} %copy-done, bf16[2,256,128]{2,1,0:T(8,128)(2,1)S(1)} %collective-permute-done.refs_7_.k_one, bf16[2,256,128]{2,1,0:T(8,128)(2,1)S(1)} %collective-permute-done.1.refs_8_.v_one, ...), custom_call_target="tpu_custom_call" | custom-call | flops 1870000000 | bytes 5100000 | tf_op jit(solution)/shard_map/pallas_call | solution.py:282
  16.5 0.0 collective-permute-done.7.refs_5_
  16.5 2.6 %shard_map.127 = (bf16[2,256,1024]{2,1,0:T(8,128)(2,1)}, bf16[4,2,2048]{2,1,0:T(2,128)(2,1)}) custom-call(s32[8,128]{1,0:T(8,128)S(1)} %get-tuple-element.21._.refs_2_.info_ref, bf16[2,256,1024]{2,1,0:T(8,128)(2,1)S(1)} %copy-done, bf16[2,256,128]{2,1,0:T(8,128)(2,1)S(1)} %collective-permute-done.refs_7_.k_one, ...), custom_call_target="tpu_custom_call", output_to_operand_aliasing={{0}: (9, {})} | custom-call | flops 1870000000 | bytes 5100000 | tf_op jit(solution)/shard_map/pallas_call | solution.py:282
  (4 shorter events, 0.0 us)
Async XLA Ops:
  0.6 7.4 %copy-start.1 = (bf16[2,256,128]{2,1,0:T(8,128)(2,1)S(1)}, bf16[2,256,128]{2,1,0:T(8,128)(2,1)}, u32[]{:S(2)}) copy-start(bf16[2,256,128]{2,1,0:T(8,128)(2,1)} %refs_3_.1) | copy-start | bytes 393220
  0.6 7.4 %copy-start.2 = (bf16[2,256,128]{2,1,0:T(8,128)(2,1)S(1)}, bf16[2,256,128]{2,1,0:T(8,128)(2,1)}, u32[]{:S(2)}) copy-start(bf16[2,256,128]{2,1,0:T(8,128)(2,1)} %refs_4_.1) | copy-start | bytes 393220
  0.7 7.4 %copy-start = (bf16[2,256,1024]{2,1,0:T(8,128)(2,1)S(1)}, bf16[2,256,1024]{2,1,0:T(8,128)(2,1)}, u32[]{:S(2)}) copy-start(bf16[2,256,1024]{2,1,0:T(8,128)(2,1)} %q_ref.7) | copy-start | bytes 3145732
  0.7 7.3 %collective-permute-start.2 = (bf16[2,256,128]{2,1,0:T(8,128)(2,1)}, bf16[2,256,128]{2,1,0:T(8,128)(2,1)S(1)}, u32[]{:S(2)}, u32[]{:S(2)}) collective-permute-start(bf16[2,256,128]{2,1,0:T(8,128)(2,1)} %refs_3_.1), channel_id=1, source_target_pairs={{0,8},{8,0},{16,24},{24,16},{1,9},{9,1},{17,25},{25,17},{2,10},{10... | collective-permute-start | bytes 393224 | tf_op jit(solution)/shard_map/ppermute | solution.py:318
  1.4 5.8 %collective-permute-start = (bf16[2,256,128]{2,1,0:T(8,128)(2,1)}, bf16[2,256,128]{2,1,0:T(8,128)(2,1)S(1)}, u32[]{:S(2)}, u32[]{:S(2)}) collective-permute-start(bf16[2,256,128]{2,1,0:T(8,128)(2,1)} %refs_3_.1), channel_id=1, source_target_pairs={{0,16},{8,24},{16,0},{24,8},{1,17},{9,25},{17,1},{25,9},{2,18},{10... | collective-permute-start | bytes 393224 | tf_op jit(solution)/shard_map/ppermute | solution.py:321
  1.6 6.4 %collective-permute-start.3 = (bf16[2,256,128]{2,1,0:T(8,128)(2,1)}, bf16[2,256,128]{2,1,0:T(8,128)(2,1)S(1)}, u32[]{:S(2)}, u32[]{:S(2)}) collective-permute-start(bf16[2,256,128]{2,1,0:T(8,128)(2,1)} %refs_4_.1), channel_id=1, source_target_pairs={{0,8},{8,0},{16,24},{24,16},{1,9},{9,1},{17,25},{25,17},{2,10},{10... | collective-permute-start | bytes 393224 | tf_op jit(solution)/shard_map/ppermute | solution.py:318
  2.0 7.7 %collective-permute-start.1 = (bf16[2,256,128]{2,1,0:T(8,128)(2,1)}, bf16[2,256,128]{2,1,0:T(8,128)(2,1)S(1)}, u32[]{:S(2)}, u32[]{:S(2)}) collective-permute-start(bf16[2,256,128]{2,1,0:T(8,128)(2,1)} %refs_4_.1), channel_id=1, source_target_pairs={{0,16},{8,24},{16,0},{24,8},{1,17},{9,25},{17,1},{25,9},{2,18},{10... | collective-permute-start | bytes 393224 | tf_op jit(solution)/shard_map/ppermute | solution.py:321
  5.9 6.0 %collective-permute-start.6 = (bf16[80,128]{1,0:T(8,128)(2,1)S(1)}, bf16[80,128]{1,0:T(8,128)(2,1)S(1)}, u32[]{:S(2)}, u32[]{:S(2)}) collective-permute-start(bf16[80,128]{1,0:T(8,128)(2,1)S(1)} %get-tuple-element.32), channel_id=1, source_target_pairs={{0,1},{1,0},{2,3},{3,2},{4,5},{5,4},{6,7},{7,6},{8,9},{9,8},{10,11... | collective-permute-start | bytes 61448 | tf_op jit(solution)/shard_map/ppermute | solution.py:324
  7.2 4.8 %collective-permute-start.4 = (bf16[2,256,128]{2,1,0:T(8,128)(2,1)S(1)}, bf16[2,256,128]{2,1,0:T(8,128)(2,1)S(1)}, u32[]{:S(2)}, u32[]{:S(2)}) collective-permute-start(bf16[2,256,128]{2,1,0:T(8,128)(2,1)S(1)} %collective-permute-done.refs_7_.k_one), channel_id=1, source_target_pairs={{0,8},{8,0},{16,24},{24,16},{1,9},{9,1},{17,25},{25,17},{2,10},{10... | collective-permute-start | bytes 393224 | tf_op jit(solution)/shard_map/ppermute | solution.py:318
  9.7 2.3 %collective-permute-start.5 = (bf16[2,256,128]{2,1,0:T(8,128)(2,1)S(1)}, bf16[2,256,128]{2,1,0:T(8,128)(2,1)S(1)}, u32[]{:S(2)}, u32[]{:S(2)}) collective-permute-start(bf16[2,256,128]{2,1,0:T(8,128)(2,1)S(1)} %collective-permute-done.1.refs_8_.v_one), channel_id=1, source_target_pairs={{0,8},{8,0},{16,24},{24,16},{1,9},{9,1},{17,25},{25,17},{2,10},{10... | collective-permute-start | bytes 393224 | tf_op jit(solution)/shard_map/ppermute | solution.py:318
  12.7 3.8 %collective-permute-start.7 = (f32[72,128]{1,0:T(8,128)S(1)}, f32[72,128]{1,0:T(8,128)S(1)}, u32[]{:S(2)}, u32[]{:S(2)}) collective-permute-start(f32[72,128]{1,0:T(8,128)S(1)} %get-tuple-element.37), channel_id=1, source_target_pairs={{0,1},{1,0},{2,3},{3,2},{4,5},{5,4},{6,7},{7,6},{8,9},{9,8},{10,11... | collective-permute-start | bytes 110600 | tf_op jit(solution)/shard_map/ppermute | solution.py:324

commit v4 on v3

v4 whole, which is shorter than its diff:
```python
import functools
import math

import jax
import jax.numpy as jnp
from jax import lax
from jax.experimental import pallas as pl
from jax.experimental.pallas import tpu as pltpu
from jax.sharding import PartitionSpec as P

D_HEAD = 128
MASKED_SCORE = -1e30
EXP2_SCALE = D_HEAD**-0.5 * math.log2(math.e)
VMEM_BYTES = 40 * 2**20
SUM_LIMIT = 2.0**100
NT = (((1,), (1,)), ((), ()))


def scores_of(queries, keys):
    return lax.dot_general(queries, keys, NT, preferred_element_type=jnp.float32)


def weighted(weights, values):
    return jnp.dot(weights.astype(jnp.bfloat16), values, preferred_element_type=jnp.float32)


def eye_of(rows):
    shape = (rows, 128)
    return lax.broadcasted_iota(jnp.int32, shape, 0) == lax.broadcasted_iota(jnp.int32, shape, 1)


def column_to_row(column):
    spread = jnp.where(eye_of(column.shape[0]), column, 0.0)
    return jnp.sum(spread, axis=0, keepdims=True)


def row_to_column(row, rows):
    spread = jnp.where(eye_of(rows), jnp.broadcast_to(row, (rows, 128)), 0.0)
    return jnp.sum(spread, axis=1, keepdims=True)


def select_rows(index, parts):
    chosen = parts[-1]
    for number in range(len(parts) - 2, -1, -1):
        chosen = jnp.where(index == number, parts[number], chosen)
    return chosen


def lane_sum(x):
    tiles = [x[:, i : i + 128] for i in range(0, x.shape[1], 128)]
    return jnp.sum(functools.reduce(jnp.add, tiles), axis=1, keepdims=True)


def lane_max(x):
    tiles = [x[:, i : i + 128] for i in range(0, x.shape[1], 128)]
    return jnp.max(functools.reduce(jnp.maximum, tiles), axis=1, keepdims=True)


def first_kernel(_, out_ref):
    out_ref[...] = jnp.zeros_like(out_ref)


def own_kernel(
    asg_hbm, plen_hbm, clen_hbm, dq, nk, nv, ck_ref, cv_ref, _,
    own_ref, other_ref, info_ref, sum_ref, top_ref, tot_ref, asg, plen, clen, flat, fk, fv, sems,
):
    moves = [(asg_hbm, asg), (plen_hbm, plen), (clen_hbm, clen)]
    copies = [pltpu.make_async_copy(a, b, sems.at[i]) for i, (a, b) in enumerate(moves)]
    for copy in copies:
        copy.start()
    role = lax.axis_index("role")
    steps, rows, columns = dq.shape
    span = steps * rows
    half = columns // 2
    group = half // D_HEAD
    queries = group * span
    slots = ck_ref.shape[1]
    fk[...] = jnp.zeros_like(fk)
    fv[...] = jnp.zeros_like(fv)
    for step in range(steps):
        at = slice(step * rows, (step + 1) * rows)
        flat[at, :] = dq[step].astype(jnp.float32)
        fk[at, :] = nk[step].astype(jnp.float32)
        fv[at, :] = nv[step].astype(jnp.float32)
    q_index = lax.broadcasted_iota(jnp.int32, (queries, 1), 0) % span
    q_step, q_row = q_index // rows, q_index % rows
    lane = lax.broadcasted_iota(jnp.int32, (queries, 128), 1)
    fresh_mask = (lane < span) & (lane % rows == q_row) & (lane // rows <= q_step)
    sides = ((own_ref, role), (other_ref, 1 - role))
    slices = [pl.ds(pl.multiple_of(kv * D_HEAD, D_HEAD), D_HEAD) for _, kv in sides]
    scores = []
    for (out, kv), cols in zip(sides, slices):
        heads = [flat[:, pl.ds(pl.multiple_of(kv * half + i * D_HEAD, D_HEAD), D_HEAD)] for i in range(group)]
        q = jnp.concatenate(heads, axis=0).astype(jnp.bfloat16)
        out[:queries, :] = q
        fresh = scores_of(q, fk[:, cols].astype(jnp.bfloat16))
        fresh = jnp.where(fresh_mask, fresh * EXP2_SCALE, MASKED_SCORE)
        scores.append((fresh, select_rows(q_row, [scores_of(q, ck_ref[r, :, cols]) for r in range(rows)])))
    for copy in copies:
        copy.wait()
    row_index = lax.broadcasted_iota(jnp.int32, (span, 128), 0)
    prompt = jnp.zeros((span, 128), jnp.float32)
    for row in range(rows):
        prompt = jnp.where(row_index % rows == row, asg[row].astype(jnp.float32), prompt)
    info = jnp.zeros((span, 128), jnp.int32)
    for row in range(plen.shape[0]):
        info = jnp.where(row_index == row, plen[row], info)
    info_ref[...] = info
    limit = select_rows(q_row, [clen[r] for r in range(rows)])
    live = lax.broadcasted_iota(jnp.int32, (queries, slots), 1) < limit
    for index, ((out, _), cols, (fresh, old)) in enumerate(zip(sides, slices, scores)):
        out[queries : queries + 2 * span, :] = jnp.concatenate([prompt, prompt], axis=0).astype(jnp.bfloat16)
        old = jnp.where(live, old * EXP2_SCALE, MASKED_SCORE)
        top = jnp.maximum(lane_max(fresh), lane_max(old))
        fresh = jnp.exp2(fresh - top)
        old = jnp.exp2(old - top)
        total = lane_sum(fresh) + lane_sum(old)
        summed = weighted(fresh, fv[:, cols].astype(jnp.bfloat16))
        for r in range(rows):
            summed = summed + weighted(jnp.where(q_row == r, old, 0.0), cv_ref[r, :, cols])
        sum_ref[index] = summed
        top_ref[index] = jnp.broadcast_to(top, (queries, 128))
        tot_ref[index] = jnp.broadcast_to(total, (queries, 128))


def prompt_kernel(span, *refs):
    messages, info_ref = refs[:2], refs[2]
    chunk_refs, outs = refs[3:-3], refs[-2:]
    queries = messages[0].shape[0] - 2 * span
    seqs, seq = lax.axis_size("seq"), lax.axis_index("seq")
    prompts, length, _ = chunk_refs[0].shape
    q = jnp.concatenate([m[:queries, :] for m in messages], axis=0)
    columns = []
    for m in messages:
        eight = m[queries : queries + 2 * span, :].astype(jnp.float32)[:span, :1]
        columns += [eight] * (queries // span)
    prompt = jnp.concatenate(columns, axis=0).astype(jnp.int32)
    limit = select_rows(prompt, [jnp.broadcast_to(info_ref[r : r + 1, :1], prompt.shape) for r in range(prompts)])
    parts = []
    for index in range(seqs):
        base = (seq + seqs - 2 * (index // 2)) % seqs
        chunk = base + (index % 2) * (1 - 2 * (seq % 2))
        keys = chunk_refs[2 * index]
        position = chunk * length + lax.broadcasted_iota(jnp.int32, (q.shape[0], length), 1)
        part = select_rows(prompt, [scores_of(q, keys[r]) for r in range(prompts)])
        parts.append(jnp.where(position < limit, part * EXP2_SCALE, MASKED_SCORE))
    top = lane_max(jnp.concatenate(parts, axis=1))
    summed = jnp.zeros((q.shape[0], D_HEAD), jnp.float32)
    total = jnp.zeros((q.shape[0], 1), jnp.float32)
    for index, part in enumerate(parts):
        weights = jnp.exp2(part - top)
        total = total + lane_sum(weights)
        for r in range(prompts):
            summed = summed + weighted(jnp.where(prompt == r, weights, 0.0), chunk_refs[2 * index + 1][r])
    for index, out in enumerate(outs):
        rows = slice(index * queries, (index + 1) * queries)
        out[:queries, :] = summed[rows]
        out[queries : queries + 8, :] = jnp.concatenate(
            [column_to_row(top[rows]), column_to_row(total[rows]), jnp.zeros((6, 128), jnp.float32)], axis=0
        )


def local_kernel(q_ref, k_own, v_own, k_near, v_near, _, *refs):
    outs, wide = refs[:-1], refs[-1]
    prompts, length, columns = q_ref.shape
    group = columns // D_HEAD
    seq = lax.axis_index("seq")
    wide[:, :length, :D_HEAD] = v_own[...]
    wide[:, length:, :D_HEAD] = v_near[...]
    wide[:, :, D_HEAD:] = jnp.ones((prompts, 2 * length, D_HEAD), jnp.bfloat16)
    causal = lax.broadcasted_iota(jnp.int32, (length, length), 1) <= lax.broadcasted_iota(
        jnp.int32, (length, length), 0
    )

    def run(with_near):
        for row in range(prompts):
            sum_ref, top_ref, tot_ref = outs[3 * row : 3 * row + 3]
            for head in range(group):
                cols = slice(head * D_HEAD, (head + 1) * D_HEAD)
                q = q_ref[row, :, cols]
                scores = jnp.where(causal, scores_of(q, k_own[row]), MASKED_SCORE)
                if with_near:
                    scores = jnp.concatenate([scores, scores_of(q, k_near[row])], axis=1)
                top = jnp.max(scores, axis=1, keepdims=True) * EXP2_SCALE
                summed = weighted(jnp.exp2(scores * EXP2_SCALE - top), wide[row, : scores.shape[1], :])
                sum_ref[:, cols] = summed[:, :D_HEAD]
                tot_ref[:, cols] = summed[:, D_HEAD:]
                top_ref[:, cols] = jnp.broadcast_to(top, (length, D_HEAD))

    @pl.when(seq % 2 == 0)
    def _():
        run(False)

    @pl.when(seq % 2 == 1)
    def _():
        run(True)


def merge_rows(span, cache, own_part, other_part, dec, flat):
    steps, rows, columns = dec.shape
    half = columns // 2
    group = half // D_HEAD
    queries = group * span
    role = lax.axis_index("role")
    for index, (part, kv) in enumerate(((own_part, role), (other_part, 1 - role))):
        top = row_to_column(part[queries : queries + 1, :], queries)
        total = row_to_column(part[queries + 1 : queries + 2, :], queries)
        cache_sum, cache_top, cache_tot = (ref[index] for ref in cache)
        high = jnp.maximum(top, cache_top)
        one, two = jnp.exp2(cache_top - high), jnp.exp2(top - high)
        result = (one * cache_sum + two * part[:queries, :]) / (one * cache_tot + two * total)
        for head in range(group):
            start = pl.multiple_of(kv * half + head * D_HEAD, D_HEAD)
            flat[:, pl.ds(start, D_HEAD)] = result[head * span : (head + 1) * span]
    for step in range(steps):
        dec[step] = flat[step * rows : (step + 1) * rows, :].astype(jnp.bfloat16)


def add_chunk(q, keys, wide, summed, total, top):
    scores = scores_of(q, keys)
    new = jnp.maximum(top, jnp.max(scores, axis=1, keepdims=True) * EXP2_SCALE)
    high = jnp.concatenate([new] * (scores.shape[1] // D_HEAD), axis=1)
    far = weighted(jnp.exp2(scores * EXP2_SCALE - high), wide)
    alpha = jnp.exp2(top - new)
    return summed * alpha + far[:, :D_HEAD], total * alpha + far[:, D_HEAD:], new


def add_chunk_at(q, keys, wide, summed, total, top):
    scores = scores_of(q, keys)
    high = jnp.concatenate([top] * (scores.shape[1] // D_HEAD), axis=1)
    far = weighted(jnp.exp2(scores * EXP2_SCALE - high), wide)
    return summed + far[:, :D_HEAD], total + far[:, D_HEAD:]


def widen(values, wide):
    wide[..., :D_HEAD] = values
    wide[..., D_HEAD:] = jnp.ones(values.shape, jnp.bfloat16)


def over_heads(q_ref, keys, wide, states, emit):
    prompts, length, columns = q_ref.shape
    blocks = [(row, slice(i, i + D_HEAD)) for row in range(prompts) for i in range(0, columns, D_HEAD)]
    worst = jnp.zeros((8, D_HEAD), jnp.float32)
    for row, cols in blocks:
        sum_ref, top_ref, tot_ref = states[3 * row : 3 * row + 3]
        top = top_ref[:, cols]
        summed, total = add_chunk_at(q_ref[row, :, cols], keys[row], wide[row], sum_ref[:, cols], tot_ref[:, cols], top)
        emit(row, cols, summed, total, top)
        for i in range(0, length, 8):
            worst = jnp.maximum(worst, total[i : i + 8])

    @pl.when(jnp.max(worst) > SUM_LIMIT)
    def _():
        for row, cols in blocks:
            sum_ref, top_ref, tot_ref = states[3 * row : 3 * row + 3]
            state = sum_ref[:, cols], tot_ref[:, cols], top_ref[:, cols]
            emit(row, cols, *add_chunk(q_ref[row, :, cols], keys[row], wide[row], *state))


def far_kernel(shift, q_ref, keys, values, _, *refs):
    states_in, states, wide = refs[: len(refs) // 2], refs[len(refs) // 2 : -1], refs[-1]

    def emit(row, cols, summed, total, top):
        for ref, value in zip(states[3 * row : 3 * row + 3], (summed, top, total)):
            ref[:, cols] = value

    @pl.when(lax.axis_index("seq") // 2 >= shift)
    def _():
        widen(values[...], wide)
        over_heads(q_ref, keys, wide, states_in, emit)

    @pl.when(lax.axis_index("seq") // 2 < shift)
    def _():
        for ref, value in zip(states, states_in):
            ref[...] = value[...]


def last_kernel(shift, info_ref, q_ref, keys, values, _, *refs):
    *states, out, wide = refs
    prompts, length, columns = q_ref.shape
    seq = lax.axis_index("seq")
    position = seq * length + lax.broadcasted_iota(jnp.int32, (length, D_HEAD), 0)

    def emit(row, cols, summed, total, top):
        live = position < info_ref[row : row + 1, :]
        out[row, :, cols] = jnp.where(live, summed / total, 0.0).astype(jnp.bfloat16)

    @pl.when(seq // 2 >= shift)
    def _():
        widen(values[...], wide)
        over_heads(q_ref, keys, wide, states, emit)

    @pl.when(seq // 2 < shift)
    def _():
        for row in range(prompts):
            sum_ref, _, tot_ref = states[3 * row : 3 * row + 3]
            for i in range(0, columns, D_HEAD):
                cols = slice(i, i + D_HEAD)
                emit(row, cols, sum_ref[:, cols], tot_ref[:, cols], None)


def finish_kernel(span, pre, cache_sum, cache_top, cache_tot, own_part, other_part, pre_hbm, dec_hbm, dec, flat, sems):
    copies = [pltpu.make_async_copy(pre, pre_hbm, sems.at[0]), pltpu.make_async_copy(dec, dec_hbm, sems.at[1])]
    copies[0].start()
    merge_rows(span, (cache_sum, cache_top, cache_tot), own_part, other_part, dec, flat)
    copies[1].start()
    for copy in copies:
        copy.wait()


VMEM = pl.BlockSpec(memory_space=pltpu.VMEM)
ANY = pl.BlockSpec(memory_space=pl.ANY)


def in_hbm(x):
    return pltpu.with_memory_space_constraint(x, pltpu.HBM)


def call(kernel, args, outs, scratch=(), specs=None, out_specs=None, aliases=None, us=1.0):
    return pl.pallas_call(
        kernel,
        out_shape=outs,
        in_specs=specs or [VMEM] * len(args),
        out_specs=out_specs or [VMEM] * len(outs),
        scratch_shapes=list(scratch),
        input_output_aliases=aliases or {},
        compiler_params=pltpu.CompilerParams(vmem_limit_bytes=VMEM_BYTES),
        cost_estimate=pl.CostEstimate(flops=int(us * 1.1e9), bytes_accessed=int(us * 3e6), transcendentals=0),
    )(*args)


def body(
    prefill_queries,
    prefill_keys,
    prefill_values,
    prompt_len,
    assignment,
    cache_len,
    cache_keys,
    cache_values,
    decode_queries,
    new_keys,
    new_values,
):
    seqs = lax.axis_size("seq")
    prompts, length, columns = prefill_queries.shape
    steps, rows, dec_columns = decode_queries.shape
    group = columns // D_HEAD
    span = steps * rows
    queries = group * span
    f32, bf16, i32 = jnp.float32, jnp.bfloat16, jnp.int32
    shape = jax.ShapeDtypeStruct
    after = lax.optimization_barrier

    def near(x):
        return lax.ppermute(x, "seq", [(i, i ^ 1) for i in range(seqs)])

    def around(x, shift):
        return lax.ppermute(x, "seq", [(i, (i + 2 * shift) % seqs) for i in range(seqs)])

    def partner(x):
        return lax.ppermute(x, "role", [(0, 1), (1, 0)])

    shifts = range(1, seqs // 2)
    far_keys = [around(prefill_keys, s) for s in shifts]
    far_values = [around(prefill_values, s) for s in shifts]
    (first,) = call(first_kernel, [in_hbm(prompt_len)], [shape((span, 128), f32)], specs=[ANY], us=3.0)
    own_keys, own_values, first = after((prefill_keys, prefill_values, first))
    near_keys, near_values = near(own_keys), near(own_values)
    message = shape((queries + 2 * span, 128), bf16)
    state = shape((2, queries, 128), f32)
    lengths = [assignment, prompt_len, cache_len]
    own_msg, other_msg, info, *cache = call(
        own_kernel,
        [in_hbm(x) for x in lengths] + [decode_queries, new_keys, new_values, cache_keys, cache_values, first],
        [message] * 2 + [shape((span, 128), i32)] + [state] * 3,
        [
            pltpu.SMEM(assignment.shape, i32),
            pltpu.SMEM(prompt_len.shape, i32),
            pltpu.SMEM(cache_len.shape, i32),
            pltpu.VMEM((span, dec_columns), f32),
            pltpu.VMEM((128, 2 * D_HEAD), f32),
            pltpu.VMEM((128, 2 * D_HEAD), f32),
            pltpu.SemaphoreType.DMA((len(lengths),)),
        ],
        specs=[ANY] * len(lengths) + [VMEM] * 5 + [ANY],
        us=1.3,
    )
    partner_msg = partner(other_msg)
    run = shape((length, columns), f32)
    states = call(
        local_kernel,
        (prefill_queries, prefill_keys, prefill_values, near_keys, near_values, info),
        [run] * (3 * prompts),
        [pltpu.VMEM((prompts, 2 * length, 2 * D_HEAD), bf16)],
        specs=[VMEM] * 5 + [ANY],
        us=2.9,
    )
    far_keys, partner_msg, states = after((far_keys, partner_msg, states))
    far_near_keys = [near(k) for k in far_keys]
    far_values, states = after((far_values, states))
    far_near_values = [near(v) for v in far_values]
    wide = pltpu.VMEM((prompts, length, 2 * D_HEAD), bf16)

    def far_step(shift, keys, values, states, marker):
        return call(
            functools.partial(far_kernel, shift),
            (prefill_queries, keys, values, marker, *states),
            [run] * len(states),
            [wide],
            specs=[VMEM] * 3 + [ANY] + [VMEM] * len(states),
            us=1.5,
        )

    marker = info
    for index, shift in enumerate(shifts):
        states = far_step(shift, far_keys[index], far_values[index], states, marker)
        if index < len(far_keys) - 1:
            states = far_step(shift, far_near_keys[index], far_near_values[index], states, marker)
    chunks = [prefill_keys, prefill_values, near_keys, near_values]
    for quad in zip(far_keys, far_values, far_near_keys, far_near_values):
        chunks += quad
    part = shape((queries + 8, 128), f32)
    own_part, partner_part = call(
        functools.partial(prompt_kernel, span),
        (own_msg, partner_msg, info, *chunks, states[0]),
        [part] * 2,
        specs=[VMEM] * (3 + len(chunks)) + [ANY],
        us=0.7,
    )
    other_part = partner(partner_part)
    (prefill_out,) = call(
        functools.partial(last_kernel, shifts[-1]),
        (info, prefill_queries, far_near_keys[-1], far_near_values[-1], own_part, *states),
        [shape(prefill_queries.shape, bf16)],
        [wide],
        specs=[VMEM] * 4 + [ANY] + [VMEM] * len(states),
        us=2.2,
    )
    return tuple(
        call(
            functools.partial(finish_kernel, span),
            (prefill_out, *cache, own_part, other_part),
            [shape(prefill_queries.shape, bf16), shape(decode_queries.shape, bf16)],
            [
                pltpu.VMEM(decode_queries.shape, bf16),
                pltpu.VMEM((span, dec_columns), f32),
                pltpu.SemaphoreType.DMA((2,)),
            ],
            out_specs=[ANY] * 2,
            us=1.0,
        )
    )


def solution(mesh):
    in_specs = (
        P(None, "seq", ("head", "role")),
        P(None, "seq", ("head", "role")),
        P(None, "seq", ("head", "role")),
        P(),
        P(("seq", "role")),
        P(("seq", "role")),
        P(("seq", "role"), None, "head"),
        P(("seq", "role"), None, "head"),
        P(None, ("seq", "role"), "head"),
        P(None, ("seq", "role"), "head"),
        P(None, ("seq", "role"), "head"),
    )
    out_specs = (P(None, "seq", ("head", "role")), P(None, ("seq", "role"), "head"))
    return jax.shard_map(body, mesh=mesh, in_specs=in_specs, out_specs=out_specs, check_vma=False)
```

time: 19.3 us -> 18.6 us (0.964)
  the two profiles are of different devices: /device:TPU:29 before, /device:TPU:28 now
where the time goes in v4:
time: 18.6 us; the launch traced here: 18.5 us
  Pallas kernels  10.5 us (56%)
  starting transfers between devices  6.21 us (33%)
  waiting for transfers between devices  0.93 us (5%)
  between operations  0.78 us (4%)
    pallas_call x7, Pallas kernels, call(): pl.pallas_call(kernel, out_shape=outs, in_specs=specs or [VMEM] * len(arg...  10.5 us
    ppermute x2, starting transfers between devices, partner(): return lax.ppermute(x, 'role', [(0, 1), (1, 0)])  3.11 us
    ppermute x2, starting transfers between devices, around(): lax.ppermute(x, 'seq', [(i, (i + 2 * shift) % seqs) for i in range(seqs)])  2.09 us
    ppermute x4, starting transfers between devices, near(): return lax.ppermute(x, 'seq', [(i, i ^ 1) for i in range(seqs)])  1.01 us
    ppermute x2, waiting for transfers between devices, partner(): return lax.ppermute(x, 'role', [(0, 1), (1, 0)])  0.69 us
  transfers between devices with their start and end apart: 8, of which 2 were waited for; matrix products, arithmetic and copies ran while one was open for 0% of the time, Pallas kernels for 48%

profile of v4, /device:TPU:28, one launch (start us, length us, event | category | flops | bytes accessed | tf_op | source)
XLA Modules:
  0.0 18.5 jit_solution(15026532190645352596)
XLA Ops:
  0.7 0.6 %collective-permute-start = (bf16[2,256,128]{2,1,0:T(8,128)(2,1)}, bf16[2,256,128]{2,1,0:T(8,128)(2,1)S(1)}, u32[]{:S(2)}, u32[]{:S(2)}) collective-permute-start(bf16[2,256,128]{2,1,0:T(8,128)(2,1)} %refs_3_.1), channel_id=1, source_target_pairs={{0,16},{8,24},{16,0},{24,8},{1,17},{9,25},{17,1},{25,9},{2,18},{10... | collective-permute-start | bytes 393224 | tf_op jit(solution)/shard_map/ppermute | solution.py:359
  1.3 1.5 %collective-permute-start.5 = (bf16[2,256,128]{2,1,0:T(8,128)(2,1)}, bf16[2,256,128]{2,1,0:T(8,128)(2,1)S(1)}, u32[]{:S(2)}, u32[]{:S(2)}) collective-permute-start(bf16[2,256,128]{2,1,0:T(8,128)(2,1)} %refs_4_.1), channel_id=1, source_target_pairs={{0,16},{8,24},{16,0},{24,8},{1,17},{9,25},{17,1},{25,9},{2,18},{10... | collective-permute-start | bytes 393224 | tf_op jit(solution)/shard_map/ppermute | solution.py:359
  2.8 0.0 collective-permute-start.2
  2.8 0.5 %collective-permute-start.3 = (bf16[2,256,128]{2,1,0:T(8,128)(2,1)S(1)}, bf16[2,256,128]{2,1,0:T(8,128)(2,1)S(1)}, u32[]{:S(2)}, u32[]{:S(2)}) collective-permute-start(bf16[2,256,128]{2,1,0:T(8,128)(2,1)S(1)} %copy-done.4), channel_id=1, source_target_pairs={{0,8},{8,0},{16,24},{24,16},{1,9},{9,1},{17,25},{25,17},{2,10},{10... | collective-permute-start | bytes 393224 | tf_op jit(solution)/shard_map/ppermute | solution.py:356
  3.3 0.0 copy-done.2
  3.3 0.0 copy-done.1
  3.3 1.6 %shard_map.123 = (bf16[80,128]{1,0:T(8,128)(2,1)S(1)}, bf16[80,128]{1,0:T(8,128)(2,1)S(1)}, s32[8,128]{1,0:T(8,128)S(1)}, f32[2,64,128]{2,1,0:T(8,128)S(1)}, f32...) custom-call(s32[2]{0:T(128)} %asg_hbm.1, s32[2]{0:T(128)} %plen_hbm.1, s32[2]{0:T(128)} %clen_hbm.1, ...), custom_call_target="tpu_custom_call" | custom-call | flops 1430000000 | bytes 3900000 | tf_op jit(solution)/shard_map/pallas_call | solution.py:320
  5.0 1.6 %collective-permute-start.1 = (bf16[80,128]{1,0:T(8,128)(2,1)S(1)}, bf16[80,128]{1,0:T(8,128)(2,1)S(1)}, u32[]{:S(2)}, u32[]{:S(2)}) collective-permute-start(bf16[80,128]{1,0:T(8,128)(2,1)S(1)} %get-tuple-element.42), channel_id=1, source_target_pairs={{0,1},{1,0},{2,3},{3,2},{4,5},{5,4},{6,7},{7,6},{8,9},{9,8},{10,11... | collective-permute-start | bytes 61448 | tf_op jit(solution)/shard_map/ppermute | solution.py:362
  6.5 0.0 collective-permute-done.2.k_near.refs_5_
  6.5 0.0 collective-permute-done.3.v_near.refs_6_
  6.5 1.6 %shard_map.124 = (f32[256,1024]{1,0:T(8,128)S(1)}, f32[256,1024]{1,0:T(8,128)S(1)}, f32[256,1024]{1,0:T(8,128)S(1)}, f32[256,1024]{1,0:T(8,128)S(1)}, f32[256,1024]{1,0:T(8,128)S(1)}, /*index=5*/f32[256,1024]{1,0:T(8,128)S(1)}) custom-call(bf16[2,256,1024]{2,1,0:T(8,128)(2,1)S(1)} %copy-done, bf16[2,256,128]{2,1,0:T(8,128)(2,1)S(1)} %copy-done.3, ...), custom_call_target="tpu_custom_call" | custom-call | flops 3190000128 | bytes 8700000 | tf_op jit(solution)/shard_map/pallas_call | solution.py:320
  8.1 0.7 %collective-permute-done.1.refs_1_ = bf16[80,128]{1,0:T(8,128)(2,1)S(1)} collective-permute-done((bf16[80,128]{1,0:T(8,128)(2,1)S(1)}, bf16[80,128]{1,0:T(8,128)(2,1)S(1)}, u32[]{:S(2)}, u32[]{:S(2)}) %collective-permute-start.1) | collective-permute-done | bytes 20512 | tf_op jit(solution)/shard_map/ppermute | solution.py:362
  8.8 0.0 collective-permute-done.keys.refs_7_
  8.8 0.2 %collective-permute-done.5.values.refs_8_ = bf16[2,256,128]{2,1,0:T(8,128)(2,1)S(1)} collective-permute-done((bf16[2,256,128]{2,1,0:T(8,128)(2,1)}, bf16[2,256,128]{2,1,0:T(8,128)(2,1)S(1)}, u32[]{:S(2)}, u32[]{:S(2)}) %collective-permute-start.5) | collective-permute-done | bytes 131104 | tf_op jit(solution)/shard_map/ppermute | solution.py:359
  9.0 0.3 %collective-permute-start.6 = (bf16[2,256,128]{2,1,0:T(8,128)(2,1)S(1)}, bf16[2,256,128]{2,1,0:T(8,128)(2,1)S(1)}, u32[]{:S(2)}, u32[]{:S(2)}) collective-permute-start(bf16[2,256,128]{2,1,0:T(8,128)(2,1)S(1)} %collective-permute-done.5.values.refs_8_), channel_id=1, source_target_pairs={{0,8},{8,0},{16,24},{24,16},{1,9},{9,1},{17,25},{25,17},{2,10},{10... | collective-permute-start | bytes 393224 | tf_op jit(solution)/shard_map/ppermute | solution.py:356
  9.4 0.2 collective-permute-start.4
  9.5 1.6 %shard_map.125 = (f32[256,1024]{1,0:T(8,128)S(1)}, f32[256,1024]{1,0:T(8,128)S(1)}, f32[256,1024]{1,0:T(8,128)S(1)}, f32[256,1024]{1,0:T(8,128)S(1)}, f32[256,1024]{1,0:T(8,128)S(1)}, /*index=5*/f32[256,1024]{1,0:T(8,128)S(1)}) custom-call(bf16[2,256,1024]{2,1,0:T(8,128)(2,1)S(1)} %copy-done, bf16[2,256,128]{2,1,0:T(8,128)(2,1)S(1)} %collective-permute-done.keys.refs_7_, ...), custom_call_target="tpu_custom_call" | custom-call | flops 1650000000 | bytes 4500000 | tf_op jit(solution)/shard_map/pallas_call | solution.py:320
  11.2 0.0 collective-permute-done.6.refs_10_.values
  11.2 0.0 collective-permute-done.4.refs_9_.keys
  11.2 0.7 %shard_map.126 = (f32[72,128]{1,0:T(8,128)S(1)}, f32[72,128]{1,0:T(8,128)S(1)}) custom-call(bf16[80,128]{1,0:T(8,128)(2,1)S(1)} %get-tuple-element.59.refs_0_, bf16[80,128]{1,0:T(8,128)(2,1)S(1)} %collective-permute-done.1.refs_1_, s32[8,128]{1,0:T(8,128)S(1)} %get-tuple-element.41._.refs_2_.info_ref, bf16[2,256,128]{2,1,0:T(8,128)(2,1)S(1)} %copy-done.3, ...), custom_call_target="tpu_custom_call" | custom-call | flops 770000000 | bytes 2100000 | tf_op jit(solution)/shard_map/pallas_call | solution.py:320
  11.9 1.5 %collective-permute-start.7 = (f32[72,128]{1,0:T(8,128)S(1)}, f32[72,128]{1,0:T(8,128)S(1)}, u32[]{:S(2)}, u32[]{:S(2)}) collective-permute-start(f32[72,128]{1,0:T(8,128)S(1)} %get-tuple-element.77), channel_id=1, source_target_pairs={{0,1},{1,0},{2,3},{3,2},{4,5},{5,4},{6,7},{7,6},{8,9},{9,8},{10,11... | collective-permute-start | bytes 110600 | tf_op jit(solution)/shard_map/ppermute | solution.py:362
  13.4 4.0 %shard_map.127.pre = bf16[2,256,1024]{2,1,0:T(8,128)(2,1)S(1)} custom-call(s32[8,128]{1,0:T(8,128)S(1)} %get-tuple-element.41._.refs_2_.info_ref, bf16[2,256,1024]{2,1,0:T(8,128)(2,1)S(1)} %copy-done, bf16[2,256,128]{2,1,0:T(8,128)(2,1)S(1)} %collective-permute-done.4.refs_9_.keys, bf16[2,256,128]{2,1,0:T(8,128)(2,1)S(1)} %collective-permute-done.6.refs_10_.values, ...), custom_call_target="tpu_custom_call" | custom-call | flops 2420000000 | bytes 6600000 | tf_op jit(solution)/shard_map/pallas_call | solution.py:320
  17.5 0.0 collective-permute-done.7.other_part
  17.5 1.0 %shard_map.128 = (bf16[2,256,1024]{2,1,0:T(8,128)(2,1)}, bf16[4,2,2048]{2,1,0:T(2,128)(2,1)}) custom-call(bf16[2,256,1024]{2,1,0:T(8,128)(2,1)S(1)} %shard_map.127.pre, f32[2,64,128]{2,1,0:T(8,128)S(1)} %get-tuple-element.74.cache_sum, f32[2,64,128]{2,1,0:T(8,128)S(1)} %get-tuple-element.75.cache_top, f32[2,64,128]{2,1,0:T(8,128)S(1)} %get-tuple-element.76.cache_tot, ...), custom_call_target="tpu_custom_call" | custom-call | flops 1100000000 | bytes 3000000 | tf_op jit(solution)/shard_map/pallas_call | solution.py:320
  (15 shorter events, 0.0 us)
Async XLA Ops:
  0.6 2.2 %copy-start.3 = (bf16[2,256,128]{2,1,0:T(8,128)(2,1)S(1)}, bf16[2,256,128]{2,1,0:T(8,128)(2,1)}, u32[]{:S(2)}) copy-start(bf16[2,256,128]{2,1,0:T(8,128)(2,1)} %refs_3_.1) | copy-start | bytes 393220
  0.6 2.2 %copy-start.4 = (bf16[2,256,128]{2,1,0:T(8,128)(2,1)S(1)}, bf16[2,256,128]{2,1,0:T(8,128)(2,1)}, u32[]{:S(2)}) copy-start(bf16[2,256,128]{2,1,0:T(8,128)(2,1)} %refs_4_.1) | copy-start | bytes 393220
  0.7 2.7 %copy-start.7 = (bf16[4,2,256]{2,1,0:T(2,128)(2,1)S(1)}, bf16[4,2,256]{2,1,0:T(2,128)(2,1)}, u32[]{:S(2)}) copy-start(bf16[4,2,256]{2,1,0:T(2,128)(2,1)} %nv.1) | copy-start | bytes 12292
  0.7 2.7 %copy-start.6 = (bf16[4,2,256]{2,1,0:T(2,128)(2,1)S(1)}, bf16[4,2,256]{2,1,0:T(2,128)(2,1)}, u32[]{:S(2)}) copy-start(bf16[4,2,256]{2,1,0:T(2,128)(2,1)} %nk.1) | copy-start | bytes 12292
  0.7 2.6 %copy-start.5 = (bf16[4,2,2048]{2,1,0:T(2,128)(2,1)S(1)}, bf16[4,2,2048]{2,1,0:T(2,128)(2,1)}, u32[]{:S(2)}) copy-start(bf16[4,2,2048]{2,1,0:T(2,128)(2,1)} %dq.1) | copy-start | bytes 98308
  0.7 2.6 %copy-start.2 = (bf16[2,1024,256]{2,1,0:T(8,128)(2,1)S(1)}, bf16[2,1024,256]{2,1,0:T(8,128)(2,1)}, u32[]{:S(2)}) copy-start(bf16[2,1024,256]{2,1,0:T(8,128)(2,1)} %cv_ref.1) | copy-start | bytes 3145732
  0.7 2.6 %copy-start.1 = (bf16[2,1024,256]{2,1,0:T(8,128)(2,1)S(1)}, bf16[2,1024,256]{2,1,0:T(8,128)(2,1)}, u32[]{:S(2)}) copy-start(bf16[2,1024,256]{2,1,0:T(8,128)(2,1)} %ck_ref.1) | copy-start | bytes 3145732
  0.7 8.1 %collective-permute-start = (bf16[2,256,128]{2,1,0:T(8,128)(2,1)}, bf16[2,256,128]{2,1,0:T(8,128)(2,1)S(1)}, u32[]{:S(2)}, u32[]{:S(2)}) collective-permute-start(bf16[2,256,128]{2,1,0:T(8,128)(2,1)} %refs_3_.1), channel_id=1, source_target_pairs={{0,16},{8,24},{16,0},{24,8},{1,17},{9,25},{17,1},{25,9},{2,18},{10... | collective-permute-start | bytes 393224 | tf_op jit(solution)/shard_map/ppermute | solution.py:359
  1.3 7.7 %collective-permute-start.5 = (bf16[2,256,128]{2,1,0:T(8,128)(2,1)}, bf16[2,256,128]{2,1,0:T(8,128)(2,1)S(1)}, u32[]{:S(2)}, u32[]{:S(2)}) collective-permute-start(bf16[2,256,128]{2,1,0:T(8,128)(2,1)} %refs_4_.1), channel_id=1, source_target_pairs={{0,16},{8,24},{16,0},{24,8},{1,17},{9,25},{17,1},{25,9},{2,18},{10... | collective-permute-start | bytes 393224 | tf_op jit(solution)/shard_map/ppermute | solution.py:359
  2.8 3.7 %copy-start = (bf16[2,256,1024]{2,1,0:T(8,128)(2,1)S(1)}, bf16[2,256,1024]{2,1,0:T(8,128)(2,1)}, u32[]{:S(2)}) copy-start(bf16[2,256,1024]{2,1,0:T(8,128)(2,1)} %q_ref.5) | copy-start | bytes 3145732
  2.8 3.7 %collective-permute-start.2 = (bf16[2,256,128]{2,1,0:T(8,128)(2,1)S(1)}, bf16[2,256,128]{2,1,0:T(8,128)(2,1)S(1)}, u32[]{:S(2)}, u32[]{:S(2)}) collective-permute-start(bf16[2,256,128]{2,1,0:T(8,128)(2,1)S(1)} %copy-done.3), channel_id=1, source_target_pairs={{0,8},{8,0},{16,24},{24,16},{1,9},{9,1},{17,25},{25,17},{2,10},{10... | collective-permute-start | bytes 393224 | tf_op jit(solution)/shard_map/ppermute | solution.py:356
  2.8 3.7 %collective-permute-start.3 = (bf16[2,256,128]{2,1,0:T(8,128)(2,1)S(1)}, bf16[2,256,128]{2,1,0:T(8,128)(2,1)S(1)}, u32[]{:S(2)}, u32[]{:S(2)}) collective-permute-start(bf16[2,256,128]{2,1,0:T(8,128)(2,1)S(1)} %copy-done.4), channel_id=1, source_target_pairs={{0,8},{8,0},{16,24},{24,16},{1,9},{9,1},{17,25},{25,17},{2,10},{10... | collective-permute-start | bytes 393224 | tf_op jit(solution)/shard_map/ppermute | solution.py:356
  5.0 3.8 %collective-permute-start.1 = (bf16[80,128]{1,0:T(8,128)(2,1)S(1)}, bf16[80,128]{1,0:T(8,128)(2,1)S(1)}, u32[]{:S(2)}, u32[]{:S(2)}) collective-permute-start(bf16[80,128]{1,0:T(8,128)(2,1)S(1)} %get-tuple-element.42), channel_id=1, source_target_pairs={{0,1},{1,0},{2,3},{3,2},{4,5},{5,4},{6,7},{7,6},{8,9},{9,8},{10,11... | collective-permute-start | bytes 61448 | tf_op jit(solution)/shard_map/ppermute | solution.py:362
  9.0 2.2 %collective-permute-start.6 = (bf16[2,256,128]{2,1,0:T(8,128)(2,1)S(1)}, bf16[2,256,128]{2,1,0:T(8,128)(2,1)S(1)}, u32[]{:S(2)}, u32[]{:S(2)}) collective-permute-start(bf16[2,256,128]{2,1,0:T(8,128)(2,1)S(1)} %collective-permute-done.5.values.refs_8_), channel_id=1, source_target_pairs={{0,8},{8,0},{16,24},{24,16},{1,9},{9,1},{17,25},{25,17},{2,10},{10... | collective-permute-start | bytes 393224 | tf_op jit(solution)/shard_map/ppermute | solution.py:356
  9.4 1.9 %collective-permute-start.4 = (bf16[2,256,128]{2,1,0:T(8,128)(2,1)S(1)}, bf16[2,256,128]{2,1,0:T(8,128)(2,1)S(1)}, u32[]{:S(2)}, u32[]{:S(2)}) collective-permute-start(bf16[2,256,128]{2,1,0:T(8,128)(2,1)S(1)} %collective-permute-done.keys.refs_7_), channel_id=1, source_target_pairs={{0,8},{8,0},{16,24},{24,16},{1,9},{9,1},{17,25},{25,17},{2,10},{10... | collective-permute-start | bytes 393224 | tf_op jit(solution)/shard_map/ppermute | solution.py:356
  11.9 5.6 %collective-permute-start.7 = (f32[72,128]{1,0:T(8,128)S(1)}, f32[72,128]{1,0:T(8,128)S(1)}, u32[]{:S(2)}, u32[]{:S(2)}) collective-permute-start(f32[72,128]{1,0:T(8,128)S(1)} %get-tuple-element.77), channel_id=1, source_target_pairs={{0,1},{1,0},{2,3},{3,2},{4,5},{5,4},{6,7},{7,6},{8,9},{9,8},{10,11... | collective-permute-start | bytes 110600 | tf_op jit(solution)/shard_map/ppermute | solution.py:362

commit v5 on v4

--- a/solution.py
+++ b/solution.py
@@ -61,13 +61,9 @@
 
 
 def own_kernel(
-    asg_hbm, plen_hbm, clen_hbm, dq, nk, nv, ck_ref, cv_ref, _,
-    own_ref, other_ref, info_ref, sum_ref, top_ref, tot_ref, asg, plen, clen, flat, fk, fv, sems,
+    asg, plen, clen, dq, nk, nv, ck_ref, cv_ref, _,
+    own_ref, other_ref, info_ref, sum_ref, top_ref, tot_ref, flat, fk, fv,
 ):
-    moves = [(asg_hbm, asg), (plen_hbm, plen), (clen_hbm, clen)]
-    copies = [pltpu.make_async_copy(a, b, sems.at[i]) for i, (a, b) in enumerate(moves)]
-    for copy in copies:
-        copy.start()
     role = lax.axis_index("role")
     steps, rows, columns = dq.shape
     span = steps * rows
@@ -96,8 +92,6 @@
         fresh = scores_of(q, fk[:, cols].astype(jnp.bfloat16))
         fresh = jnp.where(fresh_mask, fresh * EXP2_SCALE, MASKED_SCORE)
         scores.append((fresh, select_rows(q_row, [scores_of(q, ck_ref[r, :, cols]) for r in range(rows)])))
-    for copy in copies:
-        copy.wait()
     row_index = lax.broadcasted_iota(jnp.int32, (span, 128), 0)
     prompt = jnp.zeros((span, 128), jnp.float32)
     for row in range(rows):
@@ -160,24 +154,24 @@
         )
 
 
-def local_kernel(q_ref, k_own, v_own, k_near, v_near, _, *refs):
+def local_kernel(blocks, q_ref, k_own, v_own, k_near, v_near, _, *refs):
     outs, wide = refs[:-1], refs[-1]
-    prompts, length, columns = q_ref.shape
-    group = columns // D_HEAD
+    prompts, length, _ = q_ref.shape
     seq = lax.axis_index("seq")
-    wide[:, :length, :D_HEAD] = v_own[...]
-    wide[:, length:, :D_HEAD] = v_near[...]
-    wide[:, :, D_HEAD:] = jnp.ones((prompts, 2 * length, D_HEAD), jnp.bfloat16)
+    for row in sorted({row for row, _, _ in blocks}):
+        wide[row, :length, :D_HEAD] = v_own[row]
+        wide[row, length:, :D_HEAD] = v_near[row]
+        wide[row, :, D_HEAD:] = jnp.ones((2 * length, D_HEAD), jnp.bfloat16)
     causal = lax.broadcasted_iota(jnp.int32, (length, length), 1) <= lax.broadcasted_iota(
         jnp.int32, (length, length), 0
     )
 
     def run(with_near):
-        for row in range(prompts):
-            sum_ref, top_ref, tot_ref = outs[3 * row : 3 * row + 3]
-            for head in range(group):
-                cols = slice(head * D_HEAD, (head + 1) * D_HEAD)
-                q = q_ref[row, :, cols]
+        for index, (row, start, stop) in enumerate(blocks):
+            sum_ref, top_ref, tot_ref = outs[3 * index : 3 * index + 3]
+            for head in range(start, stop):
+                cols = slice((head - start) * D_HEAD, (head - start + 1) * D_HEAD)
+                q = q_ref[row, :, head * D_HEAD : (head + 1) * D_HEAD]
                 scores = jnp.where(causal, scores_of(q, k_own[row]), MASKED_SCORE)
                 if with_near:
                     scores = jnp.concatenate([scores, scores_of(q, k_near[row])], axis=1)
@@ -216,8 +210,12 @@
         dec[step] = flat[step * rows : (step + 1) * rows, :].astype(jnp.bfloat16)
 
 
-def add_chunk(q, keys, wide, summed, total, top):
-    scores = scores_of(q, keys)
+def joined(q, keys):
+    return jnp.concatenate([scores_of(q, one) for one in keys], axis=1)
+
+
+def add_keys(q, keys, wide, summed, total, top):
+    scores = joined(q, keys)
     new = jnp.maximum(top, jnp.max(scores, axis=1, keepdims=True) * EXP2_SCALE)
     high = jnp.concatenate([new] * (scores.shape[1] // D_HEAD), axis=1)
     far = weighted(jnp.exp2(scores * EXP2_SCALE - high), wide)
@@ -225,91 +223,95 @@
     return summed * alpha + far[:, :D_HEAD], total * alpha + far[:, D_HEAD:], new
 
 
-def add_chunk_at(q, keys, wide, summed, total, top):
-    scores = scores_of(q, keys)
+def add_keys_at(q, keys, wide, summed, total, top):
+    scores = joined(q, keys)
     high = jnp.concatenate([top] * (scores.shape[1] // D_HEAD), axis=1)
     far = weighted(jnp.exp2(scores * EXP2_SCALE - high), wide)
     return summed + far[:, :D_HEAD], total + far[:, D_HEAD:]
 
 
-def widen(values, wide):
-    wide[..., :D_HEAD] = values
-    wide[..., D_HEAD:] = jnp.ones(values.shape, jnp.bfloat16)
-
-
-def over_heads(q_ref, keys, wide, states, emit):
+def far_kernel(blocks, shift, last, info_ref, q_ref, k_one, v_one, k_two, v_two, _, *refs):
     prompts, length, columns = q_ref.shape
-    blocks = [(row, slice(i, i + D_HEAD)) for row in range(prompts) for i in range(0, columns, D_HEAD)]
-    worst = jnp.zeros((8, D_HEAD), jnp.float32)
-    for row, cols in blocks:
-        sum_ref, top_ref, tot_ref = states[3 * row : 3 * row + 3]
-        top = top_ref[:, cols]
-        summed, total = add_chunk_at(q_ref[row, :, cols], keys[row], wide[row], sum_ref[:, cols], tot_ref[:, cols], top)
-        emit(row, cols, summed, total, top)
-        for i in range(0, length, 8):
-            worst = jnp.maximum(worst, total[i : i + 8])
-
-    @pl.when(jnp.max(worst) > SUM_LIMIT)
-    def _():
-        for row, cols in blocks:
-            sum_ref, top_ref, tot_ref = states[3 * row : 3 * row + 3]
-            state = sum_ref[:, cols], tot_ref[:, cols], top_ref[:, cols]
-            emit(row, cols, *add_chunk(q_ref[row, :, cols], keys[row], wide[row], *state))
-
-
-def far_kernel(shift, q_ref, keys, values, _, *refs):
-    states_in, states, wide = refs[: len(refs) // 2], refs[len(refs) // 2 : -1], refs[-1]
-
-    def emit(row, cols, summed, total, top):
-        for ref, value in zip(states[3 * row : 3 * row + 3], (summed, top, total)):
-            ref[:, cols] = value
-
-    @pl.when(lax.axis_index("seq") // 2 >= shift)
-    def _():
-        widen(values[...], wide)
-        over_heads(q_ref, keys, wide, states_in, emit)
-
-    @pl.when(lax.axis_index("seq") // 2 < shift)
-    def _():
-        for ref, value in zip(states, states_in):
-            ref[...] = value[...]
-
-
-def last_kernel(shift, info_ref, q_ref, keys, values, _, *refs):
-    *states, out, wide = refs
-    prompts, length, columns = q_ref.shape
+    count = 3 * len(blocks)
+    states, outs, (wide, sem) = refs[:count], refs[count:-2], refs[-2:]
     seq = lax.axis_index("seq")
     position = seq * length + lax.broadcasted_iota(jnp.int32, (length, D_HEAD), 0)
-
-    def emit(row, cols, summed, total, top):
-        live = position < info_ref[row : row + 1, :]
-        out[row, :, cols] = jnp.where(live, summed / total, 0.0).astype(jnp.bfloat16)
+    places = [
+        (index, row, slice(head * D_HEAD, (head + 1) * D_HEAD), slice((head - start) * D_HEAD, (head - start + 1) * D_HEAD))
+        for index, (row, start, stop) in enumerate(blocks)
+        for head in range(start, stop)
+    ]
+
+    def state_of(index, at):
+        return (states[3 * index][:, at], states[3 * index + 2][:, at], states[3 * index + 1][:, at])
+
+    def emit(index, row, cols, at, summed, total, top):
+        if last:
+            live = position < info_ref[row : row + 1, :]
+            outs[0][row, :, cols] = jnp.where(live, summed / total, 0.0).astype(jnp.bfloat16)
+        else:
+            for ref, value in zip(outs[3 * index : 3 * index + 3], (summed, top, total)):
+                ref[:, at] = value
 
     @pl.when(seq // 2 >= shift)
     def _():
-        widen(values[...], wide)
-        over_heads(q_ref, keys, wide, states, emit)
+        wide[:, :length, :D_HEAD] = v_one[...]
+        wide[:, length:, :D_HEAD] = v_two[...]
+        wide[:, :, D_HEAD:] = jnp.ones((prompts, 2 * length, D_HEAD), jnp.bfloat16)
+        worst = jnp.zeros((8, D_HEAD), jnp.float32)
+        for index, row, cols, at in places:
+            state = state_of(index, at)
+            summed, total = add_keys_at(q_ref[row, :, cols], (k_one[row], k_two[row]), wide[row], *state)
+            emit(index, row, cols, at, summed, total, state[2])
+            peaks = [total[i : i + 8] for i in range(0, length, 8)]
+            worst = functools.reduce(jnp.maximum, [functools.reduce(jnp.maximum, peaks[i::4]) for i in range(4)], worst)
+
+        @pl.when(jnp.max(worst) > SUM_LIMIT)
+        def _():
+            for index, (row, start, stop) in enumerate(blocks):
+
+                @pl.loop(0, stop - start)
+                def _(head, index=index, row=row, start=start):
+                    at = pl.ds(pl.multiple_of(head * D_HEAD, D_HEAD), D_HEAD)
+                    cols = pl.ds(pl.multiple_of((start + head) * D_HEAD, D_HEAD), D_HEAD)
+                    state = state_of(index, at)
+                    new = add_keys(q_ref[row, :, cols], (k_one[row], k_two[row]), wide[row], *state)
+                    emit(index, row, cols, at, *new)
 
     @pl.when(seq // 2 < shift)
     def _():
-        for row in range(prompts):
-            sum_ref, _, tot_ref = states[3 * row : 3 * row + 3]
-            for i in range(0, columns, D_HEAD):
-                cols = slice(i, i + D_HEAD)
-                emit(row, cols, sum_ref[:, cols], tot_ref[:, cols], None)
-
-
-def finish_kernel(span, pre, cache_sum, cache_top, cache_tot, own_part, other_part, pre_hbm, dec_hbm, dec, flat, sems):
-    copies = [pltpu.make_async_copy(pre, pre_hbm, sems.at[0]), pltpu.make_async_copy(dec, dec_hbm, sems.at[1])]
-    copies[0].start()
+        for index, row, cols, at in places:
+            emit(index, row, cols, at, *state_of(index, at))
+        if last:
+            copy = pltpu.make_async_copy(outs[0], outs[1], sem)
+            copy.start()
+            copy.wait()
+
+
+def finish_kernel(
+    shift, span, pre, cache_sum, cache_top, cache_tot, own_part, other_part, _, dec_hbm, pre_hbm, dec, flat, sems
+):
+    copy = pltpu.make_async_copy(pre, pre_hbm, sems.at[0])
+    dec_copy = pltpu.make_async_copy(dec, dec_hbm, sems.at[1])
+    late = lax.axis_index("seq") // 2 >= shift
+
+    @pl.when(late)
+    def _():
+        copy.start()
+
     merge_rows(span, (cache_sum, cache_top, cache_tot), own_part, other_part, dec, flat)
-    copies[1].start()
-    for copy in copies:
+    dec_copy.start()
+
+    @pl.when(late)
+    def _():
         copy.wait()
+
+    dec_copy.wait()
 
 
 VMEM = pl.BlockSpec(memory_space=pltpu.VMEM)
 ANY = pl.BlockSpec(memory_space=pl.ANY)
+SMEM = pl.BlockSpec(memory_space=pltpu.SMEM)
 
 
 def in_hbm(x):
@@ -359,7 +361,8 @@
         return lax.ppermute(x, "seq", [(i, (i + 2 * shift) % seqs) for i in range(seqs)])
 
     def partner(x):
-        return lax.ppermute(x, "role", [(0, 1), (1, 0)])
+        moves = [(i * 2 + r, (i ^ 1) * 2 + 1 - r) for i in range(seqs) for r in range(2)]
+        return lax.ppermute(x, ("seq", "role"), moves)
 
     shifts = range(1, seqs // 2)
     far_keys = [around(prefill_keys, s) for s in shifts]
@@ -369,88 +372,80 @@
     near_keys, near_values = near(own_keys), near(own_values)
     message = shape((queries + 2 * span, 128), bf16)
     state = shape((2, queries, 128), f32)
-    lengths = [assignment, prompt_len, cache_len]
     own_msg, other_msg, info, *cache = call(
         own_kernel,
-        [in_hbm(x) for x in lengths] + [decode_queries, new_keys, new_values, cache_keys, cache_values, first],
+        [assignment, prompt_len, cache_len, decode_queries, new_keys, new_values, cache_keys, cache_values, first],
         [message] * 2 + [shape((span, 128), i32)] + [state] * 3,
         [
-            pltpu.SMEM(assignment.shape, i32),
-            pltpu.SMEM(prompt_len.shape, i32),
-            pltpu.SMEM(cache_len.shape, i32),
             pltpu.VMEM((span, dec_columns), f32),
             pltpu.VMEM((128, 2 * D_HEAD), f32),
             pltpu.VMEM((128, 2 * D_HEAD), f32),
-            pltpu.SemaphoreType.DMA((len(lengths),)),
         ],
-        specs=[ANY] * len(lengths) + [VMEM] * 5 + [ANY],
+        specs=[SMEM] * 3 + [VMEM] * 5 + [ANY],
         us=1.3,
     )
     partner_msg = partner(other_msg)
-    run = shape((length, columns), f32)
-    states = call(
-        local_kernel,
-        (prefill_queries, prefill_keys, prefill_values, near_keys, near_values, info),
-        [run] * (3 * prompts),
-        [pltpu.VMEM((prompts, 2 * length, 2 * D_HEAD), bf16)],
-        specs=[VMEM] * 5 + [ANY],
-        us=2.9,
-    )
-    far_keys, partner_msg, states = after((far_keys, partner_msg, states))
+    blocks = [(row, 0, group) for row in range(prompts - 1)]
+    blocks += [(prompts - 1, 0, group // 2), (prompts - 1, group // 2, group)]
+    runs = [[shape((length, (stop - start) * D_HEAD), f32)] * 3 for _, start, stop in blocks]
+
+    def local(some, outs, marker):
+        return call(
+            functools.partial(local_kernel, some),
+            (prefill_queries, prefill_keys, prefill_values, near_keys, near_values, marker),
+            sum(outs, []),
+            [pltpu.VMEM((prompts, 2 * length, 2 * D_HEAD), bf16)],
+            specs=[VMEM] * 5 + [ANY],
+            us=0.2 * sum(stop - start for _, start, stop in some),
+        )
+
+    states = local(blocks[:-1], runs[:-1], info)
+    far_keys, states = after((far_keys, states))
     far_near_keys = [near(k) for k in far_keys]
-    far_values, states = after((far_values, states))
+    far_values, partner_msg, states = after((far_values, partner_msg, states))
     far_near_values = [near(v) for v in far_values]
-    wide = pltpu.VMEM((prompts, length, 2 * D_HEAD), bf16)
-
-    def far_step(shift, keys, values, states, marker):
-        return call(
-            functools.partial(far_kernel, shift),
-            (prefill_queries, keys, values, marker, *states),
-            [run] * len(states),
-            [wide],
-            specs=[VMEM] * 3 + [ANY] + [VMEM] * len(states),
-            us=1.5,
-        )
-
-    marker = info
-    for index, shift in enumerate(shifts):
-        states = far_step(shift, far_keys[index], far_values[index], states, marker)
-        if index < len(far_keys) - 1:
-            states = far_step(shift, far_near_keys[index], far_near_values[index], states, marker)
-    chunks = [prefill_keys, prefill_values, near_keys, near_values]
-    for quad in zip(far_keys, far_values, far_near_keys, far_near_values):
-        chunks += quad
+    states = [*states, *local(blocks[-1:], runs[-1:], states[0])]
+    far = list(zip(far_keys, far_values, far_near_keys, far_near_values))
+    chunks = [prefill_keys, prefill_values, near_keys, near_values] + sum([list(four) for four in far], [])
     part = shape((queries + 8, 128), f32)
     own_part, partner_part = call(
         functools.partial(prompt_kernel, span),
-        (own_msg, partner_msg, info, *chunks, states[0]),
+        (own_msg, partner_msg, info, *chunks, states[-1]),
         [part] * 2,
         specs=[VMEM] * (3 + len(chunks)) + [ANY],
         us=0.7,
     )
     other_part = partner(partner_part)
-    (prefill_out,) = call(
-        functools.partial(last_kernel, shifts[-1]),
-        (info, prefill_queries, far_near_keys[-1], far_near_values[-1], own_part, *states),
-        [shape(prefill_queries.shape, bf16)],
-        [wide],
-        specs=[VMEM] * 4 + [ANY] + [VMEM] * len(states),
-        us=2.2,
+    for index, shift in enumerate(shifts):
+        last = index == len(shifts) - 1
+        outs, out_specs = sum(runs, []), [VMEM] * len(states)
+        if last:
+            outs, out_specs = [shape(prefill_queries.shape, bf16)] * 2, [VMEM, ANY]
+        states = call(
+            functools.partial(far_kernel, blocks, shift, last),
+            (info, prefill_queries, *far[index], own_part, *states),
+            outs,
+            [pltpu.VMEM((prompts, 2 * length, 2 * D_HEAD), bf16), pltpu.SemaphoreType.DMA(())],
+            specs=[VMEM] * 6 + [ANY] + [VMEM] * len(states),
+            out_specs=out_specs,
+            us=2.8,
+        )
+    pre, prefill_out = states
+    decode_out, prefill_out = call(
+        functools.partial(finish_kernel, shifts[-1], span),
+        (pre, *cache, own_part, other_part, prefill_out),
+        [shape(decode_queries.shape, bf16), shape(prefill_queries.shape, bf16)],
+        [
+            pltpu.VMEM(decode_queries.shape, bf16),
+            pltpu.VMEM((span, dec_columns), f32),
+            pltpu.SemaphoreType.DMA((2,)),
+        ],
+        specs=[VMEM] * 6 + [ANY],
+        out_specs=[ANY, ANY],
+        aliases={6: 1},
+        us=0.7,
     )
-    return tuple(
-        call(
-            functools.partial(finish_kernel, span),
-            (prefill_out, *cache, own_part, other_part),
-            [shape(prefill_queries.shape, bf16), shape(decode_queries.shape, bf16)],
-            [
-                pltpu.VMEM(decode_queries.shape, bf16),
-                pltpu.VMEM((span, dec_columns), f32),
-                pltpu.SemaphoreType.DMA((2,)),
-            ],
-            out_specs=[ANY] * 2,
-            us=1.0,
-        )
-    )
+    return prefill_out, decode_out
 
 
 def solution(mesh):

time: 18.6 us -> 25.9 us (1.39)
  Pallas kernels: 10.5 us -> 17.1 us
  waiting for transfers between devices: 0.93 us -> 1.95 us
  starting transfers between devices: 6.21 us -> 5.82 us
    pallas_call x7, Pallas kernels: 10.5 us -> 17.1 us  [call(): pl.pallas_call(kernel, out_shape=outs, in_specs=specs or [VMEM] * len(arg...]
    ppermute x2, waiting for transfers between devices: 0.22 us -> 0.88 us  [around(): lax.ppermute(x, 'seq', [(i, (i + 2 * shift) % seqs) for i in range(seqs)])]
    ppermute x2, starting transfers between devices: 3.11 us -> 2.73 us  [partner(): return lax.ppermute(x, ('seq', 'role'), moves)]
    ppermute x4, waiting for transfers between devices: 0.01 us -> 0.35 us  [near(): return lax.ppermute(x, 'seq', [(i, i ^ 1) for i in range(seqs)])]
  transfers between devices with their start and end apart: 8 -> 8, of which waited for: 2 -> 4; matrix products, arithmetic and copies ran while one was open for 0% -> 0% of each run, Pallas kernels for 48% -> 60%
where the time goes in v5:
time: 25.9 us; the launch traced here: 25.8 us
  Pallas kernels  17.1 us (66%)
  starting transfers between devices  5.82 us (22%)
  waiting for transfers between devices  1.95 us (8%)
  between operations  0.82 us (3%)
    pallas_call x7, Pallas kernels, call(): pl.pallas_call(kernel, out_shape=outs, in_specs=specs or [VMEM] * len(arg...  17.1 us
    ppermute x2, starting transfers between devices, partner(): return lax.ppermute(x, ('seq', 'role'), moves)  2.73 us
    ppermute x2, starting transfers between devices, around(): lax.ppermute(x, 'seq', [(i, (i + 2 * shift) % seqs) for i in range(seqs)])  2.09 us
    ppermute x4, starting transfers between devices, near(): return lax.ppermute(x, 'seq', [(i, i ^ 1) for i in range(seqs)])  1.01 us
    ppermute x2, waiting for transfers between devices, around(): lax.ppermute(x, 'seq', [(i, (i + 2 * shift) % seqs) for i in range(seqs)])  0.88 us
    ppermute x2, waiting for transfers between devices, partner(): return lax.ppermute(x, ('seq', 'role'), moves)  0.72 us
  transfers between devices with their start and end apart: 8, of which 4 were waited for; matrix products, arithmetic and copies ran while one was open for 0% of the time, Pallas kernels for 60%

profile of v5, /device:TPU:28, one launch (start us, length us, event | category | flops | bytes accessed | tf_op | source)
XLA Modules:
  0.0 25.8 jit_solution(14494345363058480829)
XLA Ops:
  0.7 0.6 %collective-permute-start = (bf16[2,256,128]{2,1,0:T(8,128)(2,1)}, bf16[2,256,128]{2,1,0:T(8,128)(2,1)S(1)}, u32[]{:S(2)}, u32[]{:S(2)}) collective-permute-start(bf16[2,256,128]{2,1,0:T(8,128)(2,1)} %refs_3_.1), channel_id=1, source_target_pairs={{0,16},{8,24},{16,0},{24,8},{1,17},{9,25},{17,1},{25,9},{2,18},{10... | collective-permute-start | bytes 393224 | tf_op jit(solution)/shard_map/ppermute | solution.py:361
  1.3 1.5 %collective-permute-start.3 = (bf16[2,256,128]{2,1,0:T(8,128)(2,1)}, bf16[2,256,128]{2,1,0:T(8,128)(2,1)S(1)}, u32[]{:S(2)}, u32[]{:S(2)}) collective-permute-start(bf16[2,256,128]{2,1,0:T(8,128)(2,1)} %refs_4_.1), channel_id=1, source_target_pairs={{0,16},{8,24},{16,0},{24,8},{1,17},{9,25},{17,1},{25,9},{2,18},{10... | collective-permute-start | bytes 393224 | tf_op jit(solution)/shard_map/ppermute | solution.py:361
  2.8 0.0 copy-done.3
  2.8 0.0 collective-permute-start.1
  2.9 0.5 %collective-permute-start.2 = (bf16[2,256,128]{2,1,0:T(8,128)(2,1)S(1)}, bf16[2,256,128]{2,1,0:T(8,128)(2,1)S(1)}, u32[]{:S(2)}, u32[]{:S(2)}) collective-permute-start(bf16[2,256,128]{2,1,0:T(8,128)(2,1)S(1)} %copy-done.4), channel_id=1, source_target_pairs={{0,8},{8,0},{16,24},{24,16},{1,9},{9,1},{17,25},{25,17},{2,10},{10... | collective-permute-start | bytes 393224 | tf_op jit(solution)/shard_map/ppermute | solution.py:358
  3.4 0.0 copy-done.5
  3.4 1.5 %shard_map.123 = (bf16[80,128]{1,0:T(8,128)(2,1)S(1)}, bf16[80,128]{1,0:T(8,128)(2,1)S(1)}, s32[8,128]{1,0:T(8,128)S(1)}, f32[2,64,128]{2,1,0:T(8,128)S(1)}, f32...) custom-call(s32[2]{0:T(128)S(1)} %copy-done.8, s32[2]{0:T(128)S(1)} %copy-done.9, s32[2]{0:T(128)S(1)} %copy-done.10, ...), custom_call_target="tpu_custom_call" | custom-call | flops 1430000000 | bytes 3900000 | tf_op jit(solution)/shard_map/pallas_call | solution.py:322
  4.9 1.2 %collective-permute-start.4 = (bf16[80,128]{1,0:T(8,128)(2,1)S(1)}, bf16[80,128]{1,0:T(8,128)(2,1)S(1)}, u32[]{:S(2)}, u32[]{:S(2)}) collective-permute-start(bf16[80,128]{1,0:T(8,128)(2,1)S(1)} %get-tuple-element.52), channel_id=1, source_target_pairs={{0,9},{1,8},{8,1},{9,0},{16,25},{17,24},{24,17},{25,16},{2,11},{3,... | collective-permute-start | bytes 61448 | tf_op jit(solution)/shard_map/ppermute | solution.py:365
  6.1 0.0 collective-permute-done.1.k_near.refs_5_
  6.1 0.0 collective-permute-done.2.v_near.refs_6_
  6.2 1.3 %shard_map.124 = (f32[256,1024]{1,0:T(8,128)S(1)}, f32[256,1024]{1,0:T(8,128)S(1)}, f32[256,1024]{1,0:T(8,128)S(1)}, f32[256,512]{1,0:T(8,128)S(1)}, f32[256,512]{1,0:T(8,128)S(1)}, /*index=5*/f32[256,512]{1,0:T(8,128)S(1)}) custom-call(bf16[2,256,1024]{2,1,0:T(8,128)(2,1)S(1)} %copy-done.2, bf16[2,256,128]{2,1,0:T(8,128)(2,1)S(1)} %copy-done.3, ...), custom_call_target="tpu_custom_call" | custom-call | flops 2640000000 | bytes 7200000 | tf_op jit(solution)/shard_map/pallas_call | solution.py:322
  7.4 0.0 collective-permute-done.refs_7_.k_one
  7.5 0.7 %collective-permute-done.4.refs_1_ = bf16[80,128]{1,0:T(8,128)(2,1)S(1)} collective-permute-done((bf16[80,128]{1,0:T(8,128)(2,1)S(1)}, bf16[80,128]{1,0:T(8,128)(2,1)S(1)}, u32[]{:S(2)}, u32[]{:S(2)}) %collective-permute-start.4) | collective-permute-done | bytes 20512 | tf_op jit(solution)/shard_map/ppermute | solution.py:365
  8.2 0.9 %collective-permute-done.3.refs_8_.v_one = bf16[2,256,128]{2,1,0:T(8,128)(2,1)S(1)} collective-permute-done((bf16[2,256,128]{2,1,0:T(8,128)(2,1)}, bf16[2,256,128]{2,1,0:T(8,128)(2,1)S(1)}, u32[]{:S(2)}, u32[]{:S(2)}) %collective-permute-start.3) | collective-permute-done | bytes 131104 | tf_op jit(solution)/shard_map/ppermute | solution.py:361
  9.1 0.0 collective-permute-start.6
  9.1 0.5 %collective-permute-start.5 = (bf16[2,256,128]{2,1,0:T(8,128)(2,1)S(1)}, bf16[2,256,128]{2,1,0:T(8,128)(2,1)S(1)}, u32[]{:S(2)}, u32[]{:S(2)}) collective-permute-start(bf16[2,256,128]{2,1,0:T(8,128)(2,1)S(1)} %collective-permute-done.refs_7_.k_one), channel_id=1, source_target_pairs={{0,8},{8,0},{16,24},{24,16},{1,9},{9,1},{17,25},{25,17},{2,10},{10... | collective-permute-start | bytes 393224 | tf_op jit(solution)/shard_map/ppermute | solution.py:358
  9.6 0.7 %shard_map.125 = (f32[256,512]{1,0:T(8,128)S(1)}, f32[256,512]{1,0:T(8,128)S(1)}, f32[256,512]{1,0:T(8,128)S(1)}) custom-call(bf16[2,256,1024]{2,1,0:T(8,128)(2,1)S(1)} %copy-done.2, bf16[2,256,128]{2,1,0:T(8,128)(2,1)S(1)} %copy-done.3, bf16[2,256,128]{2,1,0:T(8,128)(2,1)S(1)} %copy-done.4, bf16[2,256,128]{2,1,0:T(8,128)(2,1)S(1)} %collective-permute-done.1.k_near.refs_5_, ...), custom_call_target="tpu_custom_call" | custom-call | flops 880000000 | bytes 2400000 | tf_op jit(solution)/shard_map/pallas_call | solution.py:322
  10.2 0.2 collective-permute-done.6.refs_10_.v_two
  10.4 0.2 collective-permute-done.5.refs_9_.k_two
  10.6 0.7 %shard_map.126 = (f32[72,128]{1,0:T(8,128)S(1)}, f32[72,128]{1,0:T(8,128)S(1)}) custom-call(bf16[80,128]{1,0:T(8,128)(2,1)S(1)} %get-tuple-element.60.refs_0_, bf16[80,128]{1,0:T(8,128)(2,1)S(1)} %collective-permute-done.4.refs_1_, s32[8,128]{1,0:T(8,128)S(1)} %get-tuple-element.42._.refs_2_.info_ref, bf16[2,256,128]{2,1,0:T(8,128)(2,1)S(1)} %copy-done.3, ...), custom_call_target="tpu_custom_call" | custom-call | flops 770000000 | bytes 2100000 | tf_op jit(solution)/shard_map/pallas_call | solution.py:322
  11.3 1.5 %collective-permute-start.7 = (f32[72,128]{1,0:T(8,128)S(1)}, f32[72,128]{1,0:T(8,128)S(1)}, u32[]{:S(2)}, u32[]{:S(2)}) collective-permute-start(f32[72,128]{1,0:T(8,128)S(1)} %get-tuple-element.76), channel_id=1, source_target_pairs={{0,9},{1,8},{8,1},{9,0},{16,25},{17,24},{24,17},{25,16},{2,11},{3,... | collective-permute-start | bytes 110600 | tf_op jit(solution)/shard_map/ppermute | solution.py:365
  12.7 12.0 %shard_map.127 = (bf16[2,256,1024]{2,1,0:T(8,128)(2,1)S(1)}, bf16[2,256,1024]{2,1,0:T(8,128)(2,1)}) custom-call(s32[8,128]{1,0:T(8,128)S(1)} %get-tuple-element.42._.refs_2_.info_ref, bf16[2,256,1024]{2,1,0:T(8,128)(2,1)S(1)} %copy-done.2, bf16[2,256,128]{2,1,0:T(8,128)(2,1)S(1)} %collective-permute-done.refs_7_.k_one, ...), custom_call_target="tpu_custom_call" | custom-call | flops 3080000000 | bytes 8400000 | tf_op jit(solution)/shard_map/pallas_call | solution.py:322
  24.7 0.0 collective-permute-done.7.other_part
  24.8 1.0 %shard_map.128 = (bf16[4,2,2048]{2,1,0:T(2,128)(2,1)}, bf16[2,256,1024]{2,1,0:T(8,128)(2,1)}) custom-call(bf16[2,256,1024]{2,1,0:T(8,128)(2,1)S(1)} %get-tuple-element.72.pre, f32[2,64,128]{2,1,0:T(8,128)S(1)} %get-tuple-element.73.cache_sum, f32[2,64,128]{2,1,0:T(8,128)S(1)} %get-tuple-element.74.cache_top, ...), custom_call_target="tpu_custom_call", output_to_operand_aliasing={{1}: (6, {})} | custom-call | flops 770000000 | bytes 2100000 | tf_op jit(solution)/shard_map/pallas_call | solution.py:322
  (21 shorter events, 0.0 us)
Async XLA Ops:
  0.6 2.2 %copy-start.3 = (bf16[2,256,128]{2,1,0:T(8,128)(2,1)S(1)}, bf16[2,256,128]{2,1,0:T(8,128)(2,1)}, u32[]{:S(2)}) copy-start(bf16[2,256,128]{2,1,0:T(8,128)(2,1)} %refs_3_.1) | copy-start | bytes 393220
  0.6 2.2 %copy-start.4 = (bf16[2,256,128]{2,1,0:T(8,128)(2,1)S(1)}, bf16[2,256,128]{2,1,0:T(8,128)(2,1)}, u32[]{:S(2)}) copy-start(bf16[2,256,128]{2,1,0:T(8,128)(2,1)} %refs_4_.1) | copy-start | bytes 393220
  0.7 2.7 %copy-start.9 = (s32[2]{0:T(128)S(1)}, s32[2]{0:T(128)}, u32[]{:S(2)}) copy-start(s32[2]{0:T(128)} %plen.1) | copy-start | bytes 28
  0.7 2.7 %copy-start.7 = (bf16[4,2,256]{2,1,0:T(2,128)(2,1)S(1)}, bf16[4,2,256]{2,1,0:T(2,128)(2,1)}, u32[]{:S(2)}) copy-start(bf16[4,2,256]{2,1,0:T(2,128)(2,1)} %nv.1) | copy-start | bytes 12292
  0.7 2.7 %copy-start.6 = (bf16[4,2,256]{2,1,0:T(2,128)(2,1)S(1)}, bf16[4,2,256]{2,1,0:T(2,128)(2,1)}, u32[]{:S(2)}) copy-start(bf16[4,2,256]{2,1,0:T(2,128)(2,1)} %nk.1) | copy-start | bytes 12292
  0.7 2.7 %copy-start.5 = (bf16[4,2,2048]{2,1,0:T(2,128)(2,1)S(1)}, bf16[4,2,2048]{2,1,0:T(2,128)(2,1)}, u32[]{:S(2)}) copy-start(bf16[4,2,2048]{2,1,0:T(2,128)(2,1)} %dq.1) | copy-start | bytes 98308
  0.7 2.7 %copy-start.1 = (bf16[2,1024,256]{2,1,0:T(8,128)(2,1)S(1)}, bf16[2,1024,256]{2,1,0:T(8,128)(2,1)}, u32[]{:S(2)}) copy-start(bf16[2,1024,256]{2,1,0:T(8,128)(2,1)} %cv_ref.1) | copy-start | bytes 3145732
  0.7 2.7 %copy-start = (bf16[2,1024,256]{2,1,0:T(8,128)(2,1)S(1)}, bf16[2,1024,256]{2,1,0:T(8,128)(2,1)}, u32[]{:S(2)}) copy-start(bf16[2,1024,256]{2,1,0:T(8,128)(2,1)} %ck_ref.1) | copy-start | bytes 3145732
  0.7 2.7 %copy-start.10 = (s32[2]{0:T(128)S(1)}, s32[2]{0:T(128)}, u32[]{:S(2)}) copy-start(s32[2]{0:T(128)} %clen.1) | copy-start | bytes 28
  0.7 2.7 %copy-start.8 = (s32[2]{0:T(128)S(1)}, s32[2]{0:T(128)}, u32[]{:S(2)}) copy-start(s32[2]{0:T(128)} %asg.1) | copy-start | bytes 28
  0.7 6.7 %collective-permute-start = (bf16[2,256,128]{2,1,0:T(8,128)(2,1)}, bf16[2,256,128]{2,1,0:T(8,128)(2,1)S(1)}, u32[]{:S(2)}, u32[]{:S(2)}) collective-permute-start(bf16[2,256,128]{2,1,0:T(8,128)(2,1)} %refs_3_.1), channel_id=1, source_target_pairs={{0,16},{8,24},{16,0},{24,8},{1,17},{9,25},{17,1},{25,9},{2,18},{10... | collective-permute-start | bytes 393224 | tf_op jit(solution)/shard_map/ppermute | solution.py:361
  1.3 7.7 %collective-permute-start.3 = (bf16[2,256,128]{2,1,0:T(8,128)(2,1)}, bf16[2,256,128]{2,1,0:T(8,128)(2,1)S(1)}, u32[]{:S(2)}, u32[]{:S(2)}) collective-permute-start(bf16[2,256,128]{2,1,0:T(8,128)(2,1)} %refs_4_.1), channel_id=1, source_target_pairs={{0,16},{8,24},{16,0},{24,8},{1,17},{9,25},{17,1},{25,9},{2,18},{10... | collective-permute-start | bytes 393224 | tf_op jit(solution)/shard_map/ppermute | solution.py:361
  2.8 3.3 %copy-start.2 = (bf16[2,256,1024]{2,1,0:T(8,128)(2,1)S(1)}, bf16[2,256,1024]{2,1,0:T(8,128)(2,1)}, u32[]{:S(2)}) copy-start(bf16[2,256,1024]{2,1,0:T(8,128)(2,1)} %q_ref.5) | copy-start | bytes 3145732
  2.8 3.3 %collective-permute-start.1 = (bf16[2,256,128]{2,1,0:T(8,128)(2,1)S(1)}, bf16[2,256,128]{2,1,0:T(8,128)(2,1)S(1)}, u32[]{:S(2)}, u32[]{:S(2)}) collective-permute-start(bf16[2,256,128]{2,1,0:T(8,128)(2,1)S(1)} %copy-done.3), channel_id=1, source_target_pairs={{0,8},{8,0},{16,24},{24,16},{1,9},{9,1},{17,25},{25,17},{2,10},{10... | collective-permute-start | bytes 393224 | tf_op jit(solution)/shard_map/ppermute | solution.py:358
  2.9 3.3 %collective-permute-start.2 = (bf16[2,256,128]{2,1,0:T(8,128)(2,1)S(1)}, bf16[2,256,128]{2,1,0:T(8,128)(2,1)S(1)}, u32[]{:S(2)}, u32[]{:S(2)}) collective-permute-start(bf16[2,256,128]{2,1,0:T(8,128)(2,1)S(1)} %copy-done.4), channel_id=1, source_target_pairs={{0,8},{8,0},{16,24},{24,16},{1,9},{9,1},{17,25},{25,17},{2,10},{10... | collective-permute-start | bytes 393224 | tf_op jit(solution)/shard_map/ppermute | solution.py:358
  4.9 3.3 %collective-permute-start.4 = (bf16[80,128]{1,0:T(8,128)(2,1)S(1)}, bf16[80,128]{1,0:T(8,128)(2,1)S(1)}, u32[]{:S(2)}, u32[]{:S(2)}) collective-permute-start(bf16[80,128]{1,0:T(8,128)(2,1)S(1)} %get-tuple-element.52), channel_id=1, source_target_pairs={{0,9},{1,8},{8,1},{9,0},{16,25},{17,24},{24,17},{25,16},{2,11},{3,... | collective-permute-start | bytes 61448 | tf_op jit(solution)/shard_map/ppermute | solution.py:365
  9.1 1.3 %collective-permute-start.6 = (bf16[2,256,128]{2,1,0:T(8,128)(2,1)S(1)}, bf16[2,256,128]{2,1,0:T(8,128)(2,1)S(1)}, u32[]{:S(2)}, u32[]{:S(2)}) collective-permute-start(bf16[2,256,128]{2,1,0:T(8,128)(2,1)S(1)} %collective-permute-done.3.refs_8_.v_one), channel_id=1, source_target_pairs={{0,8},{8,0},{16,24},{24,16},{1,9},{9,1},{17,25},{25,17},{2,10},{10... | collective-permute-start | bytes 393224 | tf_op jit(solution)/shard_map/ppermute | solution.py:358
  9.1 1.5 %collective-permute-start.5 = (bf16[2,256,128]{2,1,0:T(8,128)(2,1)S(1)}, bf16[2,256,128]{2,1,0:T(8,128)(2,1)S(1)}, u32[]{:S(2)}, u32[]{:S(2)}) collective-permute-start(bf16[2,256,128]{2,1,0:T(8,128)(2,1)S(1)} %collective-permute-done.refs_7_.k_one), channel_id=1, source_target_pairs={{0,8},{8,0},{16,24},{24,16},{1,9},{9,1},{17,25},{25,17},{2,10},{10... | collective-permute-start | bytes 393224 | tf_op jit(solution)/shard_map/ppermute | solution.py:358
  11.3 13.5 %collective-permute-start.7 = (f32[72,128]{1,0:T(8,128)S(1)}, f32[72,128]{1,0:T(8,128)S(1)}, u32[]{:S(2)}, u32[]{:S(2)}) collective-permute-start(f32[72,128]{1,0:T(8,128)S(1)} %get-tuple-element.76), channel_id=1, source_target_pairs={{0,9},{1,8},{8,1},{9,0},{16,25},{17,24},{24,17},{25,16},{2,11},{3,... | collective-permute-start | bytes 110600 | tf_op jit(solution)/shard_map/ppermute | solution.py:365

commit v6 on v5

--- a/solution.py
+++ b/solution.py
@@ -259,12 +259,19 @@
         wide[:, length:, :D_HEAD] = v_two[...]
         wide[:, :, D_HEAD:] = jnp.ones((prompts, 2 * length, D_HEAD), jnp.bfloat16)
         worst = jnp.zeros((8, D_HEAD), jnp.float32)
+        if last:
+            first_copy = pltpu.make_async_copy(outs[0].at[0], outs[1].at[0], sem)
         for index, row, cols, at in places:
             state = state_of(index, at)
             summed, total = add_keys_at(q_ref[row, :, cols], (k_one[row], k_two[row]), wide[row], *state)
             emit(index, row, cols, at, summed, total, state[2])
+            if last and row == 0 and cols.stop == columns:
+                first_copy.start()
             peaks = [total[i : i + 8] for i in range(0, length, 8)]
             worst = functools.reduce(jnp.maximum, [functools.reduce(jnp.maximum, peaks[i::4]) for i in range(4)], worst)
+
+        if last:
+            first_copy.wait()
 
         @pl.when(jnp.max(worst) > SUM_LIMIT)
         def _():
@@ -278,6 +285,10 @@
                     new = add_keys(q_ref[row, :, cols], (k_one[row], k_two[row]), wide[row], *state)
                     emit(index, row, cols, at, *new)
 
+            if last:
+                first_copy.start()
+                first_copy.wait()
+
     @pl.when(seq // 2 < shift)
     def _():
         for index, row, cols, at in places:
@@ -291,7 +302,7 @@
 def finish_kernel(
     shift, span, pre, cache_sum, cache_top, cache_tot, own_part, other_part, _, dec_hbm, pre_hbm, dec, flat, sems
 ):
-    copy = pltpu.make_async_copy(pre, pre_hbm, sems.at[0])
+    copy = pltpu.make_async_copy(pre.at[1:], pre_hbm.at[1:], sems.at[0])
     dec_copy = pltpu.make_async_copy(dec, dec_hbm, sems.at[1])
     late = lax.axis_index("seq") // 2 >= shift
 

time: 25.9 us -> 26.5 us (1.023)
  Pallas kernels: 17.1 us -> 17.7 us
    pallas_call x7, Pallas kernels: 17.1 us -> 17.7 us  [call(): pl.pallas_call(kernel, out_shape=outs, in_specs=specs or [VMEM] * len(arg...]
  transfers between devices with their start and end apart: 8 -> 8, of which waited for: 4 -> 4; matrix products, arithmetic and copies ran while one was open for 0% -> 0% of each run, Pallas kernels for 60% -> 62%
where the time goes in v6:
time: 26.5 us; the launch traced here: 26.4 us
  Pallas kernels  17.7 us (67%)
  starting transfers between devices  5.82 us (22%)
  waiting for transfers between devices  1.95 us (7%)
  between operations  0.82 us (3%)
    pallas_call x7, Pallas kernels, call(): pl.pallas_call(kernel, out_shape=outs, in_specs=specs or [VMEM] * len(arg...  17.7 us
    ppermute x2, starting transfers between devices, partner(): return lax.ppermute(x, ('seq', 'role'), moves)  2.73 us
    ppermute x2, starting transfers between devices, around(): lax.ppermute(x, 'seq', [(i, (i + 2 * shift) % seqs) for i in range(seqs)])  2.09 us
    ppermute x4, starting transfers between devices, near(): return lax.ppermute(x, 'seq', [(i, i ^ 1) for i in range(seqs)])  1.01 us
    ppermute x2, waiting for transfers between devices, around(): lax.ppermute(x, 'seq', [(i, (i + 2 * shift) % seqs) for i in range(seqs)])  0.88 us
    ppermute x2, waiting for transfers between devices, partner(): return lax.ppermute(x, ('seq', 'role'), moves)  0.72 us
  transfers between devices with their start and end apart: 8, of which 4 were waited for; matrix products, arithmetic and copies ran while one was open for 0% of the time, Pallas kernels for 62%

profile of v6, /device:TPU:28, one launch (start us, length us, event | category | flops | bytes accessed | tf_op | source)
XLA Modules:
  0.0 26.4 jit_solution(17790681446717973819)
XLA Ops:
  0.7 0.6 %collective-permute-start = (bf16[2,256,128]{2,1,0:T(8,128)(2,1)}, bf16[2,256,128]{2,1,0:T(8,128)(2,1)S(1)}, u32[]{:S(2)}, u32[]{:S(2)}) collective-permute-start(bf16[2,256,128]{2,1,0:T(8,128)(2,1)} %refs_3_.1), channel_id=1, source_target_pairs={{0,16},{8,24},{16,0},{24,8},{1,17},{9,25},{17,1},{25,9},{2,18},{10... | collective-permute-start | bytes 393224 | tf_op jit(solution)/shard_map/ppermute | solution.py:372
  1.3 1.5 %collective-permute-start.3 = (bf16[2,256,128]{2,1,0:T(8,128)(2,1)}, bf16[2,256,128]{2,1,0:T(8,128)(2,1)S(1)}, u32[]{:S(2)}, u32[]{:S(2)}) collective-permute-start(bf16[2,256,128]{2,1,0:T(8,128)(2,1)} %refs_4_.1), channel_id=1, source_target_pairs={{0,16},{8,24},{16,0},{24,8},{1,17},{9,25},{17,1},{25,9},{2,18},{10... | collective-permute-start | bytes 393224 | tf_op jit(solution)/shard_map/ppermute | solution.py:372
  2.8 0.0 copy-done.3
  2.8 0.0 collective-permute-start.1
  2.9 0.5 %collective-permute-start.2 = (bf16[2,256,128]{2,1,0:T(8,128)(2,1)S(1)}, bf16[2,256,128]{2,1,0:T(8,128)(2,1)S(1)}, u32[]{:S(2)}, u32[]{:S(2)}) collective-permute-start(bf16[2,256,128]{2,1,0:T(8,128)(2,1)S(1)} %copy-done.4), channel_id=1, source_target_pairs={{0,8},{8,0},{16,24},{24,16},{1,9},{9,1},{17,25},{25,17},{2,10},{10... | collective-permute-start | bytes 393224 | tf_op jit(solution)/shard_map/ppermute | solution.py:369
  3.4 0.0 copy-done.5
  3.4 1.5 %shard_map.123 = (bf16[80,128]{1,0:T(8,128)(2,1)S(1)}, bf16[80,128]{1,0:T(8,128)(2,1)S(1)}, s32[8,128]{1,0:T(8,128)S(1)}, f32[2,64,128]{2,1,0:T(8,128)S(1)}, f32...) custom-call(s32[2]{0:T(128)S(1)} %copy-done.8, s32[2]{0:T(128)S(1)} %copy-done.9, s32[2]{0:T(128)S(1)} %copy-done.10, ...), custom_call_target="tpu_custom_call" | custom-call | flops 1430000000 | bytes 3900000 | tf_op jit(solution)/shard_map/pallas_call | solution.py:333
  4.9 1.2 %collective-permute-start.4 = (bf16[80,128]{1,0:T(8,128)(2,1)S(1)}, bf16[80,128]{1,0:T(8,128)(2,1)S(1)}, u32[]{:S(2)}, u32[]{:S(2)}) collective-permute-start(bf16[80,128]{1,0:T(8,128)(2,1)S(1)} %get-tuple-element.52), channel_id=1, source_target_pairs={{0,9},{1,8},{8,1},{9,0},{16,25},{17,24},{24,17},{25,16},{2,11},{3,... | collective-permute-start | bytes 61448 | tf_op jit(solution)/shard_map/ppermute | solution.py:376
  6.1 0.0 collective-permute-done.1.k_near.refs_5_
  6.1 0.0 collective-permute-done.2.v_near.refs_6_
  6.2 1.3 %shard_map.124 = (f32[256,1024]{1,0:T(8,128)S(1)}, f32[256,1024]{1,0:T(8,128)S(1)}, f32[256,1024]{1,0:T(8,128)S(1)}, f32[256,512]{1,0:T(8,128)S(1)}, f32[256,512]{1,0:T(8,128)S(1)}, /*index=5*/f32[256,512]{1,0:T(8,128)S(1)}) custom-call(bf16[2,256,1024]{2,1,0:T(8,128)(2,1)S(1)} %copy-done.2, bf16[2,256,128]{2,1,0:T(8,128)(2,1)S(1)} %copy-done.3, ...), custom_call_target="tpu_custom_call" | custom-call | flops 2640000000 | bytes 7200000 | tf_op jit(solution)/shard_map/pallas_call | solution.py:333
  7.4 0.0 collective-permute-done.refs_7_.k_one
  7.5 0.7 %collective-permute-done.4.refs_1_ = bf16[80,128]{1,0:T(8,128)(2,1)S(1)} collective-permute-done((bf16[80,128]{1,0:T(8,128)(2,1)S(1)}, bf16[80,128]{1,0:T(8,128)(2,1)S(1)}, u32[]{:S(2)}, u32[]{:S(2)}) %collective-permute-start.4) | collective-permute-done | bytes 20512 | tf_op jit(solution)/shard_map/ppermute | solution.py:376
  8.2 0.9 %collective-permute-done.3.refs_8_.v_one = bf16[2,256,128]{2,1,0:T(8,128)(2,1)S(1)} collective-permute-done((bf16[2,256,128]{2,1,0:T(8,128)(2,1)}, bf16[2,256,128]{2,1,0:T(8,128)(2,1)S(1)}, u32[]{:S(2)}, u32[]{:S(2)}) %collective-permute-start.3) | collective-permute-done | bytes 131104 | tf_op jit(solution)/shard_map/ppermute | solution.py:372
  9.1 0.0 collective-permute-start.6
  9.1 0.5 %collective-permute-start.5 = (bf16[2,256,128]{2,1,0:T(8,128)(2,1)S(1)}, bf16[2,256,128]{2,1,0:T(8,128)(2,1)S(1)}, u32[]{:S(2)}, u32[]{:S(2)}) collective-permute-start(bf16[2,256,128]{2,1,0:T(8,128)(2,1)S(1)} %collective-permute-done.refs_7_.k_one), channel_id=1, source_target_pairs={{0,8},{8,0},{16,24},{24,16},{1,9},{9,1},{17,25},{25,17},{2,10},{10... | collective-permute-start | bytes 393224 | tf_op jit(solution)/shard_map/ppermute | solution.py:369
  9.6 0.7 %shard_map.125 = (f32[256,512]{1,0:T(8,128)S(1)}, f32[256,512]{1,0:T(8,128)S(1)}, f32[256,512]{1,0:T(8,128)S(1)}) custom-call(bf16[2,256,1024]{2,1,0:T(8,128)(2,1)S(1)} %copy-done.2, bf16[2,256,128]{2,1,0:T(8,128)(2,1)S(1)} %copy-done.3, bf16[2,256,128]{2,1,0:T(8,128)(2,1)S(1)} %copy-done.4, bf16[2,256,128]{2,1,0:T(8,128)(2,1)S(1)} %collective-permute-done.1.k_near.refs_5_, ...), custom_call_target="tpu_custom_call" | custom-call | flops 880000000 | bytes 2400000 | tf_op jit(solution)/shard_map/pallas_call | solution.py:333
  10.2 0.2 collective-permute-done.6.refs_10_.v_two
  10.4 0.2 collective-permute-done.5.refs_9_.k_two
  10.6 0.7 %shard_map.126 = (f32[72,128]{1,0:T(8,128)S(1)}, f32[72,128]{1,0:T(8,128)S(1)}) custom-call(bf16[80,128]{1,0:T(8,128)(2,1)S(1)} %get-tuple-element.60.refs_0_, bf16[80,128]{1,0:T(8,128)(2,1)S(1)} %collective-permute-done.4.refs_1_, s32[8,128]{1,0:T(8,128)S(1)} %get-tuple-element.42._.refs_2_.info_ref, bf16[2,256,128]{2,1,0:T(8,128)(2,1)S(1)} %copy-done.3, ...), custom_call_target="tpu_custom_call" | custom-call | flops 770000000 | bytes 2100000 | tf_op jit(solution)/shard_map/pallas_call | solution.py:333
  11.3 1.5 %collective-permute-start.7 = (f32[72,128]{1,0:T(8,128)S(1)}, f32[72,128]{1,0:T(8,128)S(1)}, u32[]{:S(2)}, u32[]{:S(2)}) collective-permute-start(f32[72,128]{1,0:T(8,128)S(1)} %get-tuple-element.76), channel_id=1, source_target_pairs={{0,9},{1,8},{8,1},{9,0},{16,25},{17,24},{24,17},{25,16},{2,11},{3,... | collective-permute-start | bytes 110600 | tf_op jit(solution)/shard_map/ppermute | solution.py:376
  12.7 12.8 %shard_map.127 = (bf16[2,256,1024]{2,1,0:T(8,128)(2,1)S(1)}, bf16[2,256,1024]{2,1,0:T(8,128)(2,1)}) custom-call(s32[8,128]{1,0:T(8,128)S(1)} %get-tuple-element.42._.refs_2_.info_ref, bf16[2,256,1024]{2,1,0:T(8,128)(2,1)S(1)} %copy-done.2, bf16[2,256,128]{2,1,0:T(8,128)(2,1)S(1)} %collective-permute-done.refs_7_.k_one, ...), custom_call_target="tpu_custom_call" | custom-call | flops 3080000000 | bytes 8400000 | tf_op jit(solution)/shard_map/pallas_call | solution.py:333
  25.5 0.0 collective-permute-done.7.other_part
  25.5 0.8 %shard_map.128 = (bf16[4,2,2048]{2,1,0:T(2,128)(2,1)}, bf16[2,256,1024]{2,1,0:T(8,128)(2,1)}) custom-call(bf16[2,256,1024]{2,1,0:T(8,128)(2,1)S(1)} %get-tuple-element.72.pre, f32[2,64,128]{2,1,0:T(8,128)S(1)} %get-tuple-element.73.cache_sum, f32[2,64,128]{2,1,0:T(8,128)S(1)} %get-tuple-element.74.cache_top, ...), custom_call_target="tpu_custom_call", output_to_operand_aliasing={{1}: (6, {})} | custom-call | flops 770000000 | bytes 2100000 | tf_op jit(solution)/shard_map/pallas_call | solution.py:333
  (21 shorter events, 0.0 us)
Async XLA Ops:
  0.6 2.2 %copy-start.3 = (bf16[2,256,128]{2,1,0:T(8,128)(2,1)S(1)}, bf16[2,256,128]{2,1,0:T(8,128)(2,1)}, u32[]{:S(2)}) copy-start(bf16[2,256,128]{2,1,0:T(8,128)(2,1)} %refs_3_.1) | copy-start | bytes 393220
  0.6 2.2 %copy-start.4 = (bf16[2,256,128]{2,1,0:T(8,128)(2,1)S(1)}, bf16[2,256,128]{2,1,0:T(8,128)(2,1)}, u32[]{:S(2)}) copy-start(bf16[2,256,128]{2,1,0:T(8,128)(2,1)} %refs_4_.1) | copy-start | bytes 393220
  0.7 2.7 %copy-start.9 = (s32[2]{0:T(128)S(1)}, s32[2]{0:T(128)}, u32[]{:S(2)}) copy-start(s32[2]{0:T(128)} %plen.1) | copy-start | bytes 28
  0.7 2.7 %copy-start.7 = (bf16[4,2,256]{2,1,0:T(2,128)(2,1)S(1)}, bf16[4,2,256]{2,1,0:T(2,128)(2,1)}, u32[]{:S(2)}) copy-start(bf16[4,2,256]{2,1,0:T(2,128)(2,1)} %nv.1) | copy-start | bytes 12292
  0.7 2.7 %copy-start.6 = (bf16[4,2,256]{2,1,0:T(2,128)(2,1)S(1)}, bf16[4,2,256]{2,1,0:T(2,128)(2,1)}, u32[]{:S(2)}) copy-start(bf16[4,2,256]{2,1,0:T(2,128)(2,1)} %nk.1) | copy-start | bytes 12292
  0.7 2.7 %copy-start.5 = (bf16[4,2,2048]{2,1,0:T(2,128)(2,1)S(1)}, bf16[4,2,2048]{2,1,0:T(2,128)(2,1)}, u32[]{:S(2)}) copy-start(bf16[4,2,2048]{2,1,0:T(2,128)(2,1)} %dq.1) | copy-start | bytes 98308
  0.7 2.7 %copy-start.1 = (bf16[2,1024,256]{2,1,0:T(8,128)(2,1)S(1)}, bf16[2,1024,256]{2,1,0:T(8,128)(2,1)}, u32[]{:S(2)}) copy-start(bf16[2,1024,256]{2,1,0:T(8,128)(2,1)} %cv_ref.1) | copy-start | bytes 3145732
  0.7 2.7 %copy-start = (bf16[2,1024,256]{2,1,0:T(8,128)(2,1)S(1)}, bf16[2,1024,256]{2,1,0:T(8,128)(2,1)}, u32[]{:S(2)}) copy-start(bf16[2,1024,256]{2,1,0:T(8,128)(2,1)} %ck_ref.1) | copy-start | bytes 3145732
  0.7 2.7 %copy-start.10 = (s32[2]{0:T(128)S(1)}, s32[2]{0:T(128)}, u32[]{:S(2)}) copy-start(s32[2]{0:T(128)} %clen.1) | copy-start | bytes 28
  0.7 2.7 %copy-start.8 = (s32[2]{0:T(128)S(1)}, s32[2]{0:T(128)}, u32[]{:S(2)}) copy-start(s32[2]{0:T(128)} %asg.1) | copy-start | bytes 28
  0.7 6.7 %collective-permute-start = (bf16[2,256,128]{2,1,0:T(8,128)(2,1)}, bf16[2,256,128]{2,1,0:T(8,128)(2,1)S(1)}, u32[]{:S(2)}, u32[]{:S(2)}) collective-permute-start(bf16[2,256,128]{2,1,0:T(8,128)(2,1)} %refs_3_.1), channel_id=1, source_target_pairs={{0,16},{8,24},{16,0},{24,8},{1,17},{9,25},{17,1},{25,9},{2,18},{10... | collective-permute-start | bytes 393224 | tf_op jit(solution)/shard_map/ppermute | solution.py:372
  1.3 7.7 %collective-permute-start.3 = (bf16[2,256,128]{2,1,0:T(8,128)(2,1)}, bf16[2,256,128]{2,1,0:T(8,128)(2,1)S(1)}, u32[]{:S(2)}, u32[]{:S(2)}) collective-permute-start(bf16[2,256,128]{2,1,0:T(8,128)(2,1)} %refs_4_.1), channel_id=1, source_target_pairs={{0,16},{8,24},{16,0},{24,8},{1,17},{9,25},{17,1},{25,9},{2,18},{10... | collective-permute-start | bytes 393224 | tf_op jit(solution)/shard_map/ppermute | solution.py:372
  2.8 3.3 %copy-start.2 = (bf16[2,256,1024]{2,1,0:T(8,128)(2,1)S(1)}, bf16[2,256,1024]{2,1,0:T(8,128)(2,1)}, u32[]{:S(2)}) copy-start(bf16[2,256,1024]{2,1,0:T(8,128)(2,1)} %q_ref.5) | copy-start | bytes 3145732
  2.8 3.3 %collective-permute-start.1 = (bf16[2,256,128]{2,1,0:T(8,128)(2,1)S(1)}, bf16[2,256,128]{2,1,0:T(8,128)(2,1)S(1)}, u32[]{:S(2)}, u32[]{:S(2)}) collective-permute-start(bf16[2,256,128]{2,1,0:T(8,128)(2,1)S(1)} %copy-done.3), channel_id=1, source_target_pairs={{0,8},{8,0},{16,24},{24,16},{1,9},{9,1},{17,25},{25,17},{2,10},{10... | collective-permute-start | bytes 393224 | tf_op jit(solution)/shard_map/ppermute | solution.py:369
  2.9 3.3 %collective-permute-start.2 = (bf16[2,256,128]{2,1,0:T(8,128)(2,1)S(1)}, bf16[2,256,128]{2,1,0:T(8,128)(2,1)S(1)}, u32[]{:S(2)}, u32[]{:S(2)}) collective-permute-start(bf16[2,256,128]{2,1,0:T(8,128)(2,1)S(1)} %copy-done.4), channel_id=1, source_target_pairs={{0,8},{8,0},{16,24},{24,16},{1,9},{9,1},{17,25},{25,17},{2,10},{10... | collective-permute-start | bytes 393224 | tf_op jit(solution)/shard_map/ppermute | solution.py:369
  4.9 3.3 %collective-permute-start.4 = (bf16[80,128]{1,0:T(8,128)(2,1)S(1)}, bf16[80,128]{1,0:T(8,128)(2,1)S(1)}, u32[]{:S(2)}, u32[]{:S(2)}) collective-permute-start(bf16[80,128]{1,0:T(8,128)(2,1)S(1)} %get-tuple-element.52), channel_id=1, source_target_pairs={{0,9},{1,8},{8,1},{9,0},{16,25},{17,24},{24,17},{25,16},{2,11},{3,... | collective-permute-start | bytes 61448 | tf_op jit(solution)/shard_map/ppermute | solution.py:376
  9.1 1.3 %collective-permute-start.6 = (bf16[2,256,128]{2,1,0:T(8,128)(2,1)S(1)}, bf16[2,256,128]{2,1,0:T(8,128)(2,1)S(1)}, u32[]{:S(2)}, u32[]{:S(2)}) collective-permute-start(bf16[2,256,128]{2,1,0:T(8,128)(2,1)S(1)} %collective-permute-done.3.refs_8_.v_one), channel_id=1, source_target_pairs={{0,8},{8,0},{16,24},{24,16},{1,9},{9,1},{17,25},{25,17},{2,10},{10... | collective-permute-start | bytes 393224 | tf_op jit(solution)/shard_map/ppermute | solution.py:369
  9.1 1.5 %collective-permute-start.5 = (bf16[2,256,128]{2,1,0:T(8,128)(2,1)S(1)}, bf16[2,256,128]{2,1,0:T(8,128)(2,1)S(1)}, u32[]{:S(2)}, u32[]{:S(2)}) collective-permute-start(bf16[2,256,128]{2,1,0:T(8,128)(2,1)S(1)} %collective-permute-done.refs_7_.k_one), channel_id=1, source_target_pairs={{0,8},{8,0},{16,24},{24,16},{1,9},{9,1},{17,25},{25,17},{2,10},{10... | collective-permute-start | bytes 393224 | tf_op jit(solution)/shard_map/ppermute | solution.py:369
  11.3 14.3 %collective-permute-start.7 = (f32[72,128]{1,0:T(8,128)S(1)}, f32[72,128]{1,0:T(8,128)S(1)}, u32[]{:S(2)}, u32[]{:S(2)}) collective-permute-start(f32[72,128]{1,0:T(8,128)S(1)} %get-tuple-element.76), channel_id=1, source_target_pairs={{0,9},{1,8},{8,1},{9,0},{16,25},{17,24},{24,17},{25,16},{2,11},{3,... | collective-permute-start | bytes 110600 | tf_op jit(solution)/shard_map/ppermute | solution.py:376

commit v7 on v6

--- a/solution.py
+++ b/solution.py
@@ -61,9 +61,13 @@
 
 
 def own_kernel(
-    asg, plen, clen, dq, nk, nv, ck_ref, cv_ref, _,
-    own_ref, other_ref, info_ref, sum_ref, top_ref, tot_ref, flat, fk, fv,
+    asg_hbm, plen_hbm, clen_hbm, dq_hbm, nk_hbm, nv_hbm, ck_ref, cv_ref, _,
+    own_ref, other_ref, info_ref, sum_ref, top_ref, tot_ref, asg, plen, clen, dq, nk, nv, flat, fk, fv, sems,
 ):
+    moves = [(dq_hbm, dq), (nk_hbm, nk), (nv_hbm, nv), (asg_hbm, asg), (plen_hbm, plen), (clen_hbm, clen)]
+    copies = [pltpu.make_async_copy(a, b, sems.at[i]) for i, (a, b) in enumerate(moves)]
+    for copy in copies:
+        copy.start()
     role = lax.axis_index("role")
     steps, rows, columns = dq.shape
     span = steps * rows
@@ -73,6 +77,8 @@
     slots = ck_ref.shape[1]
     fk[...] = jnp.zeros_like(fk)
     fv[...] = jnp.zeros_like(fv)
+    for copy in copies:
+        copy.wait()
     for step in range(steps):
         at = slice(step * rows, (step + 1) * rows)
         flat[at, :] = dq[step].astype(jnp.float32)
@@ -322,7 +328,6 @@
 
 VMEM = pl.BlockSpec(memory_space=pltpu.VMEM)
 ANY = pl.BlockSpec(memory_space=pl.ANY)
-SMEM = pl.BlockSpec(memory_space=pltpu.SMEM)
 
 
 def in_hbm(x):
@@ -385,14 +390,22 @@
     state = shape((2, queries, 128), f32)
     own_msg, other_msg, info, *cache = call(
         own_kernel,
-        [assignment, prompt_len, cache_len, decode_queries, new_keys, new_values, cache_keys, cache_values, first],
+        [in_hbm(x) for x in (assignment, prompt_len, cache_len, decode_queries, new_keys, new_values)]
+        + [cache_keys, cache_values, first],
         [message] * 2 + [shape((span, 128), i32)] + [state] * 3,
         [
+            pltpu.SMEM(assignment.shape, i32),
+            pltpu.SMEM(prompt_len.shape, i32),
+            pltpu.SMEM(cache_len.shape, i32),
+            pltpu.VMEM(decode_queries.shape, bf16),
+            pltpu.VMEM(new_keys.shape, bf16),
+            pltpu.VMEM(new_values.shape, bf16),
             pltpu.VMEM((span, dec_columns), f32),
             pltpu.VMEM((128, 2 * D_HEAD), f32),
             pltpu.VMEM((128, 2 * D_HEAD), f32),
+            pltpu.SemaphoreType.DMA((6,)),
         ],
-        specs=[SMEM] * 3 + [VMEM] * 5 + [ANY],
+        specs=[ANY] * 6 + [VMEM] * 2 + [ANY],
         us=1.3,
     )
     partner_msg = partner(other_msg)
@@ -411,10 +424,10 @@
         )
 
     states = local(blocks[:-1], runs[:-1], info)
+    far_values, partner_msg, states = after((far_values, partner_msg, states))
+    far_near_values = [near(v) for v in far_values]
     far_keys, states = after((far_keys, states))
     far_near_keys = [near(k) for k in far_keys]
-    far_values, partner_msg, states = after((far_values, partner_msg, states))
-    far_near_values = [near(v) for v in far_values]
     states = [*states, *local(blocks[-1:], runs[-1:], states[0])]
     far = list(zip(far_keys, far_values, far_near_keys, far_near_values))
     chunks = [prefill_keys, prefill_values, near_keys, near_values] + sum([list(four) for four in far], [])

time: 26.5 us -> 26.5 us (level)
  Pallas kernels: 17.7 us -> 18 us
    pallas_call x7, Pallas kernels: 17.7 us -> 18 us  [call(): pl.pallas_call(kernel, out_shape=outs, in_specs=specs or [VMEM] * len(arg...]
  transfers between devices with their start and end apart: 8 -> 8, of which waited for: 4 -> 4; matrix products, arithmetic and copies ran while one was open for 0% -> 0% of each run, Pallas kernels for 62% -> 63%
where the time goes in v7:
time: 26.5 us; the launch traced here: 26.3 us
  Pallas kernels  18 us (68%)
  starting transfers between devices  5.82 us (22%)
  waiting for transfers between devices  1.73 us (7%)
  between operations  0.73 us (3%)
    pallas_call x7, Pallas kernels, call(): pl.pallas_call(kernel, out_shape=outs, in_specs=specs or [VMEM] * len(arg...  18 us
    ppermute x2, starting transfers between devices, partner(): return lax.ppermute(x, ('seq', 'role'), moves)  2.72 us
    ppermute x2, starting transfers between devices, around(): lax.ppermute(x, 'seq', [(i, (i + 2 * shift) % seqs) for i in range(seqs)])  2.09 us
    ppermute x4, starting transfers between devices, near(): return lax.ppermute(x, 'seq', [(i, i ^ 1) for i in range(seqs)])  1.01 us
    ppermute x2, waiting for transfers between devices, partner(): return lax.ppermute(x, ('seq', 'role'), moves)  0.74 us
    ppermute x2, waiting for transfers between devices, around(): lax.ppermute(x, 'seq', [(i, (i + 2 * shift) % seqs) for i in range(seqs)])  0.64 us
  transfers between devices with their start and end apart: 8, of which 4 were waited for; matrix products, arithmetic and copies ran while one was open for 0% of the time, Pallas kernels for 63%

profile of v7, /device:TPU:28, one launch (start us, length us, event | category | flops | bytes accessed | tf_op | source)
XLA Modules:
  0.0 26.3 jit_solution(8702453346754033242)
XLA Ops:
  0.6 0.0 copy-start.3
  0.7 0.6 %collective-permute-start = (bf16[2,256,128]{2,1,0:T(8,128)(2,1)}, bf16[2,256,128]{2,1,0:T(8,128)(2,1)S(1)}, u32[]{:S(2)}, u32[]{:S(2)}) collective-permute-start(bf16[2,256,128]{2,1,0:T(8,128)(2,1)} %refs_3_.1), channel_id=1, source_target_pairs={{0,16},{8,24},{16,0},{24,8},{1,17},{9,25},{17,1},{25,9},{2,18},{10... | collective-permute-start | bytes 393224 | tf_op jit(solution)/shard_map/ppermute | solution.py:377
  1.2 1.5 %collective-permute-start.1 = (bf16[2,256,128]{2,1,0:T(8,128)(2,1)}, bf16[2,256,128]{2,1,0:T(8,128)(2,1)S(1)}, u32[]{:S(2)}, u32[]{:S(2)}) collective-permute-start(bf16[2,256,128]{2,1,0:T(8,128)(2,1)} %refs_4_.1), channel_id=1, source_target_pairs={{0,16},{8,24},{16,0},{24,8},{1,17},{9,25},{17,1},{25,9},{2,18},{10... | collective-permute-start | bytes 393224 | tf_op jit(solution)/shard_map/ppermute | solution.py:377
  2.8 0.0 collective-permute-start.3
  2.8 0.5 %collective-permute-start.4 = (bf16[2,256,128]{2,1,0:T(8,128)(2,1)S(1)}, bf16[2,256,128]{2,1,0:T(8,128)(2,1)S(1)}, u32[]{:S(2)}, u32[]{:S(2)}) collective-permute-start(bf16[2,256,128]{2,1,0:T(8,128)(2,1)S(1)} %copy-done.4), channel_id=1, source_target_pairs={{0,8},{8,0},{16,24},{24,16},{1,9},{9,1},{17,25},{25,17},{2,10},{10... | collective-permute-start | bytes 393224 | tf_op jit(solution)/shard_map/ppermute | solution.py:374
  3.3 1.8 %shard_map.123 = (bf16[80,128]{1,0:T(8,128)(2,1)S(1)}, bf16[80,128]{1,0:T(8,128)(2,1)S(1)}, s32[8,128]{1,0:T(8,128)S(1)}, f32[2,64,128]{2,1,0:T(8,128)S(1)}, f32...) custom-call(s32[2]{0:T(128)} %asg_hbm.1, s32[2]{0:T(128)} %plen_hbm.1, s32[2]{0:T(128)} %clen_hbm.1, ...), custom_call_target="tpu_custom_call" | custom-call | flops 1430000000 | bytes 3900000 | tf_op jit(solution)/shard_map/pallas_call | solution.py:338
  5.1 1.2 %collective-permute-start.2 = (bf16[80,128]{1,0:T(8,128)(2,1)S(1)}, bf16[80,128]{1,0:T(8,128)(2,1)S(1)}, u32[]{:S(2)}, u32[]{:S(2)}) collective-permute-start(bf16[80,128]{1,0:T(8,128)(2,1)S(1)} %get-tuple-element.43), channel_id=1, source_target_pairs={{0,9},{1,8},{8,1},{9,0},{16,25},{17,24},{24,17},{25,16},{2,11},{3,... | collective-permute-start | bytes 61448 | tf_op jit(solution)/shard_map/ppermute | solution.py:381
  6.3 0.0 collective-permute-done.3.k_near.refs_5_
  6.3 0.0 collective-permute-done.4.v_near.refs_6_
  6.3 0.0 copy-done.2
  6.3 1.3 %shard_map.124 = (f32[256,1024]{1,0:T(8,128)S(1)}, f32[256,1024]{1,0:T(8,128)S(1)}, f32[256,1024]{1,0:T(8,128)S(1)}, f32[256,512]{1,0:T(8,128)S(1)}, f32[256,512]{1,0:T(8,128)S(1)}, /*index=5*/f32[256,512]{1,0:T(8,128)S(1)}) custom-call(bf16[2,256,1024]{2,1,0:T(8,128)(2,1)S(1)} %copy-done.2, bf16[2,256,128]{2,1,0:T(8,128)(2,1)S(1)} %copy-done.3, ...), custom_call_target="tpu_custom_call" | custom-call | flops 2640000000 | bytes 7200000 | tf_op jit(solution)/shard_map/pallas_call | solution.py:338
  7.6 0.7 %collective-permute-done.2.refs_1_ = bf16[80,128]{1,0:T(8,128)(2,1)S(1)} collective-permute-done((bf16[80,128]{1,0:T(8,128)(2,1)S(1)}, bf16[80,128]{1,0:T(8,128)(2,1)S(1)}, u32[]{:S(2)}, u32[]{:S(2)}) %collective-permute-start.2) | collective-permute-done | bytes 20512 | tf_op jit(solution)/shard_map/ppermute | solution.py:381
  8.4 0.6 %collective-permute-done.1.refs_8_.v_one = bf16[2,256,128]{2,1,0:T(8,128)(2,1)S(1)} collective-permute-done((bf16[2,256,128]{2,1,0:T(8,128)(2,1)}, bf16[2,256,128]{2,1,0:T(8,128)(2,1)S(1)}, u32[]{:S(2)}, u32[]{:S(2)}) %collective-permute-start.1) | collective-permute-done | bytes 131104 | tf_op jit(solution)/shard_map/ppermute | solution.py:377
  9.0 0.0 collective-permute-done.refs_7_.k_one
  9.0 0.2 collective-permute-start.5
  9.2 0.4 %collective-permute-start.6 = (bf16[2,256,128]{2,1,0:T(8,128)(2,1)S(1)}, bf16[2,256,128]{2,1,0:T(8,128)(2,1)S(1)}, u32[]{:S(2)}, u32[]{:S(2)}) collective-permute-start(bf16[2,256,128]{2,1,0:T(8,128)(2,1)S(1)} %collective-permute-done.1.refs_8_.v_one), channel_id=1, source_target_pairs={{0,8},{8,0},{16,24},{24,16},{1,9},{9,1},{17,25},{25,17},{2,10},{10... | collective-permute-start | bytes 393224 | tf_op jit(solution)/shard_map/ppermute | solution.py:374
  9.5 0.7 %shard_map.125 = (f32[256,512]{1,0:T(8,128)S(1)}, f32[256,512]{1,0:T(8,128)S(1)}, f32[256,512]{1,0:T(8,128)S(1)}) custom-call(bf16[2,256,1024]{2,1,0:T(8,128)(2,1)S(1)} %copy-done.2, bf16[2,256,128]{2,1,0:T(8,128)(2,1)S(1)} %copy-done.3, bf16[2,256,128]{2,1,0:T(8,128)(2,1)S(1)} %copy-done.4, bf16[2,256,128]{2,1,0:T(8,128)(2,1)S(1)} %collective-permute-done.3.k_near.refs_5_, ...), custom_call_target="tpu_custom_call" | custom-call | flops 880000000 | bytes 2400000 | tf_op jit(solution)/shard_map/pallas_call | solution.py:338
  10.2 0.2 collective-permute-done.5.refs_9_.k_two
  10.3 0.2 collective-permute-done.6.refs_10_.v_two
  10.5 0.7 %shard_map.126 = (f32[72,128]{1,0:T(8,128)S(1)}, f32[72,128]{1,0:T(8,128)S(1)}) custom-call(bf16[80,128]{1,0:T(8,128)(2,1)S(1)} %get-tuple-element.60.refs_0_, bf16[80,128]{1,0:T(8,128)(2,1)S(1)} %collective-permute-done.2.refs_1_, s32[8,128]{1,0:T(8,128)S(1)} %get-tuple-element.42._.refs_2_.info_ref, bf16[2,256,128]{2,1,0:T(8,128)(2,1)S(1)} %copy-done.3, ...), custom_call_target="tpu_custom_call" | custom-call | flops 770000000 | bytes 2100000 | tf_op jit(solution)/shard_map/pallas_call | solution.py:338
  11.2 1.5 %collective-permute-start.7 = (f32[72,128]{1,0:T(8,128)S(1)}, f32[72,128]{1,0:T(8,128)S(1)}, u32[]{:S(2)}, u32[]{:S(2)}) collective-permute-start(f32[72,128]{1,0:T(8,128)S(1)} %get-tuple-element.76), channel_id=1, source_target_pairs={{0,9},{1,8},{8,1},{9,0},{16,25},{17,24},{24,17},{25,16},{2,11},{3,... | collective-permute-start | bytes 110600 | tf_op jit(solution)/shard_map/ppermute | solution.py:381
  12.7 12.8 %shard_map.127 = (bf16[2,256,1024]{2,1,0:T(8,128)(2,1)S(1)}, bf16[2,256,1024]{2,1,0:T(8,128)(2,1)}) custom-call(s32[8,128]{1,0:T(8,128)S(1)} %get-tuple-element.42._.refs_2_.info_ref, bf16[2,256,1024]{2,1,0:T(8,128)(2,1)S(1)} %copy-done.2, bf16[2,256,128]{2,1,0:T(8,128)(2,1)S(1)} %collective-permute-done.refs_7_.k_one, ...), custom_call_target="tpu_custom_call" | custom-call | flops 3080000000 | bytes 8400000 | tf_op jit(solution)/shard_map/pallas_call | solution.py:338
  25.5 0.0 collective-permute-done.7.other_part
  25.5 0.8 %shard_map.128 = (bf16[4,2,2048]{2,1,0:T(2,128)(2,1)}, bf16[2,256,1024]{2,1,0:T(8,128)(2,1)}) custom-call(bf16[2,256,1024]{2,1,0:T(8,128)(2,1)S(1)} %get-tuple-element.72.pre, f32[2,64,128]{2,1,0:T(8,128)S(1)} %get-tuple-element.73.cache_sum, f32[2,64,128]{2,1,0:T(8,128)S(1)} %get-tuple-element.74.cache_top, ...), custom_call_target="tpu_custom_call", output_to_operand_aliasing={{1}: (6, {})} | custom-call | flops 770000000 | bytes 2100000 | tf_op jit(solution)/shard_map/pallas_call | solution.py:338
  (9 shorter events, 0.0 us)
Async XLA Ops:
  0.6 2.1 %copy-start.3 = (bf16[2,256,128]{2,1,0:T(8,128)(2,1)S(1)}, bf16[2,256,128]{2,1,0:T(8,128)(2,1)}, u32[]{:S(2)}) copy-start(bf16[2,256,128]{2,1,0:T(8,128)(2,1)} %refs_3_.1) | copy-start | bytes 393220
  0.6 2.1 %copy-start.4 = (bf16[2,256,128]{2,1,0:T(8,128)(2,1)S(1)}, bf16[2,256,128]{2,1,0:T(8,128)(2,1)}, u32[]{:S(2)}) copy-start(bf16[2,256,128]{2,1,0:T(8,128)(2,1)} %refs_4_.1) | copy-start | bytes 393220
  0.7 2.6 %copy-start.1 = (bf16[2,1024,256]{2,1,0:T(8,128)(2,1)S(1)}, bf16[2,1024,256]{2,1,0:T(8,128)(2,1)}, u32[]{:S(2)}) copy-start(bf16[2,1024,256]{2,1,0:T(8,128)(2,1)} %cv_ref.1) | copy-start | bytes 3145732
  0.7 2.6 %copy-start = (bf16[2,1024,256]{2,1,0:T(8,128)(2,1)S(1)}, bf16[2,1024,256]{2,1,0:T(8,128)(2,1)}, u32[]{:S(2)}) copy-start(bf16[2,1024,256]{2,1,0:T(8,128)(2,1)} %ck_ref.1) | copy-start | bytes 3145732
  0.7 8.3 %collective-permute-start = (bf16[2,256,128]{2,1,0:T(8,128)(2,1)}, bf16[2,256,128]{2,1,0:T(8,128)(2,1)S(1)}, u32[]{:S(2)}, u32[]{:S(2)}) collective-permute-start(bf16[2,256,128]{2,1,0:T(8,128)(2,1)} %refs_3_.1), channel_id=1, source_target_pairs={{0,16},{8,24},{16,0},{24,8},{1,17},{9,25},{17,1},{25,9},{2,18},{10... | collective-permute-start | bytes 393224 | tf_op jit(solution)/shard_map/ppermute | solution.py:377
  1.2 7.7 %collective-permute-start.1 = (bf16[2,256,128]{2,1,0:T(8,128)(2,1)}, bf16[2,256,128]{2,1,0:T(8,128)(2,1)S(1)}, u32[]{:S(2)}, u32[]{:S(2)}) collective-permute-start(bf16[2,256,128]{2,1,0:T(8,128)(2,1)} %refs_4_.1), channel_id=1, source_target_pairs={{0,16},{8,24},{16,0},{24,8},{1,17},{9,25},{17,1},{25,9},{2,18},{10... | collective-permute-start | bytes 393224 | tf_op jit(solution)/shard_map/ppermute | solution.py:377
  2.8 3.6 %copy-start.2 = (bf16[2,256,1024]{2,1,0:T(8,128)(2,1)S(1)}, bf16[2,256,1024]{2,1,0:T(8,128)(2,1)}, u32[]{:S(2)}) copy-start(bf16[2,256,1024]{2,1,0:T(8,128)(2,1)} %q_ref.5) | copy-start | bytes 3145732
  2.8 3.5 %collective-permute-start.3 = (bf16[2,256,128]{2,1,0:T(8,128)(2,1)S(1)}, bf16[2,256,128]{2,1,0:T(8,128)(2,1)S(1)}, u32[]{:S(2)}, u32[]{:S(2)}) collective-permute-start(bf16[2,256,128]{2,1,0:T(8,128)(2,1)S(1)} %copy-done.3), channel_id=1, source_target_pairs={{0,8},{8,0},{16,24},{24,16},{1,9},{9,1},{17,25},{25,17},{2,10},{10... | collective-permute-start | bytes 393224 | tf_op jit(solution)/shard_map/ppermute | solution.py:374
  2.8 3.5 %collective-permute-start.4 = (bf16[2,256,128]{2,1,0:T(8,128)(2,1)S(1)}, bf16[2,256,128]{2,1,0:T(8,128)(2,1)S(1)}, u32[]{:S(2)}, u32[]{:S(2)}) collective-permute-start(bf16[2,256,128]{2,1,0:T(8,128)(2,1)S(1)} %copy-done.4), channel_id=1, source_target_pairs={{0,8},{8,0},{16,24},{24,16},{1,9},{9,1},{17,25},{25,17},{2,10},{10... | collective-permute-start | bytes 393224 | tf_op jit(solution)/shard_map/ppermute | solution.py:374
  5.1 3.3 %collective-permute-start.2 = (bf16[80,128]{1,0:T(8,128)(2,1)S(1)}, bf16[80,128]{1,0:T(8,128)(2,1)S(1)}, u32[]{:S(2)}, u32[]{:S(2)}) collective-permute-start(bf16[80,128]{1,0:T(8,128)(2,1)S(1)} %get-tuple-element.43), channel_id=1, source_target_pairs={{0,9},{1,8},{8,1},{9,0},{16,25},{17,24},{24,17},{25,16},{2,11},{3,... | collective-permute-start | bytes 61448 | tf_op jit(solution)/shard_map/ppermute | solution.py:381
  9.0 1.3 %collective-permute-start.5 = (bf16[2,256,128]{2,1,0:T(8,128)(2,1)S(1)}, bf16[2,256,128]{2,1,0:T(8,128)(2,1)S(1)}, u32[]{:S(2)}, u32[]{:S(2)}) collective-permute-start(bf16[2,256,128]{2,1,0:T(8,128)(2,1)S(1)} %collective-permute-done.refs_7_.k_one), channel_id=1, source_target_pairs={{0,8},{8,0},{16,24},{24,16},{1,9},{9,1},{17,25},{25,17},{2,10},{10... | collective-permute-start | bytes 393224 | tf_op jit(solution)/shard_map/ppermute | solution.py:374
  9.2 1.4 %collective-permute-start.6 = (bf16[2,256,128]{2,1,0:T(8,128)(2,1)S(1)}, bf16[2,256,128]{2,1,0:T(8,128)(2,1)S(1)}, u32[]{:S(2)}, u32[]{:S(2)}) collective-permute-start(bf16[2,256,128]{2,1,0:T(8,128)(2,1)S(1)} %collective-permute-done.1.refs_8_.v_one), channel_id=1, source_target_pairs={{0,8},{8,0},{16,24},{24,16},{1,9},{9,1},{17,25},{25,17},{2,10},{10... | collective-permute-start | bytes 393224 | tf_op jit(solution)/shard_map/ppermute | solution.py:374
  11.2 14.3 %collective-permute-start.7 = (f32[72,128]{1,0:T(8,128)S(1)}, f32[72,128]{1,0:T(8,128)S(1)}, u32[]{:S(2)}, u32[]{:S(2)}) collective-permute-start(f32[72,128]{1,0:T(8,128)S(1)} %get-tuple-element.76), channel_id=1, source_target_pairs={{0,9},{1,8},{8,1},{9,0},{16,25},{17,24},{24,17},{25,16},{2,11},{3,... | collective-permute-start | bytes 110600 | tf_op jit(solution)/shard_map/ppermute | solution.py:381

commit v8 on v7

--- a/solution.py
+++ b/solution.py
@@ -37,6 +37,18 @@
 def row_to_column(row, rows):
     spread = jnp.where(eye_of(rows), jnp.broadcast_to(row, (rows, 128)), 0.0)
     return jnp.sum(spread, axis=1, keepdims=True)
+
+
+def terms_of(x):
+    terms = []
+    for _ in range(3):
+        terms.append(x.astype(jnp.bfloat16).astype(jnp.float32))
+        x = x - terms[-1]
+    return terms
+
+
+def sum_of_terms(block, first):
+    return block[first : first + 1] + block[first + 1 : first + 2] + block[first + 2 : first + 3]
 
 
 def select_rows(index, parts):
@@ -154,10 +166,10 @@
             summed = summed + weighted(jnp.where(prompt == r, weights, 0.0), chunk_refs[2 * index + 1][r])
     for index, out in enumerate(outs):
         rows = slice(index * queries, (index + 1) * queries)
-        out[:queries, :] = summed[rows]
-        out[queries : queries + 8, :] = jnp.concatenate(
-            [column_to_row(top[rows]), column_to_row(total[rows]), jnp.zeros((6, 128), jnp.float32)], axis=0
-        )
+        stats = terms_of(column_to_row(top[rows])) + terms_of(column_to_row(total[rows]))
+        stats = jnp.concatenate(stats + [jnp.zeros((16 - len(stats), 128), jnp.float32)], axis=0)
+        out[:queries, :] = summed[rows].astype(out.dtype)
+        out[queries : queries + 16, :] = stats.astype(out.dtype)
 
 
 def local_kernel(blocks, q_ref, k_own, v_own, k_near, v_near, _, *refs):
@@ -196,24 +208,15 @@
         run(True)
 
 
-def merge_rows(span, cache, own_part, other_part, dec, flat):
-    steps, rows, columns = dec.shape
-    half = columns // 2
-    group = half // D_HEAD
+def merged(span, group, cache_sum, cache_top, cache_tot, part):
     queries = group * span
-    role = lax.axis_index("role")
-    for index, (part, kv) in enumerate(((own_part, role), (other_part, 1 - role))):
-        top = row_to_column(part[queries : queries + 1, :], queries)
-        total = row_to_column(part[queries + 1 : queries + 2, :], queries)
-        cache_sum, cache_top, cache_tot = (ref[index] for ref in cache)
-        high = jnp.maximum(top, cache_top)
-        one, two = jnp.exp2(cache_top - high), jnp.exp2(top - high)
-        result = (one * cache_sum + two * part[:queries, :]) / (one * cache_tot + two * total)
-        for head in range(group):
-            start = pl.multiple_of(kv * half + head * D_HEAD, D_HEAD)
-            flat[:, pl.ds(start, D_HEAD)] = result[head * span : (head + 1) * span]
-    for step in range(steps):
-        dec[step] = flat[step * rows : (step + 1) * rows, :].astype(jnp.bfloat16)
+    stats = part[queries : queries + 16, :].astype(jnp.float32)
+    top = row_to_column(sum_of_terms(stats, 0), queries)
+    total = row_to_column(sum_of_terms(stats, 3), queries)
+    high = jnp.maximum(top, cache_top)
+    one, two = jnp.exp2(cache_top - high), jnp.exp2(top - high)
+    result = (one * cache_sum + two * part[:queries, :].astype(jnp.float32)) / (one * cache_tot + two * total)
+    return jnp.concatenate([result[head * span : (head + 1) * span] for head in range(group)], axis=1)
 
 
 def joined(q, keys):
@@ -236,10 +239,14 @@
     return summed + far[:, :D_HEAD], total + far[:, D_HEAD:]
 
 
-def far_kernel(blocks, shift, last, info_ref, q_ref, k_one, v_one, k_two, v_two, _, *refs):
+def far_kernel(blocks, shift, last, span, info_ref, q_ref, k_one, v_one, k_two, v_two, _, *refs):
     prompts, length, columns = q_ref.shape
+    group = columns // D_HEAD
     count = 3 * len(blocks)
     states, outs, (wide, sem) = refs[:count], refs[count:-2], refs[-2:]
+    if last:
+        (cache_sum, cache_top, cache_tot, own_part), outs = outs[:4], outs[4:]
+        outs[2][...] = merged(span, group, cache_sum[0], cache_top[0], cache_tot[0], own_part)
     seq = lax.axis_index("seq")
     position = seq * length + lax.broadcasted_iota(jnp.int32, (length, D_HEAD), 0)
     places = [
@@ -306,17 +313,24 @@
 
 
 def finish_kernel(
-    shift, span, pre, cache_sum, cache_top, cache_tot, own_part, other_part, _, dec_hbm, pre_hbm, dec, flat, sems
+    shift, span, pre, own_rows, cache_sum, cache_top, cache_tot, other_part, _, dec_hbm, pre_hbm, dec, flat, sems
 ):
     copy = pltpu.make_async_copy(pre.at[1:], pre_hbm.at[1:], sems.at[0])
     dec_copy = pltpu.make_async_copy(dec, dec_hbm, sems.at[1])
     late = lax.axis_index("seq") // 2 >= shift
+    role = lax.axis_index("role")
 
     @pl.when(late)
     def _():
         copy.start()
 
-    merge_rows(span, (cache_sum, cache_top, cache_tot), own_part, other_part, dec, flat)
+    steps, rows, columns = dec.shape
+    half = columns // 2
+    flat[:, pl.ds(pl.multiple_of(role * half, half), half)] = own_rows[...]
+    other = merged(span, half // D_HEAD, cache_sum[1], cache_top[1], cache_tot[1], other_part)
+    flat[:, pl.ds(pl.multiple_of((1 - role) * half, half), half)] = other
+    for step in range(steps):
+        dec[step] = flat[step * rows : (step + 1) * rows, :].astype(jnp.bfloat16)
     dec_copy.start()
 
     @pl.when(late)
@@ -431,33 +445,34 @@
     states = [*states, *local(blocks[-1:], runs[-1:], states[0])]
     far = list(zip(far_keys, far_values, far_near_keys, far_near_values))
     chunks = [prefill_keys, prefill_values, near_keys, near_values] + sum([list(four) for four in far], [])
-    part = shape((queries + 8, 128), f32)
+    parts = [shape((queries + 16, 128), f32), shape((queries + 16, 128), bf16)]
     own_part, partner_part = call(
         functools.partial(prompt_kernel, span),
         (own_msg, partner_msg, info, *chunks, states[-1]),
-        [part] * 2,
+        parts,
         specs=[VMEM] * (3 + len(chunks)) + [ANY],
         us=0.7,
     )
     other_part = partner(partner_part)
     for index, shift in enumerate(shifts):
         last = index == len(shifts) - 1
-        outs, out_specs = sum(runs, []), [VMEM] * len(states)
+        outs, out_specs, extra = sum(runs, []), [VMEM] * len(states), []
         if last:
-            outs, out_specs = [shape(prefill_queries.shape, bf16)] * 2, [VMEM, ANY]
+            outs = [shape(prefill_queries.shape, bf16)] * 2 + [shape((span, dec_columns // 2), f32)]
+            out_specs, extra = [VMEM, ANY, VMEM], [*cache, own_part]
         states = call(
-            functools.partial(far_kernel, blocks, shift, last),
-            (info, prefill_queries, *far[index], own_part, *states),
+            functools.partial(far_kernel, blocks, shift, last, span),
+            (info, prefill_queries, *far[index], own_part, *states, *extra),
             outs,
             [pltpu.VMEM((prompts, 2 * length, 2 * D_HEAD), bf16), pltpu.SemaphoreType.DMA(())],
-            specs=[VMEM] * 6 + [ANY] + [VMEM] * len(states),
+            specs=[VMEM] * 6 + [ANY] + [VMEM] * (len(states) + len(extra)),
             out_specs=out_specs,
             us=2.8,
         )
-    pre, prefill_out = states
+    pre, prefill_out, own_rows = states
     decode_out, prefill_out = call(
         functools.partial(finish_kernel, shifts[-1], span),
-        (pre, *cache, own_part, other_part, prefill_out),
+        (pre, own_rows, *cache, other_part, prefill_out),
         [shape(decode_queries.shape, bf16), shape(prefill_queries.shape, bf16)],
         [
             pltpu.VMEM(decode_queries.shape, bf16),

time: 26.5 us -> 26.6 us (level)
  no operation moved by 1% of the time
where the time goes in v8:
time: 26.6 us; the launch traced here: 26.4 us
  Pallas kernels  18.1 us (68%)
  starting transfers between devices  5.82 us (22%)
  waiting for transfers between devices  1.74 us (7%)
  between operations  0.73 us (3%)
    pallas_call x7, Pallas kernels, call(): pl.pallas_call(kernel, out_shape=outs, in_specs=specs or [VMEM] * len(arg...  18.1 us
    ppermute x2, starting transfers between devices, partner(): return lax.ppermute(x, ('seq', 'role'), moves)  2.72 us
    ppermute x2, starting transfers between devices, around(): lax.ppermute(x, 'seq', [(i, (i + 2 * shift) % seqs) for i in range(seqs)])  2.09 us
    ppermute x4, starting transfers between devices, near(): return lax.ppermute(x, 'seq', [(i, i ^ 1) for i in range(seqs)])  1.01 us
    ppermute x2, waiting for transfers between devices, partner(): return lax.ppermute(x, ('seq', 'role'), moves)  0.75 us
    ppermute x2, waiting for transfers between devices, around(): lax.ppermute(x, 'seq', [(i, (i + 2 * shift) % seqs) for i in range(seqs)])  0.64 us
  transfers between devices with their start and end apart: 8, of which 4 were waited for; matrix products, arithmetic and copies ran while one was open for 0% of the time, Pallas kernels for 63%

profile of v8, /device:TPU:28, one launch (start us, length us, event | category | flops | bytes accessed | tf_op | source)
XLA Modules:
  0.0 26.4 jit_solution(16868175902083514436)
XLA Ops:
  0.6 0.0 copy-start.3
  0.7 0.6 %collective-permute-start = (bf16[2,256,128]{2,1,0:T(8,128)(2,1)}, bf16[2,256,128]{2,1,0:T(8,128)(2,1)S(1)}, u32[]{:S(2)}, u32[]{:S(2)}) collective-permute-start(bf16[2,256,128]{2,1,0:T(8,128)(2,1)} %refs_3_.1), channel_id=1, source_target_pairs={{0,16},{8,24},{16,0},{24,8},{1,17},{9,25},{17,1},{25,9},{2,18},{10... | collective-permute-start | bytes 393224 | tf_op jit(solution)/shard_map/ppermute | solution.py:391
  1.2 1.5 %collective-permute-start.1 = (bf16[2,256,128]{2,1,0:T(8,128)(2,1)}, bf16[2,256,128]{2,1,0:T(8,128)(2,1)S(1)}, u32[]{:S(2)}, u32[]{:S(2)}) collective-permute-start(bf16[2,256,128]{2,1,0:T(8,128)(2,1)} %refs_4_.1), channel_id=1, source_target_pairs={{0,16},{8,24},{16,0},{24,8},{1,17},{9,25},{17,1},{25,9},{2,18},{10... | collective-permute-start | bytes 393224 | tf_op jit(solution)/shard_map/ppermute | solution.py:391
  2.8 0.0 collective-permute-start.3
  2.8 0.5 %collective-permute-start.4 = (bf16[2,256,128]{2,1,0:T(8,128)(2,1)S(1)}, bf16[2,256,128]{2,1,0:T(8,128)(2,1)S(1)}, u32[]{:S(2)}, u32[]{:S(2)}) collective-permute-start(bf16[2,256,128]{2,1,0:T(8,128)(2,1)S(1)} %copy-done.4), channel_id=1, source_target_pairs={{0,8},{8,0},{16,24},{24,16},{1,9},{9,1},{17,25},{25,17},{2,10},{10... | collective-permute-start | bytes 393224 | tf_op jit(solution)/shard_map/ppermute | solution.py:388
  3.3 1.8 %shard_map.123 = (bf16[80,128]{1,0:T(8,128)(2,1)S(1)}, bf16[80,128]{1,0:T(8,128)(2,1)S(1)}, s32[8,128]{1,0:T(8,128)S(1)}, f32[2,64,128]{2,1,0:T(8,128)S(1)}, f32...) custom-call(s32[2]{0:T(128)} %asg_hbm.1, s32[2]{0:T(128)} %plen_hbm.1, s32[2]{0:T(128)} %clen_hbm.1, ...), custom_call_target="tpu_custom_call" | custom-call | flops 1430000000 | bytes 3900000 | tf_op jit(solution)/shard_map/pallas_call | solution.py:352
  5.1 1.2 %collective-permute-start.2 = (bf16[80,128]{1,0:T(8,128)(2,1)S(1)}, bf16[80,128]{1,0:T(8,128)(2,1)S(1)}, u32[]{:S(2)}, u32[]{:S(2)}) collective-permute-start(bf16[80,128]{1,0:T(8,128)(2,1)S(1)} %get-tuple-element.44), channel_id=1, source_target_pairs={{0,9},{1,8},{8,1},{9,0},{16,25},{17,24},{24,17},{25,16},{2,11},{3,... | collective-permute-start | bytes 61448 | tf_op jit(solution)/shard_map/ppermute | solution.py:395
  6.3 0.0 collective-permute-done.3.k_near.refs_5_
  6.3 0.0 collective-permute-done.4.v_near.refs_6_
  6.3 0.0 copy-done.2
  6.3 1.3 %shard_map.124 = (f32[256,1024]{1,0:T(8,128)S(1)}, f32[256,1024]{1,0:T(8,128)S(1)}, f32[256,1024]{1,0:T(8,128)S(1)}, f32[256,512]{1,0:T(8,128)S(1)}, f32[256,512]{1,0:T(8,128)S(1)}, /*index=5*/f32[256,512]{1,0:T(8,128)S(1)}) custom-call(bf16[2,256,1024]{2,1,0:T(8,128)(2,1)S(1)} %copy-done.2, bf16[2,256,128]{2,1,0:T(8,128)(2,1)S(1)} %copy-done.3, ...), custom_call_target="tpu_custom_call" | custom-call | flops 2640000000 | bytes 7200000 | tf_op jit(solution)/shard_map/pallas_call | solution.py:352
  7.6 0.7 %collective-permute-done.2.refs_1_ = bf16[80,128]{1,0:T(8,128)(2,1)S(1)} collective-permute-done((bf16[80,128]{1,0:T(8,128)(2,1)S(1)}, bf16[80,128]{1,0:T(8,128)(2,1)S(1)}, u32[]{:S(2)}, u32[]{:S(2)}) %collective-permute-start.2) | collective-permute-done | bytes 20512 | tf_op jit(solution)/shard_map/ppermute | solution.py:395
  8.4 0.6 %collective-permute-done.1.refs_8_.v_one = bf16[2,256,128]{2,1,0:T(8,128)(2,1)S(1)} collective-permute-done((bf16[2,256,128]{2,1,0:T(8,128)(2,1)}, bf16[2,256,128]{2,1,0:T(8,128)(2,1)S(1)}, u32[]{:S(2)}, u32[]{:S(2)}) %collective-permute-start.1) | collective-permute-done | bytes 131104 | tf_op jit(solution)/shard_map/ppermute | solution.py:391
  9.0 0.0 collective-permute-done.refs_7_.k_one
  9.0 0.1 collective-permute-start.5
  9.1 0.4 %collective-permute-start.6 = (bf16[2,256,128]{2,1,0:T(8,128)(2,1)S(1)}, bf16[2,256,128]{2,1,0:T(8,128)(2,1)S(1)}, u32[]{:S(2)}, u32[]{:S(2)}) collective-permute-start(bf16[2,256,128]{2,1,0:T(8,128)(2,1)S(1)} %collective-permute-done.1.refs_8_.v_one), channel_id=1, source_target_pairs={{0,8},{8,0},{16,24},{24,16},{1,9},{9,1},{17,25},{25,17},{2,10},{10... | collective-permute-start | bytes 393224 | tf_op jit(solution)/shard_map/ppermute | solution.py:388
  9.5 0.7 %shard_map.125 = (f32[256,512]{1,0:T(8,128)S(1)}, f32[256,512]{1,0:T(8,128)S(1)}, f32[256,512]{1,0:T(8,128)S(1)}) custom-call(bf16[2,256,1024]{2,1,0:T(8,128)(2,1)S(1)} %copy-done.2, bf16[2,256,128]{2,1,0:T(8,128)(2,1)S(1)} %copy-done.3, bf16[2,256,128]{2,1,0:T(8,128)(2,1)S(1)} %copy-done.4, bf16[2,256,128]{2,1,0:T(8,128)(2,1)S(1)} %collective-permute-done.3.k_near.refs_5_, ...), custom_call_target="tpu_custom_call" | custom-call | flops 880000000 | bytes 2400000 | tf_op jit(solution)/shard_map/pallas_call | solution.py:352
  10.2 0.2 collective-permute-done.5.refs_9_.k_two
  10.3 0.2 collective-permute-done.6.refs_10_.v_two
  10.5 0.7 %shard_map.126 = (f32[80,128]{1,0:T(8,128)S(1)}, bf16[80,128]{1,0:T(8,128)(2,1)S(1)}) custom-call(bf16[80,128]{1,0:T(8,128)(2,1)S(1)} %get-tuple-element.61.refs_0_, bf16[80,128]{1,0:T(8,128)(2,1)S(1)} %collective-permute-done.2.refs_1_, s32[8,128]{1,0:T(8,128)S(1)} %get-tuple-element.43._.refs_2_.info_ref, bf16[2,256,128]{2,1,0:T(8,128)(2,1)S(1)} %copy-done.3, ...), custom_call_target="tpu_custom_call" | custom-call | flops 770000000 | bytes 2100000 | tf_op jit(solution)/shard_map/pallas_call | solution.py:352
  11.2 1.5 %collective-permute-start.7 = (bf16[80,128]{1,0:T(8,128)(2,1)S(1)}, bf16[80,128]{1,0:T(8,128)(2,1)S(1)}, u32[]{:S(2)}, u32[]{:S(2)}) collective-permute-start(bf16[80,128]{1,0:T(8,128)(2,1)S(1)} %get-tuple-element.78), channel_id=1, source_target_pairs={{0,9},{1,8},{8,1},{9,0},{16,25},{17,24},{24,17},{25,16},{2,11},{3,... | collective-permute-start | bytes 61448 | tf_op jit(solution)/shard_map/ppermute | solution.py:395
  12.7 12.9 %shard_map.127 = (bf16[2,256,1024]{2,1,0:T(8,128)(2,1)S(1)}, bf16[2,256,1024]{2,1,0:T(8,128)(2,1)}, f32[8,1024]{1,0:T(8,128)S(1)}) custom-call(s32[8,128]{1,0:T(8,128)S(1)} %get-tuple-element.43._.refs_2_.info_ref, bf16[2,256,1024]{2,1,0:T(8,128)(2,1)S(1)} %copy-done.2, bf16[2,256,128]{2,1,0:T(8,128)(2,1)S(1)} %collective-permute-done.refs_7_.k_one, ...), custom_call_target="tpu_custom_call" | custom-call | flops 3080000000 | bytes 8400000 | tf_op jit(solution)/shard_map/pallas_call | solution.py:352
  25.6 0.0 collective-permute-done.7.other_part
  25.6 0.8 %shard_map.128 = (bf16[4,2,2048]{2,1,0:T(2,128)(2,1)}, bf16[2,256,1024]{2,1,0:T(8,128)(2,1)}) custom-call(bf16[2,256,1024]{2,1,0:T(8,128)(2,1)S(1)} %get-tuple-element.76.pre, f32[8,1024]{1,0:T(8,128)S(1)} %get-tuple-element.77.own_rows, f32[2,64,128]{2,1,0:T(8,128)S(1)} %get-tuple-element.73.refs_9_.cache_sum, ...), custom_call_target="tpu_custom_call", output_to_operand_aliasing={{1}: (6, {})} | custom-call | flops 770000000 | bytes 2100000 | tf_op jit(solution)/shard_map/pallas_call | solution.py:352
  (9 shorter events, 0.0 us)
Async XLA Ops:
  0.6 2.1 %copy-start.3 = (bf16[2,256,128]{2,1,0:T(8,128)(2,1)S(1)}, bf16[2,256,128]{2,1,0:T(8,128)(2,1)}, u32[]{:S(2)}) copy-start(bf16[2,256,128]{2,1,0:T(8,128)(2,1)} %refs_3_.1) | copy-start | bytes 393220
  0.6 2.1 %copy-start.4 = (bf16[2,256,128]{2,1,0:T(8,128)(2,1)S(1)}, bf16[2,256,128]{2,1,0:T(8,128)(2,1)}, u32[]{:S(2)}) copy-start(bf16[2,256,128]{2,1,0:T(8,128)(2,1)} %refs_4_.1) | copy-start | bytes 393220
  0.7 2.6 %copy-start.1 = (bf16[2,1024,256]{2,1,0:T(8,128)(2,1)S(1)}, bf16[2,1024,256]{2,1,0:T(8,128)(2,1)}, u32[]{:S(2)}) copy-start(bf16[2,1024,256]{2,1,0:T(8,128)(2,1)} %cv_ref.1) | copy-start | bytes 3145732
  0.7 2.6 %copy-start = (bf16[2,1024,256]{2,1,0:T(8,128)(2,1)S(1)}, bf16[2,1024,256]{2,1,0:T(8,128)(2,1)}, u32[]{:S(2)}) copy-start(bf16[2,1024,256]{2,1,0:T(8,128)(2,1)} %ck_ref.1) | copy-start | bytes 3145732
  0.7 8.3 %collective-permute-start = (bf16[2,256,128]{2,1,0:T(8,128)(2,1)}, bf16[2,256,128]{2,1,0:T(8,128)(2,1)S(1)}, u32[]{:S(2)}, u32[]{:S(2)}) collective-permute-start(bf16[2,256,128]{2,1,0:T(8,128)(2,1)} %refs_3_.1), channel_id=1, source_target_pairs={{0,16},{8,24},{16,0},{24,8},{1,17},{9,25},{17,1},{25,9},{2,18},{10... | collective-permute-start | bytes 393224 | tf_op jit(solution)/shard_map/ppermute | solution.py:391
  1.2 7.7 %collective-permute-start.1 = (bf16[2,256,128]{2,1,0:T(8,128)(2,1)}, bf16[2,256,128]{2,1,0:T(8,128)(2,1)S(1)}, u32[]{:S(2)}, u32[]{:S(2)}) collective-permute-start(bf16[2,256,128]{2,1,0:T(8,128)(2,1)} %refs_4_.1), channel_id=1, source_target_pairs={{0,16},{8,24},{16,0},{24,8},{1,17},{9,25},{17,1},{25,9},{2,18},{10... | collective-permute-start | bytes 393224 | tf_op jit(solution)/shard_map/ppermute | solution.py:391
  2.8 3.6 %copy-start.2 = (bf16[2,256,1024]{2,1,0:T(8,128)(2,1)S(1)}, bf16[2,256,1024]{2,1,0:T(8,128)(2,1)}, u32[]{:S(2)}) copy-start(bf16[2,256,1024]{2,1,0:T(8,128)(2,1)} %q_ref.5) | copy-start | bytes 3145732
  2.8 3.5 %collective-permute-start.3 = (bf16[2,256,128]{2,1,0:T(8,128)(2,1)S(1)}, bf16[2,256,128]{2,1,0:T(8,128)(2,1)S(1)}, u32[]{:S(2)}, u32[]{:S(2)}) collective-permute-start(bf16[2,256,128]{2,1,0:T(8,128)(2,1)S(1)} %copy-done.3), channel_id=1, source_target_pairs={{0,8},{8,0},{16,24},{24,16},{1,9},{9,1},{17,25},{25,17},{2,10},{10... | collective-permute-start | bytes 393224 | tf_op jit(solution)/shard_map/ppermute | solution.py:388
  2.8 3.5 %collective-permute-start.4 = (bf16[2,256,128]{2,1,0:T(8,128)(2,1)S(1)}, bf16[2,256,128]{2,1,0:T(8,128)(2,1)S(1)}, u32[]{:S(2)}, u32[]{:S(2)}) collective-permute-start(bf16[2,256,128]{2,1,0:T(8,128)(2,1)S(1)} %copy-done.4), channel_id=1, source_target_pairs={{0,8},{8,0},{16,24},{24,16},{1,9},{9,1},{17,25},{25,17},{2,10},{10... | collective-permute-start | bytes 393224 | tf_op jit(solution)/shard_map/ppermute | solution.py:388
  5.1 3.3 %collective-permute-start.2 = (bf16[80,128]{1,0:T(8,128)(2,1)S(1)}, bf16[80,128]{1,0:T(8,128)(2,1)S(1)}, u32[]{:S(2)}, u32[]{:S(2)}) collective-permute-start(bf16[80,128]{1,0:T(8,128)(2,1)S(1)} %get-tuple-element.44), channel_id=1, source_target_pairs={{0,9},{1,8},{8,1},{9,0},{16,25},{17,24},{24,17},{25,16},{2,11},{3,... | collective-permute-start | bytes 61448 | tf_op jit(solution)/shard_map/ppermute | solution.py:395
  9.0 1.3 %collective-permute-start.5 = (bf16[2,256,128]{2,1,0:T(8,128)(2,1)S(1)}, bf16[2,256,128]{2,1,0:T(8,128)(2,1)S(1)}, u32[]{:S(2)}, u32[]{:S(2)}) collective-permute-start(bf16[2,256,128]{2,1,0:T(8,128)(2,1)S(1)} %collective-permute-done.refs_7_.k_one), channel_id=1, source_target_pairs={{0,8},{8,0},{16,24},{24,16},{1,9},{9,1},{17,25},{25,17},{2,10},{10... | collective-permute-start | bytes 393224 | tf_op jit(solution)/shard_map/ppermute | solution.py:388
  9.1 1.4 %collective-permute-start.6 = (bf16[2,256,128]{2,1,0:T(8,128)(2,1)S(1)}, bf16[2,256,128]{2,1,0:T(8,128)(2,1)S(1)}, u32[]{:S(2)}, u32[]{:S(2)}) collective-permute-start(bf16[2,256,128]{2,1,0:T(8,128)(2,1)S(1)} %collective-permute-done.1.refs_8_.v_one), channel_id=1, source_target_pairs={{0,8},{8,0},{16,24},{24,16},{1,9},{9,1},{17,25},{25,17},{2,10},{10... | collective-permute-start | bytes 393224 | tf_op jit(solution)/shard_map/ppermute | solution.py:388
  11.2 14.4 %collective-permute-start.7 = (bf16[80,128]{1,0:T(8,128)(2,1)S(1)}, bf16[80,128]{1,0:T(8,128)(2,1)S(1)}, u32[]{:S(2)}, u32[]{:S(2)}) collective-permute-start(bf16[80,128]{1,0:T(8,128)(2,1)S(1)} %get-tuple-element.78), channel_id=1, source_target_pairs={{0,9},{1,8},{8,1},{9,0},{16,25},{17,24},{24,17},{25,16},{2,11},{3,... | collective-permute-start | bytes 61448 | tf_op jit(solution)/shard_map/ppermute | solution.py:395

commit v9 on v8

--- a/solution.py
+++ b/solution.py
@@ -172,40 +172,86 @@
         out[queries : queries + 16, :] = stats.astype(out.dtype)
 
 
-def local_kernel(blocks, q_ref, k_own, v_own, k_near, v_near, _, *refs):
-    outs, wide = refs[:-1], refs[-1]
-    prompts, length, _ = q_ref.shape
-    seq = lax.axis_index("seq")
-    for row in sorted({row for row, _, _ in blocks}):
-        wide[row, :length, :D_HEAD] = v_own[row]
-        wide[row, length:, :D_HEAD] = v_near[row]
-        wide[row, :, D_HEAD:] = jnp.ones((2 * length, D_HEAD), jnp.bfloat16)
+def local_heads(block, with_near, q_ref, k_own, k_near, wide, outs):
+    row, start, stop = block
+    length = q_ref.shape[1]
+    sum_ref, top_ref, tot_ref = outs
     causal = lax.broadcasted_iota(jnp.int32, (length, length), 1) <= lax.broadcasted_iota(
         jnp.int32, (length, length), 0
     )
-
-    def run(with_near):
-        for index, (row, start, stop) in enumerate(blocks):
-            sum_ref, top_ref, tot_ref = outs[3 * index : 3 * index + 3]
-            for head in range(start, stop):
-                cols = slice((head - start) * D_HEAD, (head - start + 1) * D_HEAD)
-                q = q_ref[row, :, head * D_HEAD : (head + 1) * D_HEAD]
-                scores = jnp.where(causal, scores_of(q, k_own[row]), MASKED_SCORE)
-                if with_near:
-                    scores = jnp.concatenate([scores, scores_of(q, k_near[row])], axis=1)
-                top = jnp.max(scores, axis=1, keepdims=True) * EXP2_SCALE
-                summed = weighted(jnp.exp2(scores * EXP2_SCALE - top), wide[row, : scores.shape[1], :])
-                sum_ref[:, cols] = summed[:, :D_HEAD]
-                tot_ref[:, cols] = summed[:, D_HEAD:]
-                top_ref[:, cols] = jnp.broadcast_to(top, (length, D_HEAD))
-
-    @pl.when(seq % 2 == 0)
-    def _():
-        run(False)
-
-    @pl.when(seq % 2 == 1)
-    def _():
-        run(True)
+    for head in range(start, stop):
+        cols = slice((head - start) * D_HEAD, (head - start + 1) * D_HEAD)
+        q = q_ref[row, :, head * D_HEAD : (head + 1) * D_HEAD]
+        scores = jnp.where(causal, scores_of(q, k_own[row]), MASKED_SCORE)
+        if with_near:
+            scores = jnp.concatenate([scores, scores_of(q, k_near[row])], axis=1)
+        top = jnp.max(scores, axis=1, keepdims=True) * EXP2_SCALE
+        summed = weighted(jnp.exp2(scores * EXP2_SCALE - top), wide[row, : scores.shape[1], :])
+        sum_ref[:, cols] = summed[:, :D_HEAD]
+        tot_ref[:, cols] = summed[:, D_HEAD:]
+        top_ref[:, cols] = jnp.broadcast_to(top, (length, D_HEAD))
+
+
+def widen(rows, v_one, v_two, wide):
+    length = v_one.shape[1]
+    for row in rows:
+        wide[row, :length, :D_HEAD] = v_one[row]
+        wide[row, length:, :D_HEAD] = v_two[row]
+        wide[row, :, D_HEAD:] = jnp.ones((2 * length, D_HEAD), jnp.bfloat16)
+
+
+def local_kernel(blocks, shift, q_ref, k_own, v_own, k_near, v_near, _, *refs):
+    outs, wide = refs[:-1], refs[-1]
+    prompts = q_ref.shape[0]
+    seq = lax.axis_index("seq")
+    widen(range(prompts), v_own, v_near, wide)
+
+    def run(some, with_near):
+        for index in some:
+            local_heads(blocks[index], with_near, q_ref, k_own, k_near, wide, outs[3 * index : 3 * index + 3])
+
+    for core in range(2):
+
+        @pl.when(seq % 2 == core)
+        def _(core=core):
+            run(range(len(blocks) - 1), core == 1)
+
+            @pl.when(seq // 2 >= shift)
+            def _():
+                run([len(blocks) - 1], core == 1)
+
+
+def window_kernel(blocks, shift, keep, q_ref, k_own, v_own, k_near, v_near, k_one, v_one, _, *refs):
+    first_in, last_in, first_out, last_out = (refs[3 * i : 3 * i + 3] for i in range(4))
+    wide = refs[-1]
+    seq = lax.axis_index("seq")
+    length = q_ref.shape[1]
+    late = seq // 2 >= shift
+
+    def emit(index, row, cols, at, summed, total, top):
+        for ref, value in zip(first_out, (summed, top, total)):
+            ref[:, at] = value
+
+    @pl.when(late)
+    def _():
+        widen([0], v_one, v_one, wide)
+        add_blocks([(0, *blocks[0])], lambda row: ([k_one[row]], wide[row, :length]), q_ref, first_in, emit)
+        if keep:
+            for ref, value in zip(last_out, last_in):
+                ref[...] = value[...]
+
+    @pl.when(jnp.logical_not(late))
+    def _():
+        widen([blocks[-1][0]], v_own, v_near, wide)
+        for core in range(2):
+
+            @pl.when(seq % 2 == core)
+            def _(core=core):
+                local_heads(blocks[-1], core == 1, q_ref, k_own, k_near, wide, last_out)
+
+        if keep:
+            for ref, value in zip(first_out, first_in):
+                ref[...] = value[...]
 
 
 def merged(span, group, cache_sum, cache_top, cache_tot, part):
@@ -239,24 +285,58 @@
     return summed + far[:, :D_HEAD], total + far[:, D_HEAD:]
 
 
-def far_kernel(blocks, shift, last, span, info_ref, q_ref, k_one, v_one, k_two, v_two, _, *refs):
-    prompts, length, columns = q_ref.shape
+def add_blocks(blocks, far_of, q_ref, states, emit, row_done=None, before=None, after=None):
+    length = q_ref.shape[1]
+
+    def state_of(index, at):
+        return (states[3 * index][:, at], states[3 * index + 2][:, at], states[3 * index + 1][:, at])
+
+    worst = jnp.zeros((8, D_HEAD), jnp.float32)
+    for index, row, start, stop in blocks:
+        for head in range(start, stop):
+            cols = slice(head * D_HEAD, (head + 1) * D_HEAD)
+            at = slice((head - start) * D_HEAD, (head - start + 1) * D_HEAD)
+            state = state_of(index, at)
+            summed, total = add_keys_at(q_ref[row, :, cols], *far_of(row), *state)
+            emit(index, row, cols, at, summed, total, state[2])
+            if row_done and cols.stop == q_ref.shape[2]:
+                row_done(row)
+            peaks = [total[i : i + 8] for i in range(0, length, 8)]
+            worst = functools.reduce(jnp.maximum, [functools.reduce(jnp.maximum, peaks[i::4]) for i in range(4)], worst)
+
+    if before:
+        before()
+
+    @pl.when(jnp.max(worst) > SUM_LIMIT)
+    def _():
+        for index, row, start, stop in blocks:
+
+            @pl.loop(0, stop - start)
+            def _(head, index=index, row=row, start=start):
+                at = pl.ds(pl.multiple_of(head * D_HEAD, D_HEAD), D_HEAD)
+                cols = pl.ds(pl.multiple_of((start + head) * D_HEAD, D_HEAD), D_HEAD)
+                new = add_keys(q_ref[row, :, cols], *far_of(row), *state_of(index, at))
+                emit(index, row, cols, at, *new)
+
+        if after:
+            after()
+
+
+def far_kernel(blocks, chosen, shift, last, span, info_ref, q_ref, k_one, v_one, k_two, v_two, _, *refs):
+    _, length, columns = q_ref.shape
     group = columns // D_HEAD
     count = 3 * len(blocks)
-    states, outs, (wide, sem) = refs[:count], refs[count:-2], refs[-2:]
+    states, others, outs, (wide, sem) = refs[:count], refs[count : 2 * count], refs[2 * count : -2], refs[-2:]
     if last:
         (cache_sum, cache_top, cache_tot, own_part), outs = outs[:4], outs[4:]
         outs[2][...] = merged(span, group, cache_sum[0], cache_top[0], cache_tot[0], own_part)
     seq = lax.axis_index("seq")
     position = seq * length + lax.broadcasted_iota(jnp.int32, (length, D_HEAD), 0)
-    places = [
-        (index, row, slice(head * D_HEAD, (head + 1) * D_HEAD), slice((head - start) * D_HEAD, (head - start + 1) * D_HEAD))
-        for index, (row, start, stop) in enumerate(blocks)
-        for head in range(start, stop)
-    ]
-
-    def state_of(index, at):
-        return (states[3 * index][:, at], states[3 * index + 2][:, at], states[3 * index + 1][:, at])
+    places = [(index, *block) for index, block in enumerate(blocks)]
+
+    def far_of(row):
+        first, stop = chosen[row][0] * length, (chosen[row][-1] + 1) * length
+        return [(k_one, k_two)[i][row] for i in chosen[row]], wide[row, first:stop]
 
     def emit(index, row, cols, at, summed, total, top):
         if last:
@@ -266,46 +346,36 @@
             for ref, value in zip(outs[3 * index : 3 * index + 3], (summed, top, total)):
                 ref[:, at] = value
 
+    hooks = {}
+    if last:
+        first_copy = pltpu.make_async_copy(outs[0].at[0], outs[1].at[0], sem)
+
+        def row_done(row):
+            if row == 0:
+                first_copy.start()
+
+        def after():
+            first_copy.start()
+            first_copy.wait()
+
+        hooks = {"row_done": row_done, "before": first_copy.wait, "after": after}
+
     @pl.when(seq // 2 >= shift)
     def _():
-        wide[:, :length, :D_HEAD] = v_one[...]
-        wide[:, length:, :D_HEAD] = v_two[...]
-        wide[:, :, D_HEAD:] = jnp.ones((prompts, 2 * length, D_HEAD), jnp.bfloat16)
-        worst = jnp.zeros((8, D_HEAD), jnp.float32)
-        if last:
-            first_copy = pltpu.make_async_copy(outs[0].at[0], outs[1].at[0], sem)
-        for index, row, cols, at in places:
-            state = state_of(index, at)
-            summed, total = add_keys_at(q_ref[row, :, cols], (k_one[row], k_two[row]), wide[row], *state)
-            emit(index, row, cols, at, summed, total, state[2])
-            if last and row == 0 and cols.stop == columns:
-                first_copy.start()
-            peaks = [total[i : i + 8] for i in range(0, length, 8)]
-            worst = functools.reduce(jnp.maximum, [functools.reduce(jnp.maximum, peaks[i::4]) for i in range(4)], worst)
-
-        if last:
-            first_copy.wait()
-
-        @pl.when(jnp.max(worst) > SUM_LIMIT)
-        def _():
-            for index, (row, start, stop) in enumerate(blocks):
-
-                @pl.loop(0, stop - start)
-                def _(head, index=index, row=row, start=start):
-                    at = pl.ds(pl.multiple_of(head * D_HEAD, D_HEAD), D_HEAD)
-                    cols = pl.ds(pl.multiple_of((start + head) * D_HEAD, D_HEAD), D_HEAD)
-                    state = state_of(index, at)
-                    new = add_keys(q_ref[row, :, cols], (k_one[row], k_two[row]), wide[row], *state)
-                    emit(index, row, cols, at, *new)
-
-            if last:
-                first_copy.start()
-                first_copy.wait()
+        widen(range(q_ref.shape[0]), v_one, v_two, wide)
+        add_blocks(places, far_of, q_ref, states, emit, **hooks)
 
     @pl.when(seq // 2 < shift)
     def _():
-        for index, row, cols, at in places:
-            emit(index, row, cols, at, *state_of(index, at))
+        for index, row, start, stop in places:
+
+            @pl.loop(0, stop - start)
+            def _(head, index=index, row=row, start=start):
+                at = pl.ds(pl.multiple_of(head * D_HEAD, D_HEAD), D_HEAD)
+                cols = pl.ds(pl.multiple_of((start + head) * D_HEAD, D_HEAD), D_HEAD)
+                kept = others[3 * index : 3 * index + 3]
+                emit(index, row, cols, at, kept[0][:, at], kept[2][:, at], kept[1][:, at])
+
         if last:
             copy = pltpu.make_async_copy(outs[0], outs[1], sem)
             copy.start()
@@ -427,28 +497,40 @@
     blocks += [(prompts - 1, 0, group // 2), (prompts - 1, group // 2, group)]
     runs = [[shape((length, (stop - start) * D_HEAD), f32)] * 3 for _, start, stop in blocks]
 
-    def local(some, outs, marker):
-        return call(
-            functools.partial(local_kernel, some),
-            (prefill_queries, prefill_keys, prefill_values, near_keys, near_values, marker),
-            sum(outs, []),
-            [pltpu.VMEM((prompts, 2 * length, 2 * D_HEAD), bf16)],
-            specs=[VMEM] * 5 + [ANY],
-            us=0.2 * sum(stop - start for _, start, stop in some),
-        )
-
-    states = local(blocks[:-1], runs[:-1], info)
+    last_shift = shifts[-1]
+    wide = pltpu.VMEM((prompts, 2 * length, 2 * D_HEAD), bf16)
+    mine = (prefill_queries, prefill_keys, prefill_values, near_keys, near_values)
+    states = call(
+        functools.partial(local_kernel, blocks, last_shift),
+        (*mine, info),
+        sum(runs, []),
+        [wide],
+        specs=[VMEM] * 5 + [ANY],
+        us=2.6,
+    )
     far_values, partner_msg, states = after((far_values, partner_msg, states))
     far_near_values = [near(v) for v in far_values]
     far_keys, states = after((far_keys, states))
     far_near_keys = [near(k) for k in far_keys]
-    states = [*states, *local(blocks[-1:], runs[-1:], states[0])]
+    keep = len(shifts) > 1
+    window = call(
+        functools.partial(window_kernel, blocks, last_shift, keep),
+        (*mine, far_keys[-1], far_values[-1], info, *states[:3], *states[-3:]),
+        runs[0] + runs[-1],
+        [wide],
+        specs=[VMEM] * 7 + [ANY] + [VMEM] * 6,
+        us=1.0,
+    )
+    others = [*states[:-3], *window[3:]]
+    states = [*window[:3], *states[3:]]
+    if keep:
+        states = others = [*window[:3], *states[3:-3], *window[3:]]
     far = list(zip(far_keys, far_values, far_near_keys, far_near_values))
     chunks = [prefill_keys, prefill_values, near_keys, near_values] + sum([list(four) for four in far], [])
     parts = [shape((queries + 16, 128), f32), shape((queries + 16, 128), bf16)]
     own_part, partner_part = call(
         functools.partial(prompt_kernel, span),
-        (own_msg, partner_msg, info, *chunks, states[-1]),
+        (own_msg, partner_msg, info, *chunks, window[0]),
         parts,
         specs=[VMEM] * (3 + len(chunks)) + [ANY],
         us=0.7,
@@ -456,18 +538,19 @@
     other_part = partner(partner_part)
     for index, shift in enumerate(shifts):
         last = index == len(shifts) - 1
+        chosen = {row: (1,) if last and row == 0 else (0, 1) for row in range(prompts)}
         outs, out_specs, extra = sum(runs, []), [VMEM] * len(states), []
         if last:
             outs = [shape(prefill_queries.shape, bf16)] * 2 + [shape((span, dec_columns // 2), f32)]
             out_specs, extra = [VMEM, ANY, VMEM], [*cache, own_part]
-        states = call(
-            functools.partial(far_kernel, blocks, shift, last, span),
-            (info, prefill_queries, *far[index], own_part, *states, *extra),
+        states = others = call(
+            functools.partial(far_kernel, blocks, chosen, shift, last, span),
+            (info, prefill_queries, *far[index], own_part, *states, *others, *extra),
             outs,
-            [pltpu.VMEM((prompts, 2 * length, 2 * D_HEAD), bf16), pltpu.SemaphoreType.DMA(())],
-            specs=[VMEM] * 6 + [ANY] + [VMEM] * (len(states) + len(extra)),
+            [wide, pltpu.SemaphoreType.DMA(())],
+            specs=[VMEM] * 6 + [ANY] + [VMEM] * (2 * len(states) + len(extra)),
             out_specs=out_specs,
-            us=2.8,
+            us=2.4,
         )
     pre, prefill_out, own_rows = states
     decode_out, prefill_out = call(

time: 26.6 us -> 25 us (0.940)
  waiting for transfers between devices: 1.74 us -> 1.01 us
  Pallas kernels: 18.1 us -> 17.5 us
    ppermute x2, starting transfers between devices: 2.72 us -> 1.74 us  [partner(): return lax.ppermute(x, ('seq', 'role'), moves)]
    ppermute x4, starting transfers between devices: 1.01 us -> 1.74 us  [near(): return lax.ppermute(x, 'seq', [(i, i ^ 1) for i in range(seqs)])]
    ppermute x2, waiting for transfers between devices: 0.75 us -> 0.12 us  [partner(): return lax.ppermute(x, ('seq', 'role'), moves)]
    pallas_call x7, Pallas kernels: 18.1 us -> 17.5 us  [call(): pl.pallas_call(kernel, out_shape=outs, in_specs=specs or [VMEM] * len(arg...]
  transfers between devices with their start and end apart: 8 -> 8, of which waited for: 4 -> 3; matrix products, arithmetic and copies ran while one was open for 0% -> 0% of each run, Pallas kernels for 63% -> 64%
where the time goes in v9:
time: 25 us; the launch traced here: 24.9 us
  Pallas kernels  17.5 us (70%)
  starting transfers between devices  5.57 us (22%)
  waiting for transfers between devices  1.01 us (4%)
  between operations  0.74 us (3%)
    pallas_call x7, Pallas kernels, call(): pl.pallas_call(kernel, out_shape=outs, in_specs=specs or [VMEM] * len(arg...  17.5 us
    ppermute x2, starting transfers between devices, around(): lax.ppermute(x, 'seq', [(i, (i + 2 * shift) % seqs) for i in range(seqs)])  2.09 us
    ppermute x4, starting transfers between devices, near(): return lax.ppermute(x, 'seq', [(i, i ^ 1) for i in range(seqs)])  1.74 us
    ppermute x2, starting transfers between devices, partner(): return lax.ppermute(x, ('seq', 'role'), moves)  1.74 us
    ppermute x2, waiting for transfers between devices, around(): lax.ppermute(x, 'seq', [(i, (i + 2 * shift) % seqs) for i in range(seqs)])  0.64 us
  transfers between devices with their start and end apart: 8, of which 3 were waited for; matrix products, arithmetic and copies ran while one was open for 0% of the time, Pallas kernels for 64%

profile of v9, /device:TPU:28, one launch (start us, length us, event | category | flops | bytes accessed | tf_op | source)
XLA Modules:
  0.0 24.9 jit_solution(11297964071864319987)
XLA Ops:
  0.7 0.6 %collective-permute-start = (bf16[2,256,128]{2,1,0:T(8,128)(2,1)}, bf16[2,256,128]{2,1,0:T(8,128)(2,1)S(1)}, u32[]{:S(2)}, u32[]{:S(2)}) collective-permute-start(bf16[2,256,128]{2,1,0:T(8,128)(2,1)} %refs_3_.1), channel_id=1, source_target_pairs={{0,16},{8,24},{16,0},{24,8},{1,17},{9,25},{17,1},{25,9},{2,18},{10... | collective-permute-start | bytes 393224 | tf_op jit(solution)/shard_map/ppermute | solution.py:461
  1.2 1.5 %collective-permute-start.1 = (bf16[2,256,128]{2,1,0:T(8,128)(2,1)}, bf16[2,256,128]{2,1,0:T(8,128)(2,1)S(1)}, u32[]{:S(2)}, u32[]{:S(2)}) collective-permute-start(bf16[2,256,128]{2,1,0:T(8,128)(2,1)} %refs_4_.1), channel_id=1, source_target_pairs={{0,16},{8,24},{16,0},{24,8},{1,17},{9,25},{17,1},{25,9},{2,18},{10... | collective-permute-start | bytes 393224 | tf_op jit(solution)/shard_map/ppermute | solution.py:461
  2.8 0.0 copy-done.1
  2.8 0.0 collective-permute-start.3
  2.8 0.5 %collective-permute-start.4 = (bf16[2,256,128]{2,1,0:T(8,128)(2,1)S(1)}, bf16[2,256,128]{2,1,0:T(8,128)(2,1)S(1)}, u32[]{:S(2)}, u32[]{:S(2)}) collective-permute-start(bf16[2,256,128]{2,1,0:T(8,128)(2,1)S(1)} %copy-done.2), channel_id=1, source_target_pairs={{0,8},{8,0},{16,24},{24,16},{1,9},{9,1},{17,25},{25,17},{2,10},{10... | collective-permute-start | bytes 393224 | tf_op jit(solution)/shard_map/ppermute | solution.py:458
  3.3 1.8 %shard_map.123 = (bf16[80,128]{1,0:T(8,128)(2,1)S(1)}, bf16[80,128]{1,0:T(8,128)(2,1)S(1)}, s32[8,128]{1,0:T(8,128)S(1)}, f32[2,64,128]{2,1,0:T(8,128)S(1)}, f32...) custom-call(s32[2]{0:T(128)} %asg_hbm.1, s32[2]{0:T(128)} %plen_hbm.1, s32[2]{0:T(128)} %clen_hbm.1, ...), custom_call_target="tpu_custom_call" | custom-call | flops 1430000000 | bytes 3900000 | tf_op jit(solution)/shard_map/pallas_call | solution.py:422
  5.1 1.2 %collective-permute-start.2 = (bf16[80,128]{1,0:T(8,128)(2,1)S(1)}, bf16[80,128]{1,0:T(8,128)(2,1)S(1)}, u32[]{:S(2)}, u32[]{:S(2)}) collective-permute-start(bf16[80,128]{1,0:T(8,128)(2,1)S(1)} %get-tuple-element.56), channel_id=1, source_target_pairs={{0,9},{1,8},{8,1},{9,0},{16,25},{17,24},{24,17},{25,16},{2,11},{3,... | collective-permute-start | bytes 61448 | tf_op jit(solution)/shard_map/ppermute | solution.py:465
  6.3 0.0 collective-permute-done.3.k_near.refs_5_
  6.3 0.0 collective-permute-done.4.v_near.refs_6_
  6.3 0.0 copy-done
  6.3 1.9 %shard_map.124 = (f32[256,1024]{1,0:T(8,128)S(1)}, f32[256,1024]{1,0:T(8,128)S(1)}, f32[256,1024]{1,0:T(8,128)S(1)}, f32[256,512]{1,0:T(8,128)S(1)}, f32[256,512...) custom-call(bf16[2,256,1024]{2,1,0:T(8,128)(2,1)S(1)} %copy-done, ...), custom_call_target="tpu_custom_call" | custom-call | flops 2860000000 | bytes 7800000 | tf_op jit(solution)/shard_map/pallas_call | solution.py:422
  8.2 0.1 collective-permute-done.2.refs_1_
  8.4 0.6 %collective-permute-done.1.v_one.refs_8_ = bf16[2,256,128]{2,1,0:T(8,128)(2,1)S(1)} collective-permute-done((bf16[2,256,128]{2,1,0:T(8,128)(2,1)}, bf16[2,256,128]{2,1,0:T(8,128)(2,1)S(1)}, u32[]{:S(2)}, u32[]{:S(2)}) %collective-permute-start.1) | collective-permute-done | bytes 131104 | tf_op jit(solution)/shard_map/ppermute | solution.py:461
  9.0 0.0 collective-permute-done.k_one.refs_7_
  9.0 1.2 %collective-permute-start.5 = (bf16[2,256,128]{2,1,0:T(8,128)(2,1)S(1)}, bf16[2,256,128]{2,1,0:T(8,128)(2,1)S(1)}, u32[]{:S(2)}, u32[]{:S(2)}) collective-permute-start(bf16[2,256,128]{2,1,0:T(8,128)(2,1)S(1)} %collective-permute-done.k_one.refs_7_), channel_id=1, source_target_pairs={{0,8},{8,0},{16,24},{24,16},{1,9},{9,1},{17,25},{25,17},{2,10},{10... | collective-permute-start | bytes 393224 | tf_op jit(solution)/shard_map/ppermute | solution.py:458
  10.2 0.1 collective-permute-start.6
  10.2 1.0 %shard_map.125 = (f32[256,1024]{1,0:T(8,128)S(1)}, f32[256,1024]{1,0:T(8,128)S(1)}, f32[256,1024]{1,0:T(8,128)S(1)}, f32[256,512]{1,0:T(8,128)S(1)}, f32[256,512]{1,0:T(8,128)S(1)}, /*index=5*/f32[256,512]{1,0:T(8,128)S(1)}) custom-call(bf16[2,256,1024]{2,1,0:T(8,128)(2,1)S(1)} %copy-done, bf16[2,256,128]{2,1,0:T(8,128)(2,1)S(1)} %copy-done.1, ...), custom_call_target="tpu_custom_call" | custom-call | flops 1100000000 | bytes 3000000 | tf_op jit(solution)/shard_map/pallas_call | solution.py:422
  11.3 0.0 collective-permute-done.5.refs_9_.k_two
  11.3 0.2 collective-permute-done.6.refs_10_.v_two
  11.5 0.7 %shard_map.126 = (f32[80,128]{1,0:T(8,128)S(1)}, bf16[80,128]{1,0:T(8,128)(2,1)S(1)}) custom-call(bf16[80,128]{1,0:T(8,128)(2,1)S(1)} %get-tuple-element.79.refs_0_, bf16[80,128]{1,0:T(8,128)(2,1)S(1)} %collective-permute-done.2.refs_1_, s32[8,128]{1,0:T(8,128)S(1)} %get-tuple-element.55._.refs_2_.info_ref, bf16[2,256,128]{2,1,0:T(8,128)(2,1)S(1)} %copy-done.1, ...), custom_call_target="tpu_custom_call" | custom-call | flops 770000000 | bytes 2100000 | tf_op jit(solution)/shard_map/pallas_call | solution.py:422
  12.2 0.5 %collective-permute-start.7 = (bf16[80,128]{1,0:T(8,128)(2,1)S(1)}, bf16[80,128]{1,0:T(8,128)(2,1)S(1)}, u32[]{:S(2)}, u32[]{:S(2)}) collective-permute-start(bf16[80,128]{1,0:T(8,128)(2,1)S(1)} %get-tuple-element.102), channel_id=1, source_target_pairs={{0,9},{1,8},{8,1},{9,0},{16,25},{17,24},{24,17},{25,16},{2,11},{3,... | collective-permute-start | bytes 61448 | tf_op jit(solution)/shard_map/ppermute | solution.py:465
  12.7 11.3 %shard_map.127 = (bf16[2,256,1024]{2,1,0:T(8,128)(2,1)S(1)}, bf16[2,256,1024]{2,1,0:T(8,128)(2,1)}, f32[8,1024]{1,0:T(8,128)S(1)}) custom-call(s32[8,128]{1,0:T(8,128)S(1)} %get-tuple-element.55._.refs_2_.info_ref, bf16[2,256,1024]{2,1,0:T(8,128)(2,1)S(1)} %copy-done, bf16[2,256,128]{2,1,0:T(8,128)(2,1)S(1)} %collective-permute-done.k_one.refs_7_, ...), custom_call_target="tpu_custom_call" | custom-call | flops 2640000000 | bytes 7200000 | tf_op jit(solution)/shard_map/pallas_call | solution.py:422
  24.0 0.0 collective-permute-done.7.other_part
  24.0 0.8 %shard_map.128 = (bf16[4,2,2048]{2,1,0:T(2,128)(2,1)}, bf16[2,256,1024]{2,1,0:T(8,128)(2,1)}) custom-call(bf16[2,256,1024]{2,1,0:T(8,128)(2,1)S(1)} %get-tuple-element.100.pre, f32[8,1024]{1,0:T(8,128)S(1)} %get-tuple-element.101.own_rows, f32[2,64,128]{2,1,0:T(8,128)S(1)} %get-tuple-element.97.refs_18_.cache_sum, ...), custom_call_target="tpu_custom_call", output_to_operand_aliasing={{1}: (6, {})} | custom-call | flops 770000000 | bytes 2100000 | tf_op jit(solution)/shard_map/pallas_call | solution.py:422
  (9 shorter events, 0.0 us)
Async XLA Ops:
  0.6 2.1 %copy-start.1 = (bf16[2,256,128]{2,1,0:T(8,128)(2,1)S(1)}, bf16[2,256,128]{2,1,0:T(8,128)(2,1)}, u32[]{:S(2)}) copy-start(bf16[2,256,128]{2,1,0:T(8,128)(2,1)} %refs_3_.1) | copy-start | bytes 393220
  0.6 2.1 %copy-start.2 = (bf16[2,256,128]{2,1,0:T(8,128)(2,1)S(1)}, bf16[2,256,128]{2,1,0:T(8,128)(2,1)}, u32[]{:S(2)}) copy-start(bf16[2,256,128]{2,1,0:T(8,128)(2,1)} %refs_4_.1) | copy-start | bytes 393220
  0.7 2.6 %copy-start.4 = (bf16[2,1024,256]{2,1,0:T(8,128)(2,1)S(1)}, bf16[2,1024,256]{2,1,0:T(8,128)(2,1)}, u32[]{:S(2)}) copy-start(bf16[2,1024,256]{2,1,0:T(8,128)(2,1)} %cv_ref.1) | copy-start | bytes 3145732
  0.7 2.6 %copy-start.3 = (bf16[2,1024,256]{2,1,0:T(8,128)(2,1)S(1)}, bf16[2,1024,256]{2,1,0:T(8,128)(2,1)}, u32[]{:S(2)}) copy-start(bf16[2,1024,256]{2,1,0:T(8,128)(2,1)} %ck_ref.1) | copy-start | bytes 3145732
  0.7 8.3 %collective-permute-start = (bf16[2,256,128]{2,1,0:T(8,128)(2,1)}, bf16[2,256,128]{2,1,0:T(8,128)(2,1)S(1)}, u32[]{:S(2)}, u32[]{:S(2)}) collective-permute-start(bf16[2,256,128]{2,1,0:T(8,128)(2,1)} %refs_3_.1), channel_id=1, source_target_pairs={{0,16},{8,24},{16,0},{24,8},{1,17},{9,25},{17,1},{25,9},{2,18},{10... | collective-permute-start | bytes 393224 | tf_op jit(solution)/shard_map/ppermute | solution.py:461
  1.2 7.7 %collective-permute-start.1 = (bf16[2,256,128]{2,1,0:T(8,128)(2,1)}, bf16[2,256,128]{2,1,0:T(8,128)(2,1)S(1)}, u32[]{:S(2)}, u32[]{:S(2)}) collective-permute-start(bf16[2,256,128]{2,1,0:T(8,128)(2,1)} %refs_4_.1), channel_id=1, source_target_pairs={{0,16},{8,24},{16,0},{24,8},{1,17},{9,25},{17,1},{25,9},{2,18},{10... | collective-permute-start | bytes 393224 | tf_op jit(solution)/shard_map/ppermute | solution.py:461
  2.8 3.6 %copy-start = (bf16[2,256,1024]{2,1,0:T(8,128)(2,1)S(1)}, bf16[2,256,1024]{2,1,0:T(8,128)(2,1)}, u32[]{:S(2)}) copy-start(bf16[2,256,1024]{2,1,0:T(8,128)(2,1)} %q_ref.5) | copy-start | bytes 3145732
  2.8 3.5 %collective-permute-start.3 = (bf16[2,256,128]{2,1,0:T(8,128)(2,1)S(1)}, bf16[2,256,128]{2,1,0:T(8,128)(2,1)S(1)}, u32[]{:S(2)}, u32[]{:S(2)}) collective-permute-start(bf16[2,256,128]{2,1,0:T(8,128)(2,1)S(1)} %copy-done.1), channel_id=1, source_target_pairs={{0,8},{8,0},{16,24},{24,16},{1,9},{9,1},{17,25},{25,17},{2,10},{10... | collective-permute-start | bytes 393224 | tf_op jit(solution)/shard_map/ppermute | solution.py:458
  2.8 3.5 %collective-permute-start.4 = (bf16[2,256,128]{2,1,0:T(8,128)(2,1)S(1)}, bf16[2,256,128]{2,1,0:T(8,128)(2,1)S(1)}, u32[]{:S(2)}, u32[]{:S(2)}) collective-permute-start(bf16[2,256,128]{2,1,0:T(8,128)(2,1)S(1)} %copy-done.2), channel_id=1, source_target_pairs={{0,8},{8,0},{16,24},{24,16},{1,9},{9,1},{17,25},{25,17},{2,10},{10... | collective-permute-start | bytes 393224 | tf_op jit(solution)/shard_map/ppermute | solution.py:458
  5.1 3.3 %collective-permute-start.2 = (bf16[80,128]{1,0:T(8,128)(2,1)S(1)}, bf16[80,128]{1,0:T(8,128)(2,1)S(1)}, u32[]{:S(2)}, u32[]{:S(2)}) collective-permute-start(bf16[80,128]{1,0:T(8,128)(2,1)S(1)} %get-tuple-element.56), channel_id=1, source_target_pairs={{0,9},{1,8},{8,1},{9,0},{16,25},{17,24},{24,17},{25,16},{2,11},{3,... | collective-permute-start | bytes 61448 | tf_op jit(solution)/shard_map/ppermute | solution.py:465
  9.0 2.3 %collective-permute-start.5 = (bf16[2,256,128]{2,1,0:T(8,128)(2,1)S(1)}, bf16[2,256,128]{2,1,0:T(8,128)(2,1)S(1)}, u32[]{:S(2)}, u32[]{:S(2)}) collective-permute-start(bf16[2,256,128]{2,1,0:T(8,128)(2,1)S(1)} %collective-permute-done.k_one.refs_7_), channel_id=1, source_target_pairs={{0,8},{8,0},{16,24},{24,16},{1,9},{9,1},{17,25},{25,17},{2,10},{10... | collective-permute-start | bytes 393224 | tf_op jit(solution)/shard_map/ppermute | solution.py:458
  10.2 1.3 %collective-permute-start.6 = (bf16[2,256,128]{2,1,0:T(8,128)(2,1)S(1)}, bf16[2,256,128]{2,1,0:T(8,128)(2,1)S(1)}, u32[]{:S(2)}, u32[]{:S(2)}) collective-permute-start(bf16[2,256,128]{2,1,0:T(8,128)(2,1)S(1)} %collective-permute-done.1.v_one.refs_8_), channel_id=1, source_target_pairs={{0,8},{8,0},{16,24},{24,16},{1,9},{9,1},{17,25},{25,17},{2,10},{10... | collective-permute-start | bytes 393224 | tf_op jit(solution)/shard_map/ppermute | solution.py:458
  12.2 11.8 %collective-permute-start.7 = (bf16[80,128]{1,0:T(8,128)(2,1)S(1)}, bf16[80,128]{1,0:T(8,128)(2,1)S(1)}, u32[]{:S(2)}, u32[]{:S(2)}) collective-permute-start(bf16[80,128]{1,0:T(8,128)(2,1)S(1)} %get-tuple-element.102), channel_id=1, source_target_pairs={{0,9},{1,8},{8,1},{9,0},{16,25},{17,24},{24,17},{25,16},{2,11},{3,... | collective-permute-start | bytes 61448 | tf_op jit(solution)/shard_map/ppermute | solution.py:465

commit v10 on v9

--- a/solution.py
+++ b/solution.py
@@ -235,7 +235,7 @@
     @pl.when(late)
     def _():
         widen([0], v_one, v_one, wide)
-        add_blocks([(0, *blocks[0])], lambda row: ([k_one[row]], wide[row, :length]), q_ref, first_in, emit)
+        add_blocks([(0, *blocks[0])], lambda index, row: ([k_one[row]], wide[row, :length]), q_ref, first_in, emit)
         if keep:
             for ref, value in zip(last_out, last_in):
                 ref[...] = value[...]
@@ -297,7 +297,7 @@
             cols = slice(head * D_HEAD, (head + 1) * D_HEAD)
             at = slice((head - start) * D_HEAD, (head - start + 1) * D_HEAD)
             state = state_of(index, at)
-            summed, total = add_keys_at(q_ref[row, :, cols], *far_of(row), *state)
+            summed, total = add_keys_at(q_ref[row, :, cols], *far_of(index, row), *state)
             emit(index, row, cols, at, summed, total, state[2])
             if row_done and cols.stop == q_ref.shape[2]:
                 row_done(row)
@@ -315,7 +315,7 @@
             def _(head, index=index, row=row, start=start):
                 at = pl.ds(pl.multiple_of(head * D_HEAD, D_HEAD), D_HEAD)
                 cols = pl.ds(pl.multiple_of((start + head) * D_HEAD, D_HEAD), D_HEAD)
-                new = add_keys(q_ref[row, :, cols], *far_of(row), *state_of(index, at))
+                new = add_keys(q_ref[row, :, cols], *far_of(index, row), *state_of(index, at))
                 emit(index, row, cols, at, *new)
 
         if after:
@@ -334,9 +334,9 @@
     position = seq * length + lax.broadcasted_iota(jnp.int32, (length, D_HEAD), 0)
     places = [(index, *block) for index, block in enumerate(blocks)]
 
-    def far_of(row):
-        first, stop = chosen[row][0] * length, (chosen[row][-1] + 1) * length
-        return [(k_one, k_two)[i][row] for i in chosen[row]], wide[row, first:stop]
+    def far_of(index, row):
+        first, stop = chosen[index][0] * length, (chosen[index][-1] + 1) * length
+        return [(k_one, k_two)[i][row] for i in chosen[index]], wide[row, first:stop]
 
     def emit(index, row, cols, at, summed, total, top):
         if last:
@@ -493,8 +493,10 @@
         us=1.3,
     )
     partner_msg = partner(other_msg)
-    blocks = [(row, 0, group) for row in range(prompts - 1)]
-    blocks += [(prompts - 1, 0, group // 2), (prompts - 1, group // 2, group)]
+    blocks = []
+    for row in range(prompts):
+        cut = row == 0 or row == prompts - 1
+        blocks += [(row, 0, group // 2), (row, group // 2, group)] if cut else [(row, 0, group)]
     runs = [[shape((length, (stop - start) * D_HEAD), f32)] * 3 for _, start, stop in blocks]
 
     last_shift = shifts[-1]
@@ -538,7 +540,7 @@
     other_part = partner(partner_part)
     for index, shift in enumerate(shifts):
         last = index == len(shifts) - 1
-        chosen = {row: (1,) if last and row == 0 else (0, 1) for row in range(prompts)}
+        chosen = [(1,) if last and number == 0 else (0, 1) for number in range(len(blocks))]
         outs, out_specs, extra = sum(runs, []), [VMEM] * len(states), []
         if last:
             outs = [shape(prefill_queries.shape, bf16)] * 2 + [shape((span, dec_columns // 2), f32)]

time: 25 us -> 25.8 us (1.032)
  Pallas kernels: 17.5 us -> 18 us
  waiting for transfers between devices: 1.01 us -> 1.31 us
    pallas_call x7, Pallas kernels: 17.5 us -> 18 us  [call(): pl.pallas_call(kernel, out_shape=outs, in_specs=specs or [VMEM] * len(arg...]
    ppermute x4, waiting for transfers between devices: 0.25 us -> 0.55 us  [near(): return lax.ppermute(x, 'seq', [(i, i ^ 1) for i in range(seqs)])]
  transfers between devices with their start and end apart: 8 -> 8, of which waited for: 3 -> 4; matrix products, arithmetic and copies ran while one was open for 0% -> 0% of each run, Pallas kernels for 64% -> 64%
where the time goes in v10:
time: 25.8 us; the launch traced here: 25.6 us
  Pallas kernels  18 us (70%)
  starting transfers between devices  5.57 us (22%)
  waiting for transfers between devices  1.31 us (5%)
  between operations  0.73 us (3%)
    pallas_call x7, Pallas kernels, call(): pl.pallas_call(kernel, out_shape=outs, in_specs=specs or [VMEM] * len(arg...  18 us
    ppermute x2, starting transfers between devices, around(): lax.ppermute(x, 'seq', [(i, (i + 2 * shift) % seqs) for i in range(seqs)])  2.09 us
    ppermute x4, starting transfers between devices, near(): return lax.ppermute(x, 'seq', [(i, i ^ 1) for i in range(seqs)])  1.75 us
    ppermute x2, starting transfers between devices, partner(): return lax.ppermute(x, ('seq', 'role'), moves)  1.73 us
    ppermute x2, waiting for transfers between devices, around(): lax.ppermute(x, 'seq', [(i, (i + 2 * shift) % seqs) for i in range(seqs)])  0.64 us
    ppermute x4, waiting for transfers between devices, near(): return lax.ppermute(x, 'seq', [(i, i ^ 1) for i in range(seqs)])  0.55 us
  transfers between devices with their start and end apart: 8, of which 4 were waited for; matrix products, arithmetic and copies ran while one was open for 0% of the time, Pallas kernels for 64%

profile of v10, /device:TPU:28, one launch (start us, length us, event | category | flops | bytes accessed | tf_op | source)
XLA Modules:
  0.0 25.6 jit_solution(8640513572555727669)
XLA Ops:
  0.7 0.6 %collective-permute-start = (bf16[2,256,128]{2,1,0:T(8,128)(2,1)}, bf16[2,256,128]{2,1,0:T(8,128)(2,1)S(1)}, u32[]{:S(2)}, u32[]{:S(2)}) collective-permute-start(bf16[2,256,128]{2,1,0:T(8,128)(2,1)} %refs_3_.1), channel_id=1, source_target_pairs={{0,16},{8,24},{16,0},{24,8},{1,17},{9,25},{17,1},{25,9},{2,18},{10... | collective-permute-start | bytes 393224 | tf_op jit(solution)/shard_map/ppermute | solution.py:461
  1.2 1.5 %collective-permute-start.1 = (bf16[2,256,128]{2,1,0:T(8,128)(2,1)}, bf16[2,256,128]{2,1,0:T(8,128)(2,1)S(1)}, u32[]{:S(2)}, u32[]{:S(2)}) collective-permute-start(bf16[2,256,128]{2,1,0:T(8,128)(2,1)} %refs_4_.1), channel_id=1, source_target_pairs={{0,16},{8,24},{16,0},{24,8},{1,17},{9,25},{17,1},{25,9},{2,18},{10... | collective-permute-start | bytes 393224 | tf_op jit(solution)/shard_map/ppermute | solution.py:461
  2.8 0.0 copy-done.1
  2.8 0.0 collective-permute-start.3
  2.8 0.5 %collective-permute-start.4 = (bf16[2,256,128]{2,1,0:T(8,128)(2,1)S(1)}, bf16[2,256,128]{2,1,0:T(8,128)(2,1)S(1)}, u32[]{:S(2)}, u32[]{:S(2)}) collective-permute-start(bf16[2,256,128]{2,1,0:T(8,128)(2,1)S(1)} %copy-done.2), channel_id=1, source_target_pairs={{0,8},{8,0},{16,24},{24,16},{1,9},{9,1},{17,25},{25,17},{2,10},{10... | collective-permute-start | bytes 393224 | tf_op jit(solution)/shard_map/ppermute | solution.py:458
  3.3 0.0 copy-done.4
  3.3 1.8 %shard_map.123 = (bf16[80,128]{1,0:T(8,128)(2,1)S(1)}, bf16[80,128]{1,0:T(8,128)(2,1)S(1)}, s32[8,128]{1,0:T(8,128)S(1)}, f32[2,64,128]{2,1,0:T(8,128)S(1)}, f32...) custom-call(s32[2]{0:T(128)} %asg_hbm.1, s32[2]{0:T(128)} %plen_hbm.1, s32[2]{0:T(128)} %clen_hbm.1, ...), custom_call_target="tpu_custom_call" | custom-call | flops 1430000000 | bytes 3900000 | tf_op jit(solution)/shard_map/pallas_call | solution.py:422
  5.1 1.2 %collective-permute-start.2 = (bf16[80,128]{1,0:T(8,128)(2,1)S(1)}, bf16[80,128]{1,0:T(8,128)(2,1)S(1)}, u32[]{:S(2)}, u32[]{:S(2)}) collective-permute-start(bf16[80,128]{1,0:T(8,128)(2,1)S(1)} %get-tuple-element.65), channel_id=1, source_target_pairs={{0,9},{1,8},{8,1},{9,0},{16,25},{17,24},{24,17},{25,16},{2,11},{3,... | collective-permute-start | bytes 61448 | tf_op jit(solution)/shard_map/ppermute | solution.py:465
  6.3 0.0 collective-permute-done.3.k_near.refs_5_
  6.3 0.0 collective-permute-done.4.v_near.refs_6_
  6.3 1.9 %shard_map.124 = (f32[256,512]{1,0:T(8,128)S(1)}, f32[256,512]{1,0:T(8,128)S(1)}, f32[256,512]{1,0:T(8,128)S(1)}, f32[256,512]{1,0:T(8,128)S(1)}, f32[256,512]{1...) custom-call(bf16[2,256,1024]{2,1,0:T(8,128)(2,1)S(1)} %copy-done, ...), custom_call_target="tpu_custom_call" | custom-call | flops 2860000000 | bytes 7800000 | tf_op jit(solution)/shard_map/pallas_call | solution.py:422
  8.2 0.1 collective-permute-done.2.refs_1_
  8.4 0.6 %collective-permute-done.1.v_one.refs_8_ = bf16[2,256,128]{2,1,0:T(8,128)(2,1)S(1)} collective-permute-done((bf16[2,256,128]{2,1,0:T(8,128)(2,1)}, bf16[2,256,128]{2,1,0:T(8,128)(2,1)S(1)}, u32[]{:S(2)}, u32[]{:S(2)}) %collective-permute-start.1) | collective-permute-done | bytes 131104 | tf_op jit(solution)/shard_map/ppermute | solution.py:461
  9.0 0.0 collective-permute-done.k_one.refs_7_
  9.0 1.2 %collective-permute-start.5 = (bf16[2,256,128]{2,1,0:T(8,128)(2,1)S(1)}, bf16[2,256,128]{2,1,0:T(8,128)(2,1)S(1)}, u32[]{:S(2)}, u32[]{:S(2)}) collective-permute-start(bf16[2,256,128]{2,1,0:T(8,128)(2,1)S(1)} %collective-permute-done.k_one.refs_7_), channel_id=1, source_target_pairs={{0,8},{8,0},{16,24},{24,16},{1,9},{9,1},{17,25},{25,17},{2,10},{10... | collective-permute-start | bytes 393224 | tf_op jit(solution)/shard_map/ppermute | solution.py:458
  10.2 0.1 collective-permute-start.6
  10.3 0.7 %shard_map.125 = (f32[256,512]{1,0:T(8,128)S(1)}, f32[256,512]{1,0:T(8,128)S(1)}, f32[256,512]{1,0:T(8,128)S(1)}, f32[256,512]{1,0:T(8,128)S(1)}, f32[256,512]{1,0:T(8,128)S(1)}, /*index=5*/f32[256,512]{1,0:T(8,128)S(1)}) custom-call(bf16[2,256,1024]{2,1,0:T(8,128)(2,1)S(1)} %copy-done, bf16[2,256,128]{2,1,0:T(8,128)(2,1)S(1)} %copy-done.1, ...), custom_call_target="tpu_custom_call" | custom-call | flops 1100000000 | bytes 3000000 | tf_op jit(solution)/shard_map/pallas_call | solution.py:422
  11.0 0.2 collective-permute-done.5.refs_9_.k_two
  11.2 0.4 %collective-permute-done.6.refs_10_.v_two = bf16[2,256,128]{2,1,0:T(8,128)(2,1)S(1)} collective-permute-done((bf16[2,256,128]{2,1,0:T(8,128)(2,1)S(1)}, bf16[2,256,128]{2,1,0:T(8,128)(2,1)S(1)}, u32[]{:S(2)}, u32[]{:S(2)}) %collective-permute-start.6) | collective-permute-done | bytes 131104 | tf_op jit(solution)/shard_map/ppermute | solution.py:458
  11.5 0.7 %shard_map.126 = (f32[80,128]{1,0:T(8,128)S(1)}, bf16[80,128]{1,0:T(8,128)(2,1)S(1)}) custom-call(bf16[80,128]{1,0:T(8,128)(2,1)S(1)} %get-tuple-element.94.refs_0_, bf16[80,128]{1,0:T(8,128)(2,1)S(1)} %collective-permute-done.2.refs_1_, s32[8,128]{1,0:T(8,128)S(1)} %get-tuple-element.64._.refs_2_.info_ref, bf16[2,256,128]{2,1,0:T(8,128)(2,1)S(1)} %copy-done.1, ...), custom_call_target="tpu_custom_call" | custom-call | flops 770000000 | bytes 2100000 | tf_op jit(solution)/shard_map/pallas_call | solution.py:422
  12.2 0.5 %collective-permute-start.7 = (bf16[80,128]{1,0:T(8,128)(2,1)S(1)}, bf16[80,128]{1,0:T(8,128)(2,1)S(1)}, u32[]{:S(2)}, u32[]{:S(2)}) collective-permute-start(bf16[80,128]{1,0:T(8,128)(2,1)S(1)} %get-tuple-element.120), channel_id=1, source_target_pairs={{0,9},{1,8},{8,1},{9,0},{16,25},{17,24},{24,17},{25,16},{2,11},{3,... | collective-permute-start | bytes 61448 | tf_op jit(solution)/shard_map/ppermute | solution.py:465
  12.7 12.1 %shard_map.127 = (bf16[2,256,1024]{2,1,0:T(8,128)(2,1)S(1)}, bf16[2,256,1024]{2,1,0:T(8,128)(2,1)}, f32[8,1024]{1,0:T(8,128)S(1)}) custom-call(s32[8,128]{1,0:T(8,128)S(1)} %get-tuple-element.64._.refs_2_.info_ref, bf16[2,256,1024]{2,1,0:T(8,128)(2,1)S(1)} %copy-done, bf16[2,256,128]{2,1,0:T(8,128)(2,1)S(1)} %collective-permute-done.k_one.refs_7_, ...), custom_call_target="tpu_custom_call" | custom-call | flops 2640000000 | bytes 7200000 | tf_op jit(solution)/shard_map/pallas_call | solution.py:422
  24.8 0.0 collective-permute-done.7.other_part
  24.8 0.8 %shard_map.128 = (bf16[4,2,2048]{2,1,0:T(2,128)(2,1)}, bf16[2,256,1024]{2,1,0:T(8,128)(2,1)}) custom-call(bf16[2,256,1024]{2,1,0:T(8,128)(2,1)S(1)} %get-tuple-element.118.pre, f32[8,1024]{1,0:T(8,128)S(1)} %get-tuple-element.119.own_rows, f32[2,64,128]{2,1,0:T(8,128)S(1)} %get-tuple-element.115.refs_24_.cache_sum, ...), custom_call_target="tpu_custom_call", output_to_operand_aliasing={{1}: (6, {})} | custom-call | flops 770000000 | bytes 2100000 | tf_op jit(solution)/shard_map/pallas_call | solution.py:422
  (9 shorter events, 0.0 us)
Async XLA Ops:
  0.6 2.1 %copy-start.1 = (bf16[2,256,128]{2,1,0:T(8,128)(2,1)S(1)}, bf16[2,256,128]{2,1,0:T(8,128)(2,1)}, u32[]{:S(2)}) copy-start(bf16[2,256,128]{2,1,0:T(8,128)(2,1)} %refs_3_.1) | copy-start | bytes 393220
  0.6 2.1 %copy-start.2 = (bf16[2,256,128]{2,1,0:T(8,128)(2,1)S(1)}, bf16[2,256,128]{2,1,0:T(8,128)(2,1)}, u32[]{:S(2)}) copy-start(bf16[2,256,128]{2,1,0:T(8,128)(2,1)} %refs_4_.1) | copy-start | bytes 393220
  0.7 2.6 %copy-start.4 = (bf16[2,1024,256]{2,1,0:T(8,128)(2,1)S(1)}, bf16[2,1024,256]{2,1,0:T(8,128)(2,1)}, u32[]{:S(2)}) copy-start(bf16[2,1024,256]{2,1,0:T(8,128)(2,1)} %cv_ref.1) | copy-start | bytes 3145732
  0.7 2.6 %copy-start.3 = (bf16[2,1024,256]{2,1,0:T(8,128)(2,1)S(1)}, bf16[2,1024,256]{2,1,0:T(8,128)(2,1)}, u32[]{:S(2)}) copy-start(bf16[2,1024,256]{2,1,0:T(8,128)(2,1)} %ck_ref.1) | copy-start | bytes 3145732
  0.7 8.3 %collective-permute-start = (bf16[2,256,128]{2,1,0:T(8,128)(2,1)}, bf16[2,256,128]{2,1,0:T(8,128)(2,1)S(1)}, u32[]{:S(2)}, u32[]{:S(2)}) collective-permute-start(bf16[2,256,128]{2,1,0:T(8,128)(2,1)} %refs_3_.1), channel_id=1, source_target_pairs={{0,16},{8,24},{16,0},{24,8},{1,17},{9,25},{17,1},{25,9},{2,18},{10... | collective-permute-start | bytes 393224 | tf_op jit(solution)/shard_map/ppermute | solution.py:461
  1.2 7.7 %collective-permute-start.1 = (bf16[2,256,128]{2,1,0:T(8,128)(2,1)}, bf16[2,256,128]{2,1,0:T(8,128)(2,1)S(1)}, u32[]{:S(2)}, u32[]{:S(2)}) collective-permute-start(bf16[2,256,128]{2,1,0:T(8,128)(2,1)} %refs_4_.1), channel_id=1, source_target_pairs={{0,16},{8,24},{16,0},{24,8},{1,17},{9,25},{17,1},{25,9},{2,18},{10... | collective-permute-start | bytes 393224 | tf_op jit(solution)/shard_map/ppermute | solution.py:461
  2.8 3.6 %copy-start = (bf16[2,256,1024]{2,1,0:T(8,128)(2,1)S(1)}, bf16[2,256,1024]{2,1,0:T(8,128)(2,1)}, u32[]{:S(2)}) copy-start(bf16[2,256,1024]{2,1,0:T(8,128)(2,1)} %q_ref.5) | copy-start | bytes 3145732
  2.8 3.5 %collective-permute-start.3 = (bf16[2,256,128]{2,1,0:T(8,128)(2,1)S(1)}, bf16[2,256,128]{2,1,0:T(8,128)(2,1)S(1)}, u32[]{:S(2)}, u32[]{:S(2)}) collective-permute-start(bf16[2,256,128]{2,1,0:T(8,128)(2,1)S(1)} %copy-done.1), channel_id=1, source_target_pairs={{0,8},{8,0},{16,24},{24,16},{1,9},{9,1},{17,25},{25,17},{2,10},{10... | collective-permute-start | bytes 393224 | tf_op jit(solution)/shard_map/ppermute | solution.py:458
  2.8 3.5 %collective-permute-start.4 = (bf16[2,256,128]{2,1,0:T(8,128)(2,1)S(1)}, bf16[2,256,128]{2,1,0:T(8,128)(2,1)S(1)}, u32[]{:S(2)}, u32[]{:S(2)}) collective-permute-start(bf16[2,256,128]{2,1,0:T(8,128)(2,1)S(1)} %copy-done.2), channel_id=1, source_target_pairs={{0,8},{8,0},{16,24},{24,16},{1,9},{9,1},{17,25},{25,17},{2,10},{10... | collective-permute-start | bytes 393224 | tf_op jit(solution)/shard_map/ppermute | solution.py:458
  5.1 3.3 %collective-permute-start.2 = (bf16[80,128]{1,0:T(8,128)(2,1)S(1)}, bf16[80,128]{1,0:T(8,128)(2,1)S(1)}, u32[]{:S(2)}, u32[]{:S(2)}) collective-permute-start(bf16[80,128]{1,0:T(8,128)(2,1)S(1)} %get-tuple-element.65), channel_id=1, source_target_pairs={{0,9},{1,8},{8,1},{9,0},{16,25},{17,24},{24,17},{25,16},{2,11},{3,... | collective-permute-start | bytes 61448 | tf_op jit(solution)/shard_map/ppermute | solution.py:465
  9.0 2.2 %collective-permute-start.5 = (bf16[2,256,128]{2,1,0:T(8,128)(2,1)S(1)}, bf16[2,256,128]{2,1,0:T(8,128)(2,1)S(1)}, u32[]{:S(2)}, u32[]{:S(2)}) collective-permute-start(bf16[2,256,128]{2,1,0:T(8,128)(2,1)S(1)} %collective-permute-done.k_one.refs_7_), channel_id=1, source_target_pairs={{0,8},{8,0},{16,24},{24,16},{1,9},{9,1},{17,25},{25,17},{2,10},{10... | collective-permute-start | bytes 393224 | tf_op jit(solution)/shard_map/ppermute | solution.py:458
  10.2 1.3 %collective-permute-start.6 = (bf16[2,256,128]{2,1,0:T(8,128)(2,1)S(1)}, bf16[2,256,128]{2,1,0:T(8,128)(2,1)S(1)}, u32[]{:S(2)}, u32[]{:S(2)}) collective-permute-start(bf16[2,256,128]{2,1,0:T(8,128)(2,1)S(1)} %collective-permute-done.1.v_one.refs_8_), channel_id=1, source_target_pairs={{0,8},{8,0},{16,24},{24,16},{1,9},{9,1},{17,25},{25,17},{2,10},{10... | collective-permute-start | bytes 393224 | tf_op jit(solution)/shard_map/ppermute | solution.py:458
  12.2 12.6 %collective-permute-start.7 = (bf16[80,128]{1,0:T(8,128)(2,1)S(1)}, bf16[80,128]{1,0:T(8,128)(2,1)S(1)}, u32[]{:S(2)}, u32[]{:S(2)}) collective-permute-start(bf16[80,128]{1,0:T(8,128)(2,1)S(1)} %get-tuple-element.120), channel_id=1, source_target_pairs={{0,9},{1,8},{8,1},{9,0},{16,25},{17,24},{24,17},{25,16},{2,11},{3,... | collective-permute-start | bytes 61448 | tf_op jit(solution)/shard_map/ppermute | solution.py:465

commit v11 on v10

--- a/solution.py
+++ b/solution.py
@@ -495,8 +495,8 @@
     partner_msg = partner(other_msg)
     blocks = []
     for row in range(prompts):
-        cut = row == 0 or row == prompts - 1
-        blocks += [(row, 0, group // 2), (row, group // 2, group)] if cut else [(row, 0, group)]
+        cut = {prompts - 1: group // 2, 0: group // 4}.get(row)
+        blocks += [(row, 0, cut), (row, cut, group)] if cut else [(row, 0, group)]
     runs = [[shape((length, (stop - start) * D_HEAD), f32)] * 3 for _, start, stop in blocks]
 
     last_shift = shifts[-1]

time: 25.8 us -> 26.2 us (1.016)
  no operation moved by 1% of the time
where the time goes in v11:
time: 26.2 us; the launch traced here: 26 us
  Pallas kernels  18.2 us (69%)
  starting transfers between devices  5.58 us (21%)
  waiting for transfers between devices  1.48 us (6%)
  between operations  0.74 us (3%)
    pallas_call x7, Pallas kernels, call(): pl.pallas_call(kernel, out_shape=outs, in_specs=specs or [VMEM] * len(arg...  18.2 us
    ppermute x2, starting transfers between devices, around(): lax.ppermute(x, 'seq', [(i, (i + 2 * shift) % seqs) for i in range(seqs)])  2.09 us
    ppermute x4, starting transfers between devices, near(): return lax.ppermute(x, 'seq', [(i, i ^ 1) for i in range(seqs)])  1.75 us
    ppermute x2, starting transfers between devices, partner(): return lax.ppermute(x, ('seq', 'role'), moves)  1.74 us
    ppermute x4, waiting for transfers between devices, near(): return lax.ppermute(x, 'seq', [(i, i ^ 1) for i in range(seqs)])  0.72 us
    ppermute x2, waiting for transfers between devices, around(): lax.ppermute(x, 'seq', [(i, (i + 2 * shift) % seqs) for i in range(seqs)])  0.64 us
  transfers between devices with their start and end apart: 8, of which 4 were waited for; matrix products, arithmetic and copies ran while one was open for 0% of the time, Pallas kernels for 64%

profile of v11, /device:TPU:28, one launch (start us, length us, event | category | flops | bytes accessed | tf_op | source)
XLA Modules:
  0.0 26.0 jit_solution(16867344238994599722)
XLA Ops:
  0.7 0.6 %collective-permute-start = (bf16[2,256,128]{2,1,0:T(8,128)(2,1)}, bf16[2,256,128]{2,1,0:T(8,128)(2,1)S(1)}, u32[]{:S(2)}, u32[]{:S(2)}) collective-permute-start(bf16[2,256,128]{2,1,0:T(8,128)(2,1)} %refs_3_.1), channel_id=1, source_target_pairs={{0,16},{8,24},{16,0},{24,8},{1,17},{9,25},{17,1},{25,9},{2,18},{10... | collective-permute-start | bytes 393224 | tf_op jit(solution)/shard_map/ppermute | solution.py:461
  1.2 1.5 %collective-permute-start.1 = (bf16[2,256,128]{2,1,0:T(8,128)(2,1)}, bf16[2,256,128]{2,1,0:T(8,128)(2,1)S(1)}, u32[]{:S(2)}, u32[]{:S(2)}) collective-permute-start(bf16[2,256,128]{2,1,0:T(8,128)(2,1)} %refs_4_.1), channel_id=1, source_target_pairs={{0,16},{8,24},{16,0},{24,8},{1,17},{9,25},{17,1},{25,9},{2,18},{10... | collective-permute-start | bytes 393224 | tf_op jit(solution)/shard_map/ppermute | solution.py:461
  2.8 0.0 copy-done.1
  2.8 0.0 collective-permute-start.3
  2.8 0.5 %collective-permute-start.4 = (bf16[2,256,128]{2,1,0:T(8,128)(2,1)S(1)}, bf16[2,256,128]{2,1,0:T(8,128)(2,1)S(1)}, u32[]{:S(2)}, u32[]{:S(2)}) collective-permute-start(bf16[2,256,128]{2,1,0:T(8,128)(2,1)S(1)} %copy-done.2), channel_id=1, source_target_pairs={{0,8},{8,0},{16,24},{24,16},{1,9},{9,1},{17,25},{25,17},{2,10},{10... | collective-permute-start | bytes 393224 | tf_op jit(solution)/shard_map/ppermute | solution.py:458
  3.3 0.0 copy-done.4
  3.3 1.8 %shard_map.123 = (bf16[80,128]{1,0:T(8,128)(2,1)S(1)}, bf16[80,128]{1,0:T(8,128)(2,1)S(1)}, s32[8,128]{1,0:T(8,128)S(1)}, f32[2,64,128]{2,1,0:T(8,128)S(1)}, f32...) custom-call(s32[2]{0:T(128)} %asg_hbm.1, s32[2]{0:T(128)} %plen_hbm.1, s32[2]{0:T(128)} %clen_hbm.1, ...), custom_call_target="tpu_custom_call" | custom-call | flops 1430000000 | bytes 3900000 | tf_op jit(solution)/shard_map/pallas_call | solution.py:422
  5.1 1.2 %collective-permute-start.2 = (bf16[80,128]{1,0:T(8,128)(2,1)S(1)}, bf16[80,128]{1,0:T(8,128)(2,1)S(1)}, u32[]{:S(2)}, u32[]{:S(2)}) collective-permute-start(bf16[80,128]{1,0:T(8,128)(2,1)S(1)} %get-tuple-element.65), channel_id=1, source_target_pairs={{0,9},{1,8},{8,1},{9,0},{16,25},{17,24},{24,17},{25,16},{2,11},{3,... | collective-permute-start | bytes 61448 | tf_op jit(solution)/shard_map/ppermute | solution.py:465
  6.3 0.0 collective-permute-done.3.k_near.refs_5_
  6.3 0.0 collective-permute-done.4.v_near.refs_6_
  6.3 1.9 %shard_map.124 = (f32[256,256]{1,0:T(8,128)S(1)}, f32[256,256]{1,0:T(8,128)S(1)}, f32[256,256]{1,0:T(8,128)S(1)}, f32[256,768]{1,0:T(8,128)S(1)}, f32[256,768]{1...) custom-call(bf16[2,256,1024]{2,1,0:T(8,128)(2,1)S(1)} %copy-done, ...), custom_call_target="tpu_custom_call" | custom-call | flops 2860000000 | bytes 7800000 | tf_op jit(solution)/shard_map/pallas_call | solution.py:422
  8.2 0.1 collective-permute-done.2.refs_1_
  8.4 0.6 %collective-permute-done.1.v_one.refs_8_ = bf16[2,256,128]{2,1,0:T(8,128)(2,1)S(1)} collective-permute-done((bf16[2,256,128]{2,1,0:T(8,128)(2,1)}, bf16[2,256,128]{2,1,0:T(8,128)(2,1)S(1)}, u32[]{:S(2)}, u32[]{:S(2)}) %collective-permute-start.1) | collective-permute-done | bytes 131104 | tf_op jit(solution)/shard_map/ppermute | solution.py:461
  9.0 0.0 collective-permute-done.k_one.refs_7_
  9.0 1.2 %collective-permute-start.5 = (bf16[2,256,128]{2,1,0:T(8,128)(2,1)S(1)}, bf16[2,256,128]{2,1,0:T(8,128)(2,1)S(1)}, u32[]{:S(2)}, u32[]{:S(2)}) collective-permute-start(bf16[2,256,128]{2,1,0:T(8,128)(2,1)S(1)} %collective-permute-done.k_one.refs_7_), channel_id=1, source_target_pairs={{0,8},{8,0},{16,24},{24,16},{1,9},{9,1},{17,25},{25,17},{2,10},{10... | collective-permute-start | bytes 393224 | tf_op jit(solution)/shard_map/ppermute | solution.py:458
  10.2 0.1 collective-permute-start.6
  10.2 0.6 %shard_map.125 = (f32[256,256]{1,0:T(8,128)S(1)}, f32[256,256]{1,0:T(8,128)S(1)}, f32[256,256]{1,0:T(8,128)S(1)}, f32[256,512]{1,0:T(8,128)S(1)}, f32[256,512]{1,0:T(8,128)S(1)}, /*index=5*/f32[256,512]{1,0:T(8,128)S(1)}) custom-call(bf16[2,256,1024]{2,1,0:T(8,128)(2,1)S(1)} %copy-done, bf16[2,256,128]{2,1,0:T(8,128)(2,1)S(1)} %copy-done.1, ...), custom_call_target="tpu_custom_call" | custom-call | flops 1100000000 | bytes 3000000 | tf_op jit(solution)/shard_map/pallas_call | solution.py:422
  10.8 0.3 %collective-permute-done.5.refs_9_.k_two = bf16[2,256,128]{2,1,0:T(8,128)(2,1)S(1)} collective-permute-done((bf16[2,256,128]{2,1,0:T(8,128)(2,1)S(1)}, bf16[2,256,128]{2,1,0:T(8,128)(2,1)S(1)}, u32[]{:S(2)}, u32[]{:S(2)}) %collective-permute-start.5) | collective-permute-done | bytes 131104 | tf_op jit(solution)/shard_map/ppermute | solution.py:458
  11.2 0.4 %collective-permute-done.6.refs_10_.v_two = bf16[2,256,128]{2,1,0:T(8,128)(2,1)S(1)} collective-permute-done((bf16[2,256,128]{2,1,0:T(8,128)(2,1)S(1)}, bf16[2,256,128]{2,1,0:T(8,128)(2,1)S(1)}, u32[]{:S(2)}, u32[]{:S(2)}) %collective-permute-start.6) | collective-permute-done | bytes 131104 | tf_op jit(solution)/shard_map/ppermute | solution.py:458
  11.5 0.7 %shard_map.126 = (f32[80,128]{1,0:T(8,128)S(1)}, bf16[80,128]{1,0:T(8,128)(2,1)S(1)}) custom-call(bf16[80,128]{1,0:T(8,128)(2,1)S(1)} %get-tuple-element.94.refs_0_, bf16[80,128]{1,0:T(8,128)(2,1)S(1)} %collective-permute-done.2.refs_1_, s32[8,128]{1,0:T(8,128)S(1)} %get-tuple-element.64._.refs_2_.info_ref, bf16[2,256,128]{2,1,0:T(8,128)(2,1)S(1)} %copy-done.1, ...), custom_call_target="tpu_custom_call" | custom-call | flops 770000000 | bytes 2100000 | tf_op jit(solution)/shard_map/pallas_call | solution.py:422
  12.2 0.5 %collective-permute-start.7 = (bf16[80,128]{1,0:T(8,128)(2,1)S(1)}, bf16[80,128]{1,0:T(8,128)(2,1)S(1)}, u32[]{:S(2)}, u32[]{:S(2)}) collective-permute-start(bf16[80,128]{1,0:T(8,128)(2,1)S(1)} %get-tuple-element.120), channel_id=1, source_target_pairs={{0,9},{1,8},{8,1},{9,0},{16,25},{17,24},{24,17},{25,16},{2,11},{3,... | collective-permute-start | bytes 61448 | tf_op jit(solution)/shard_map/ppermute | solution.py:465
  12.7 12.5 %shard_map.127 = (bf16[2,256,1024]{2,1,0:T(8,128)(2,1)S(1)}, bf16[2,256,1024]{2,1,0:T(8,128)(2,1)}, f32[8,1024]{1,0:T(8,128)S(1)}) custom-call(s32[8,128]{1,0:T(8,128)S(1)} %get-tuple-element.64._.refs_2_.info_ref, bf16[2,256,1024]{2,1,0:T(8,128)(2,1)S(1)} %copy-done, bf16[2,256,128]{2,1,0:T(8,128)(2,1)S(1)} %collective-permute-done.k_one.refs_7_, ...), custom_call_target="tpu_custom_call" | custom-call | flops 2640000000 | bytes 7200000 | tf_op jit(solution)/shard_map/pallas_call | solution.py:422
  25.2 0.0 collective-permute-done.7.other_part
  25.2 0.8 %shard_map.128 = (bf16[4,2,2048]{2,1,0:T(2,128)(2,1)}, bf16[2,256,1024]{2,1,0:T(8,128)(2,1)}) custom-call(bf16[2,256,1024]{2,1,0:T(8,128)(2,1)S(1)} %get-tuple-element.118.pre, f32[8,1024]{1,0:T(8,128)S(1)} %get-tuple-element.119.own_rows, f32[2,64,128]{2,1,0:T(8,128)S(1)} %get-tuple-element.115.refs_24_.cache_sum, ...), custom_call_target="tpu_custom_call", output_to_operand_aliasing={{1}: (6, {})} | custom-call | flops 770000000 | bytes 2100000 | tf_op jit(solution)/shard_map/pallas_call | solution.py:422
  (9 shorter events, 0.0 us)
Async XLA Ops:
  0.6 2.1 %copy-start.1 = (bf16[2,256,128]{2,1,0:T(8,128)(2,1)S(1)}, bf16[2,256,128]{2,1,0:T(8,128)(2,1)}, u32[]{:S(2)}) copy-start(bf16[2,256,128]{2,1,0:T(8,128)(2,1)} %refs_3_.1) | copy-start | bytes 393220
  0.6 2.1 %copy-start.2 = (bf16[2,256,128]{2,1,0:T(8,128)(2,1)S(1)}, bf16[2,256,128]{2,1,0:T(8,128)(2,1)}, u32[]{:S(2)}) copy-start(bf16[2,256,128]{2,1,0:T(8,128)(2,1)} %refs_4_.1) | copy-start | bytes 393220
  0.7 2.6 %copy-start.4 = (bf16[2,1024,256]{2,1,0:T(8,128)(2,1)S(1)}, bf16[2,1024,256]{2,1,0:T(8,128)(2,1)}, u32[]{:S(2)}) copy-start(bf16[2,1024,256]{2,1,0:T(8,128)(2,1)} %cv_ref.1) | copy-start | bytes 3145732
  0.7 2.6 %copy-start.3 = (bf16[2,1024,256]{2,1,0:T(8,128)(2,1)S(1)}, bf16[2,1024,256]{2,1,0:T(8,128)(2,1)}, u32[]{:S(2)}) copy-start(bf16[2,1024,256]{2,1,0:T(8,128)(2,1)} %ck_ref.1) | copy-start | bytes 3145732
  0.7 8.3 %collective-permute-start = (bf16[2,256,128]{2,1,0:T(8,128)(2,1)}, bf16[2,256,128]{2,1,0:T(8,128)(2,1)S(1)}, u32[]{:S(2)}, u32[]{:S(2)}) collective-permute-start(bf16[2,256,128]{2,1,0:T(8,128)(2,1)} %refs_3_.1), channel_id=1, source_target_pairs={{0,16},{8,24},{16,0},{24,8},{1,17},{9,25},{17,1},{25,9},{2,18},{10... | collective-permute-start | bytes 393224 | tf_op jit(solution)/shard_map/ppermute | solution.py:461
  1.2 7.7 %collective-permute-start.1 = (bf16[2,256,128]{2,1,0:T(8,128)(2,1)}, bf16[2,256,128]{2,1,0:T(8,128)(2,1)S(1)}, u32[]{:S(2)}, u32[]{:S(2)}) collective-permute-start(bf16[2,256,128]{2,1,0:T(8,128)(2,1)} %refs_4_.1), channel_id=1, source_target_pairs={{0,16},{8,24},{16,0},{24,8},{1,17},{9,25},{17,1},{25,9},{2,18},{10... | collective-permute-start | bytes 393224 | tf_op jit(solution)/shard_map/ppermute | solution.py:461
  2.8 3.6 %copy-start = (bf16[2,256,1024]{2,1,0:T(8,128)(2,1)S(1)}, bf16[2,256,1024]{2,1,0:T(8,128)(2,1)}, u32[]{:S(2)}) copy-start(bf16[2,256,1024]{2,1,0:T(8,128)(2,1)} %q_ref.5) | copy-start | bytes 3145732
  2.8 3.5 %collective-permute-start.3 = (bf16[2,256,128]{2,1,0:T(8,128)(2,1)S(1)}, bf16[2,256,128]{2,1,0:T(8,128)(2,1)S(1)}, u32[]{:S(2)}, u32[]{:S(2)}) collective-permute-start(bf16[2,256,128]{2,1,0:T(8,128)(2,1)S(1)} %copy-done.1), channel_id=1, source_target_pairs={{0,8},{8,0},{16,24},{24,16},{1,9},{9,1},{17,25},{25,17},{2,10},{10... | collective-permute-start | bytes 393224 | tf_op jit(solution)/shard_map/ppermute | solution.py:458
  2.8 3.5 %collective-permute-start.4 = (bf16[2,256,128]{2,1,0:T(8,128)(2,1)S(1)}, bf16[2,256,128]{2,1,0:T(8,128)(2,1)S(1)}, u32[]{:S(2)}, u32[]{:S(2)}) collective-permute-start(bf16[2,256,128]{2,1,0:T(8,128)(2,1)S(1)} %copy-done.2), channel_id=1, source_target_pairs={{0,8},{8,0},{16,24},{24,16},{1,9},{9,1},{17,25},{25,17},{2,10},{10... | collective-permute-start | bytes 393224 | tf_op jit(solution)/shard_map/ppermute | solution.py:458
  5.1 3.3 %collective-permute-start.2 = (bf16[80,128]{1,0:T(8,128)(2,1)S(1)}, bf16[80,128]{1,0:T(8,128)(2,1)S(1)}, u32[]{:S(2)}, u32[]{:S(2)}) collective-permute-start(bf16[80,128]{1,0:T(8,128)(2,1)S(1)} %get-tuple-element.65), channel_id=1, source_target_pairs={{0,9},{1,8},{8,1},{9,0},{16,25},{17,24},{24,17},{25,16},{2,11},{3,... | collective-permute-start | bytes 61448 | tf_op jit(solution)/shard_map/ppermute | solution.py:465
  9.0 2.2 %collective-permute-start.5 = (bf16[2,256,128]{2,1,0:T(8,128)(2,1)S(1)}, bf16[2,256,128]{2,1,0:T(8,128)(2,1)S(1)}, u32[]{:S(2)}, u32[]{:S(2)}) collective-permute-start(bf16[2,256,128]{2,1,0:T(8,128)(2,1)S(1)} %collective-permute-done.k_one.refs_7_), channel_id=1, source_target_pairs={{0,8},{8,0},{16,24},{24,16},{1,9},{9,1},{17,25},{25,17},{2,10},{10... | collective-permute-start | bytes 393224 | tf_op jit(solution)/shard_map/ppermute | solution.py:458
  10.2 1.3 %collective-permute-start.6 = (bf16[2,256,128]{2,1,0:T(8,128)(2,1)S(1)}, bf16[2,256,128]{2,1,0:T(8,128)(2,1)S(1)}, u32[]{:S(2)}, u32[]{:S(2)}) collective-permute-start(bf16[2,256,128]{2,1,0:T(8,128)(2,1)S(1)} %collective-permute-done.1.v_one.refs_8_), channel_id=1, source_target_pairs={{0,8},{8,0},{16,24},{24,16},{1,9},{9,1},{17,25},{25,17},{2,10},{10... | collective-permute-start | bytes 393224 | tf_op jit(solution)/shard_map/ppermute | solution.py:458
  12.2 13.0 %collective-permute-start.7 = (bf16[80,128]{1,0:T(8,128)(2,1)S(1)}, bf16[80,128]{1,0:T(8,128)(2,1)S(1)}, u32[]{:S(2)}, u32[]{:S(2)}) collective-permute-start(bf16[80,128]{1,0:T(8,128)(2,1)S(1)} %get-tuple-element.120), channel_id=1, source_target_pairs={{0,9},{1,8},{8,1},{9,0},{16,25},{17,24},{24,17},{25,16},{2,11},{3,... | collective-permute-start | bytes 61448 | tf_op jit(solution)/shard_map/ppermute | solution.py:465
